TPU v7x, 32 devices: a whole 2x2x4 slice. The times are simulated.
32 devices in a mesh: dp: 8 (over y, x, core), tensor: 4 (over z).
Axes of the slice: x: 2, y: 2, z: 4, core: 2. Of those that a mesh axis runs over, the one named last changes fastest.
Arguments:
- tokens: bfloat16 [10240, 1536], P('dp'), may hold values from -6 to 6
- cotangent: bfloat16 [10240, 1536], P('dp'), may hold values from -6 to 6
- routes: int32 [10240, 8], P('dp'), may hold values from 0 to 15, all different within a row; in each aligned block of 640 rows (0 to 639, 640 to 1279, ...) at most 512 rows name the same one
- inproj_weight: float32 [1536, 8, 320], P('dp', 'tensor'), may hold values from -0.15625 to 0.15625
- inproj_first: float32 [1536, 8, 320], P('dp', 'tensor'), may hold values from -64 to 64
- inproj_second: float32 [1536, 8, 320], P('dp', 'tensor'), may hold values from 307.2 to 4096
- outproj_weight: float32 [8, 192, 1536], P('tensor', None, 'dp'), may hold values from -2.5 to 2.5
- outproj_first: float32 [8, 192, 1536], P('tensor', None, 'dp'), may hold values from -7 to 7
- outproj_second: float32 [8, 192, 1536], P('tensor', None, 'dp'), may hold values from 3.072 to 40.96
- gateup_weight: float32 [16, 1536, 2, 512], P(None, 'dp', None, 'tensor'), may hold values from -0.15625 to 0.15625
- gateup_first: float32 [16, 1536, 2, 512], P(None, 'dp', None, 'tensor'), may hold values from -10 to 10
- gateup_second: float32 [16, 1536, 2, 512], P(None, 'dp', None, 'tensor'), may hold values from 6.144 to 81.92
- down_weight: float32 [16, 512, 1536], P(None, 'tensor', 'dp'), may hold values from -0.5 to 0.5
- down_first: float32 [16, 512, 1536], P(None, 'tensor', 'dp'), may hold values from -4 to 4
- down_second: float32 [16, 512, 1536], P(None, 'tensor', 'dp'), may hold values from 1.024 to 13.312
- router_weight: float32 [1536, 16], P('dp'), may hold values from -0.078125 to 0.078125
- router_first: float32 [1536, 16], P('dp'), may hold values from -256 to 256
- router_second: float32 [1536, 16], P('dp'), may hold values from 4915.2 to 65536
- gains: float32 [2, 1536], P(None, 'dp'), may hold values from 0.5 to 1.5
- gains_first: float32 [2, 1536], P(None, 'dp'), may hold values from -64 to 64
- gains_second: float32 [2, 1536], P(None, 'dp'), may hold values from 307.2 to 4096
Outputs:
- block_out: bfloat16 [10240, 1536], P('dp')
- tokens_grad: float32 [10240, 1536], P('dp')
- inproj_next: float32 [1536, 8, 320], P('dp', 'tensor')
- inproj_first_next: float32 [1536, 8, 320], P('dp', 'tensor')
- inproj_second_next: float32 [1536, 8, 320], P('dp', 'tensor')
- outproj_next: float32 [8, 192, 1536], P('tensor', None, 'dp')
- outproj_first_next: float32 [8, 192, 1536], P('tensor', None, 'dp')
- outproj_second_next: float32 [8, 192, 1536], P('tensor', None, 'dp')
- gateup_next: float32 [16, 1536, 2, 512], P(None, 'dp', None, 'tensor')
- gateup_first_next: float32 [16, 1536, 2, 512], P(None, 'dp', None, 'tensor')
- gateup_second_next: float32 [16, 1536, 2, 512], P(None, 'dp', None, 'tensor')
- down_next: float32 [16, 512, 1536], P(None, 'tensor', 'dp')
- down_first_next: float32 [16, 512, 1536], P(None, 'tensor', 'dp')
- down_second_next: float32 [16, 512, 1536], P(None, 'tensor', 'dp')
- router_next: float32 [1536, 16], P('dp')
- router_first_next: float32 [1536, 16], P('dp')
- router_second_next: float32 [1536, 16], P('dp')
- gains_next: float32 [2, 1536], P(None, 'dp')
- gains_first_next: float32 [2, 1536], P(None, 'dp')
- gains_second_next: float32 [2, 1536], P(None, 'dp')
Inputs may be any that keep to these rules, and one draw needn't show every extreme that they name: `routes`: in each block of 640 rows no expert is named by more than 512 rows, and in every draw some expert of some block by exactly 512; the 8 experts of a row differ.
All inputs are finite; a program needn't handle non-finite values.
Results may differ from a plain program's by a relative error of at most 0.015.
Values may be sent and summed in bfloat16 or wider, within the bound.
A program may use at most 576 MiB of HBM per device.

v0:
```python
import jax
import jax.numpy as jnp
from jax import lax
from jax.sharding import PartitionSpec as P

HEAD_DIM = 64
TOPK = 8
EXPERTS = 16
PROMPT_DEV = 128
CONT = 512
MICRO = 2
STEP = 10
GROUP = 3
TOK_MB = 640
CAP = 512


eps_norm = 1e-05
learn_rates = (0.05, 0.3, 0.05, 0.05, 0.05, 0.4)
beta_first = 0.9
beta_second = 0.95
adam_eps = 1e-08
weight_decay = 0.1


def angles_for(positions, head_size):
    half_dim = head_size // 2
    freqs = 10000.0 ** (-2.0 * jnp.arange(half_dim, dtype=jnp.float32) / head_size)
    angles = positions.astype(jnp.float32)[..., None] * freqs
    return (jnp.cos(angles), jnp.sin(angles))


def rotate(values, cosine, sine):
    half_dim = values.shape[-1] // 2
    first_half = values[..., :half_dim]
    second_half = values[..., half_dim:]
    return jnp.concatenate(
        [first_half * cosine - second_half * sine, second_half * cosine + first_half * sine],
        axis=-1,
    )


def expert_slots(route_rows):
    flat_routes = route_rows.reshape(-1)
    onehot = (flat_routes[:, None] == jnp.arange(EXPERTS, dtype=jnp.int32)[None, :]).astype(
        jnp.int32
    )
    earlier = jnp.cumsum(onehot, axis=0, dtype=jnp.int32) - onehot
    slot_index = jnp.sum(earlier * onehot, axis=1, dtype=jnp.int32)
    destination = flat_routes * CAP + slot_index
    source = (
        jnp.zeros((EXPERTS * CAP,), jnp.int32)
        .at[destination]
        .set(jnp.arange(flat_routes.shape[0], dtype=jnp.int32))
    )
    filled = jnp.zeros((EXPERTS * CAP,), jnp.float32).at[destination].set(1.0)
    return (destination, source, filled)


def adam_update(weight, moment_one, moment_two, gradient, decay_rate, learn_rate):
    first_next = beta_first * moment_one + (1.0 - beta_first) * gradient
    second_next = beta_second * moment_two + (1.0 - beta_second) * gradient * gradient
    corr_first = 1.0 - beta_first**STEP
    corr_second = 1.0 - beta_second**STEP
    update = first_next / corr_first / (jnp.sqrt(second_next / corr_second) + adam_eps)
    return (weight - learn_rate * (update + decay_rate * weight), first_next, second_next)


def micro_step(
    inputs_low, outgrad_low, route_rows, weights_low, gain_pair, cosine, sine, allowed, prompt_total
):
    inproj_low, outproj_low, gateup_low, down_low, router_low = weights_low
    model_width = inproj_low.shape[0]
    kv_local = inproj_low.shape[1]
    hidden_local = down_low.shape[1]
    tok_rows = inputs_low.shape[0]
    query_width = GROUP * HEAD_DIM
    factor = HEAD_DIM ** (-0.5)
    cos_query = cosine[:, None, None, :]
    sin_query = sine[:, None, None, :]
    cos_key = cosine[:, None, :]
    sin_key = sine[:, None, :]
    inproj_flat = inproj_low.reshape(model_width, -1)
    outproj_flat = outproj_low.reshape(-1, model_width)
    inputs = inputs_low.astype(jnp.float32)
    inverse_first = lax.rsqrt(jnp.mean(inputs * inputs, axis=-1, keepdims=True) + eps_norm)
    norm_first = inputs * inverse_first
    normed_first = (norm_first * gain_pair[0]).astype(jnp.bfloat16)
    mixed = jnp.dot(normed_first, inproj_flat, preferred_element_type=jnp.float32).reshape(
        tok_rows, kv_local, -1
    )
    queries = rotate(
        mixed[..., :query_width].reshape(tok_rows, kv_local, GROUP, HEAD_DIM), cos_query, sin_query
    ).astype(jnp.bfloat16)
    keys = rotate(mixed[..., query_width : query_width + HEAD_DIM], cos_key, sin_key).astype(
        jnp.bfloat16
    )
    values = mixed[..., query_width + HEAD_DIM :].astype(jnp.bfloat16)
    prompt_keys, prompt_values = (
        lax.all_gather(keys[:PROMPT_DEV], "dp", axis=0, tiled=True),
        lax.all_gather(values[:PROMPT_DEV], "dp", axis=0, tiled=True),
    )
    keys_all = jnp.concatenate([prompt_keys, keys[PROMPT_DEV:]], axis=0)
    values_all = jnp.concatenate([prompt_values, values[PROMPT_DEV:]], axis=0)
    scores = (
        jnp.einsum("tkgd,skd->kgts", queries, keys_all, preferred_element_type=jnp.float32) * factor
    )
    scores = jnp.where(allowed, scores, -1e30)
    row_max = jnp.max(scores, axis=-1, keepdims=True)
    exponent = jnp.exp(scores - row_max)
    softened = exponent / jnp.sum(exponent, axis=-1, keepdims=True)
    soft_low = softened.astype(jnp.bfloat16)
    attended = (
        jnp.einsum("kgts,skd->tkgd", soft_low, values_all, preferred_element_type=jnp.float32)
        .astype(jnp.bfloat16)
        .reshape(tok_rows, -1)
    )
    branch = lax.psum(jnp.dot(attended, outproj_flat, preferred_element_type=jnp.float32), "tensor")
    middle = inputs + branch
    inverse_second = lax.rsqrt(jnp.mean(middle * middle, axis=-1, keepdims=True) + eps_norm)
    norm_second = middle * inverse_second
    normed_own = (norm_second * gain_pair[1]).astype(jnp.bfloat16)
    logits = jnp.dot(normed_own, router_low, preferred_element_type=jnp.float32)
    onehot = (route_rows[..., None] == jnp.arange(EXPERTS, dtype=jnp.int32)).astype(jnp.float32)
    chosen = jnp.sum(onehot * logits[:, None, :], axis=-1)
    gates = jax.nn.softmax(chosen, axis=-1)
    destination, source, filled = expert_slots(route_rows)
    token_of_slot = source // TOPK
    expert_rows = normed_own[token_of_slot].reshape(EXPERTS, CAP, model_width)
    gateup_flat = gateup_low.reshape(EXPERTS, model_width, -1)
    hidden = jnp.einsum(
        "ecd,edf->ecf", expert_rows, gateup_flat, preferred_element_type=jnp.float32
    )
    gate_part = hidden[..., :hidden_local]
    up_part = hidden[..., hidden_local:]
    sigmoid_gate = jax.nn.sigmoid(gate_part)
    silu_gate = gate_part * sigmoid_gate
    active = (silu_gate * up_part).astype(jnp.bfloat16)
    result = jnp.einsum("ecf,efd->ecd", active, down_low, preferred_element_type=jnp.float32)
    picked = result.reshape(EXPERTS * CAP, model_width)[destination].reshape(
        tok_rows, TOPK, model_width
    )
    outgrad = outgrad_low.astype(jnp.float32)
    mixture = lax.psum(
        jnp.sum(picked * gates[..., None], axis=1).astype(jnp.bfloat16), "tensor"
    ).astype(jnp.float32)
    block_out = (middle + mixture).astype(jnp.bfloat16)
    gate_grad = lax.psum(jnp.sum(picked * outgrad[:, None, :], axis=-1), "tensor")
    slot_gate = gates.reshape(-1)[source] * filled
    result_grad = (
        (slot_gate[:, None] * outgrad[token_of_slot])
        .astype(jnp.bfloat16)
        .reshape(EXPERTS, CAP, model_width)
    )
    active_grad = jnp.einsum(
        "ecd,efd->ecf", result_grad, down_low, preferred_element_type=jnp.float32
    )
    down_grad = jnp.einsum("ecf,ecd->efd", active, result_grad, preferred_element_type=jnp.float32)
    gate_part_grad = active_grad * up_part * sigmoid_gate * (1.0 + gate_part * (1.0 - sigmoid_gate))
    up_part_grad = active_grad * silu_gate
    hidden_grad = jnp.concatenate([gate_part_grad, up_part_grad], axis=-1).astype(jnp.bfloat16)
    gateup_grad = jnp.einsum(
        "ecd,ecf->edf", expert_rows, hidden_grad, preferred_element_type=jnp.float32
    ).reshape(gateup_low.shape)
    rows_grad = jnp.einsum(
        "ecf,edf->ecd", hidden_grad, gateup_flat, preferred_element_type=jnp.float32
    )
    normed_second_part = jnp.sum(
        rows_grad.reshape(EXPERTS * CAP, model_width)[destination].reshape(
            tok_rows, TOPK, model_width
        ),
        axis=1,
    )
    chosen_grad = gates * (gate_grad - jnp.sum(gates * gate_grad, axis=-1, keepdims=True))
    logits_grad = jnp.sum(onehot * chosen_grad[..., None], axis=1).astype(jnp.bfloat16)
    router_grad = jnp.dot(normed_own.T, logits_grad, preferred_element_type=jnp.float32)
    normed_second_grad = lax.psum(normed_second_part, "tensor") + jnp.dot(
        logits_grad, router_low.T, preferred_element_type=jnp.float32
    )
    norm_second_grad = normed_second_grad * gain_pair[1]
    gain_second_grad = jnp.sum(normed_second_grad * norm_second, axis=0)
    middle_grad = outgrad + inverse_second * (
        norm_second_grad
        - norm_second * jnp.mean(norm_second_grad * norm_second, axis=-1, keepdims=True)
    )
    branch_own = middle_grad.astype(jnp.bfloat16)
    outproj_grad = jnp.dot(attended.T, branch_own, preferred_element_type=jnp.float32).reshape(
        outproj_low.shape
    )
    attended_grad = (
        jnp.dot(branch_own, outproj_flat.T, preferred_element_type=jnp.float32)
        .astype(jnp.bfloat16)
        .reshape(tok_rows, kv_local, GROUP, HEAD_DIM)
    )
    soft_grad = jnp.einsum(
        "tkgd,skd->kgts", attended_grad, values_all, preferred_element_type=jnp.float32
    )
    values_all_grad = jnp.einsum(
        "kgts,tkgd->skd", soft_low, attended_grad, preferred_element_type=jnp.float32
    )
    row_delta = jnp.sum(softened * soft_grad, axis=-1, keepdims=True)
    scores_grad = (softened * (soft_grad - row_delta)).astype(jnp.bfloat16)
    queries_grad = (
        jnp.einsum("kgts,skd->tkgd", scores_grad, keys_all, preferred_element_type=jnp.float32)
        * factor
    )
    keys_all_grad = (
        jnp.einsum("kgts,tkgd->skd", scores_grad, queries, preferred_element_type=jnp.float32)
        * factor
    )
    prompt_keys_grad, prompt_values_grad = (
        lax.psum_scatter(keys_all_grad[:prompt_total], "dp", scatter_dimension=0, tiled=True),
        lax.psum_scatter(values_all_grad[:prompt_total], "dp", scatter_dimension=0, tiled=True),
    )
    keys_grad = jnp.concatenate([prompt_keys_grad, keys_all_grad[prompt_total:]], axis=0)
    values_grad = jnp.concatenate([prompt_values_grad, values_all_grad[prompt_total:]], axis=0)
    queries_raw_grad = rotate(queries_grad, cos_query, -sin_query).reshape(tok_rows, kv_local, -1)
    keys_raw_grad = rotate(keys_grad, cos_key, -sin_key)
    mixed_grad = (
        jnp.concatenate([queries_raw_grad, keys_raw_grad, values_grad], axis=-1)
        .astype(jnp.bfloat16)
        .reshape(tok_rows, -1)
    )
    inproj_grad = jnp.dot(normed_first.T, mixed_grad, preferred_element_type=jnp.float32).reshape(
        inproj_low.shape
    )
    normed_first_grad = lax.psum(
        jnp.dot(mixed_grad, inproj_flat.T, preferred_element_type=jnp.float32).astype(jnp.bfloat16),
        "tensor",
    ).astype(jnp.float32)
    norm_first_grad = normed_first_grad * gain_pair[0]
    gain_first_grad = jnp.sum(normed_first_grad * norm_first, axis=0)
    inputs_grad = middle_grad + inverse_first * (
        norm_first_grad
        - norm_first * jnp.mean(norm_first_grad * norm_first, axis=-1, keepdims=True)
    )
    gains_grad = jnp.stack([gain_first_grad, gain_second_grad], axis=0)
    grads = (inproj_grad, outproj_grad, gateup_grad, down_grad, router_grad, gains_grad)
    return (block_out, inputs_grad, grads)


def shards(
    tokens,
    cotangent,
    routes,
    inproj_weight,
    inproj_first,
    inproj_second,
    outproj_weight,
    outproj_first,
    outproj_second,
    gateup_weight,
    gateup_first,
    gateup_second,
    down_weight,
    down_first,
    down_second,
    router_weight,
    router_first,
    router_second,
    gains,
    gains_first,
    gains_second,
):
    gathered = (
        lax.all_gather(inproj_weight, "dp", axis=0, tiled=True),
        lax.all_gather(outproj_weight, "dp", axis=2, tiled=True),
        lax.all_gather(gateup_weight, "dp", axis=1, tiled=True),
        lax.all_gather(down_weight, "dp", axis=2, tiled=True),
        lax.all_gather(router_weight, "dp", axis=0, tiled=True),
        lax.all_gather(gains, "dp", axis=1, tiled=True),
    )
    inproj_full, outproj_full, gateup_full, down_full, router_full, gain_pair = gathered
    weights_low = (
        inproj_full.astype(jnp.bfloat16),
        outproj_full.astype(jnp.bfloat16),
        gateup_full.astype(jnp.bfloat16),
        down_full.astype(jnp.bfloat16),
        router_full.astype(jnp.bfloat16),
    )
    prompt_total = PROMPT_DEV * lax.axis_size("dp")
    device_index = lax.axis_index("dp")
    inner = jnp.arange(TOK_MB, dtype=jnp.int32)
    positions = jnp.where(
        inner < PROMPT_DEV, device_index * PROMPT_DEV + inner, prompt_total + inner - PROMPT_DEV
    )
    cosine, sine = angles_for(positions, HEAD_DIM)
    key_index = jnp.arange(prompt_total + CONT, dtype=jnp.int32)
    allowed = (key_index[None, :] <= positions[:, None]) & (
        (key_index[None, :] < prompt_total) | (inner[:, None] >= PROMPT_DEV)
    )
    totals = None
    out_blocks = []
    grad_blocks = []
    for micro_index in range(MICRO):
        row_start = micro_index * TOK_MB
        block_out, inputs_grad, grads = micro_step(
            tokens[row_start : row_start + TOK_MB],
            cotangent[row_start : row_start + TOK_MB],
            routes[row_start : row_start + TOK_MB],
            weights_low,
            gain_pair,
            cosine,
            sine,
            allowed,
            prompt_total,
        )
        out_blocks.append(block_out)
        grad_blocks.append(inputs_grad)
        totals = (
            tuple(grads) if totals is None else jax.tree.map(jnp.add, tuple(totals), tuple(grads))
        )
    reduced = tuple(
        (
            lax.psum_scatter(totals[0], "dp", scatter_dimension=0, tiled=True),
            lax.psum_scatter(totals[1], "dp", scatter_dimension=2, tiled=True),
            lax.psum_scatter(totals[2], "dp", scatter_dimension=1, tiled=True),
            lax.psum_scatter(totals[3], "dp", scatter_dimension=2, tiled=True),
            lax.psum_scatter(totals[4], "dp", scatter_dimension=0, tiled=True),
            lax.psum_scatter(totals[5], "dp", scatter_dimension=1, tiled=True),
        )
    )
    tokens_grad = jnp.concatenate(grad_blocks, axis=0)
    triples = (
        (inproj_weight, inproj_first, inproj_second),
        (outproj_weight, outproj_first, outproj_second),
        (gateup_weight, gateup_first, gateup_second),
        (down_weight, down_first, down_second),
        (router_weight, router_first, router_second),
        (gains, gains_first, gains_second),
    )
    decays = (weight_decay, weight_decay, weight_decay, weight_decay, weight_decay, 0.0)
    results = [jnp.concatenate(out_blocks, axis=0), tokens_grad]
    for triple, gradient, decay_rate, learn_rate in zip(triples, reduced, decays, learn_rates):
        results.extend(
            adam_update(triple[0], triple[1], triple[2], gradient, decay_rate, learn_rate)
        )
    return tuple(results)


def solution(mesh):
    return jax.shard_map(
        shards,
        mesh=mesh,
        in_specs=(
            P("dp", None),
            P("dp", None),
            P("dp", None),
            P("dp", "tensor", None),
            P("dp", "tensor", None),
            P("dp", "tensor", None),
            P("tensor", None, "dp"),
            P("tensor", None, "dp"),
            P("tensor", None, "dp"),
            P(None, "dp", None, "tensor"),
            P(None, "dp", None, "tensor"),
            P(None, "dp", None, "tensor"),
            P(None, "tensor", "dp"),
            P(None, "tensor", "dp"),
            P(None, "tensor", "dp"),
            P("dp", None),
            P("dp", None),
            P("dp", None),
            P(None, "dp"),
            P(None, "dp"),
            P(None, "dp"),
        ),
        out_specs=(
            P("dp", None),
            P("dp", None),
            P("dp", "tensor", None),
            P("dp", "tensor", None),
            P("dp", "tensor", None),
            P("tensor", None, "dp"),
            P("tensor", None, "dp"),
            P("tensor", None, "dp"),
            P(None, "dp", None, "tensor"),
            P(None, "dp", None, "tensor"),
            P(None, "dp", None, "tensor"),
            P(None, "tensor", "dp"),
            P(None, "tensor", "dp"),
            P(None, "tensor", "dp"),
            P("dp", None),
            P("dp", None),
            P("dp", None),
            P(None, "dp"),
            P(None, "dp"),
            P(None, "dp"),
        ),
        check_vma=False,
    )
```

profile of v0, /device:TPU:0, one launch (start us, length us, event | category | flops | bytes accessed | tf_op | source)
XLA Modules:
  0.0 2258.5 jit_solution(10479332406125970864)
XLA Ops:
  42.5 27.9 %all-gather.7.cloned.1.call-done = bf16[1536,2,320]{2,1,0:T(2,128)(2,1)} async-done(((bf16[192,2,320]{2,1,0:T(2,128)(2,1)}), bf16[1536,2,320]{2,1,0:T(2,128)(2,1)}) %all-gather.7.cloned.1.call-update) | async-done | bytes 1966096 | tf_op jit(solution)/shard_map/all_gather | solution.py:266
  208.2 19.8 scatter_custom_fusion
  228.0 19.8 scatter_custom_fusion.2
  248.2 19.8 scatter_custom_fusion.3
  268.0 19.3 scatter_custom_fusion.1
  294.3 55.5 %gather_fusion.8 = f32[8192,1536]{1,0:T(8,128)} fusion(f32[640,1536]{1,0:T(8,128)} %get-tuple-element.201, s32[8192]{0:T(1024)S(1)} %get-tuple-element.235), kind=kCustom, calls=%fused_computation.8 | custom fusion | bytes 100696064 | tf_op jit(solution)/shard_map/gather | solution.py:151
  349.8 48.9 %copy.317 = f32[16,512,1536]{1,2,0:T(8,128)} copy(f32[16,512,1536]{2,1,0:T(8,128)} %bitcast.323) | data formatting | bytes 100663296 | tf_op jit(solution)/shard_map/gather | solution.py:151
  399.3 54.9 %gather_fusion.5 = f32[8192,1536]{1,0:T(8,128)} fusion(f32[640,1536]{1,0:T(8,128)} %get-tuple-element.200, s32[8192]{0:T(1024)S(1)} %get-tuple-element.233), kind=kCustom, calls=%fused_computation.5 | custom fusion | bytes 100696064 | tf_op jit(solution)/shard_map/gather | solution.py:151
  454.3 49.4 %copy.308 = f32[16,512,1536]{1,2,0:T(8,128)} copy(f32[16,512,1536]{2,1,0:T(8,128)} %bitcast.324) | data formatting | bytes 100663296 | tf_op jit(solution)/shard_map/gather | solution.py:151
  523.4 51.9 %gather_fusion = bf16[8192,1536]{1,0:T(8,128)(2,1)} fusion(bf16[640,1536]{1,0:T(8,128)(2,1)} %get-tuple-element.238, s32[8192]{0:T(1024)S(1)} %get-tuple-element.233), kind=kCustom, calls=%fused_computation | custom fusion | bytes 50364416 | tf_op jit(solution)/shard_map/gather | solution.py:129
  575.3 37.3 %gather_fusion.2 = bf16[8192,1536]{1,0:T(8,128)(2,1)} fusion(bf16[640,1536]{1,0:T(8,128)(2,1)S(1)} %get-tuple-element.239, s32[8192]{0:T(1024)S(1)} %copy-done.91), kind=kCustom, calls=%fused_computation.2 | custom fusion | bytes 50364416 | tf_op jit(solution)/shard_map/gather | solution.py:129
  616.6 45.5 %gather_fusion.7 = f32[8192]{0:T(1024)S(1)} fusion(f32[5120]{0:T(1024)S(1)} %div.220, s32[8192]{0:T(1024)S(1)} %copy-done.113), kind=kCustom, calls=%fused_computation.7 | custom fusion | bytes 98304 | tf_op jit(solution)/shard_map/gather | solution.py:149
  662.7 45.5 %gather_fusion.4 = f32[8192]{0:T(1024)S(1)} fusion(f32[5120]{0:T(1024)S(1)} %div.217, s32[8192]{0:T(1024)S(1)} %copy-done.112), kind=kCustom, calls=%fused_computation.4 | custom fusion | bytes 98304 | tf_op jit(solution)/shard_map/gather | solution.py:149
  708.9 31.3 %copy.295 = bf16[16,1536,2,128]{1,3,2,0:T(8,128)(2,1)} copy(bf16[16,1536,2,128]{3,2,1,0:T(2,128)(2,1)} %all-gather.11.cloned.1.call-done) | data formatting | bytes 25165824 | tf_op jit(solution)/shard_map/convert_element_type | solution.py:277
  740.1 17.7 fusion.220
  757.8 17.9 fusion.224
  775.8 23.9 %multiply_convert_fusion.9 = (bf16[16,512,128]{1,2,0:T(8,128)(2,1)S(1)}, bf16[16,512,128]{1,2,0:T(8,128)(2,1)}, bf16[16,512,128]{1,2,0:T(8,128)(2,1)}) fusion(f32[16,512,256]{1,2,0:T(8,128)} %fusion.224, bf16[16,128,1536]{2,1,0:T(8,128)(2,1)} %copy.297, f32[16,512,1536]{1,2,0:T(8,128)} %copy.317, f32[16,512]{1,0:T(8,128)S(1)} %mul.945), kind=kOutput, calls=%fused_computation.89 | convolution fusion | flops 3262119936 | bytes 71335936 | tf_op jit(solution)/shard_map/ecd,efd->ecf/dot_general | solution.py:155
  799.7 23.4 %fusion.64 = f32[16,512,1536]{2,1,0:T(8,128)} fusion(bf16[16,1536,256]{1,2,0:T(8,128)(2,1)} %bitcast.329, bf16[16,512,128]{1,2,0:T(8,128)(2,1)} %get-tuple-element.193, bf16[16,512,128]{1,2,0:T(8,128)(2,1)S(1)} %get-tuple-element.192), kind=kOutput, calls=%fused_computation.138 | convolution fusion | flops 6450839552 | bytes 67108864 | tf_op jit(solution)/shard_map/ecf,edf->ecd/dot_general | solution.py:165
  823.1 49.2 %gather_fusion.9 = f32[5120,1536]{1,0:T(8,128)} fusion(f32[8192,1536]{1,0:T(8,128)} %bitcast.322, s32[5120]{0:T(1024)S(1)} %copy-done.100), kind=kCustom, calls=%fused_computation.9 | custom fusion | bytes 62935040 | tf_op jit(solution)/shard_map/gather | solution.py:169
  872.4 16.3 bitcast_reduce_fusion
  888.6 24.0 %multiply_convert_fusion.11 = (bf16[16,512,128]{1,2,0:T(8,128)(2,1)S(1)}, bf16[16,512,128]{1,2,0:T(8,128)(2,1)}, bf16[16,512,128]{1,2,0:T(8,128)(2,1)}) fusion(f32[16,512,256]{1,2,0:T(8,128)} %fusion.220, bf16[16,128,1536]{2,1,0:T(8,128)(2,1)} %copy.297, f32[16,512,1536]{1,2,0:T(8,128)} %copy.308, f32[16,512]{1,0:T(8,128)S(1)} %copy-done.47), kind=kOutput, calls=%fused_computation.91 | convolution fusion | flops 3262119936 | bytes 71335936 | tf_op jit(solution)/shard_map/ecd,efd->ecf/dot_general | solution.py:155
  912.6 23.4 %fusion.66 = f32[16,512,1536]{2,1,0:T(8,128)} fusion(bf16[16,1536,256]{1,2,0:T(8,128)(2,1)} %bitcast.330, bf16[16,512,128]{1,2,0:T(8,128)(2,1)} %get-tuple-element.191, bf16[16,512,128]{1,2,0:T(8,128)(2,1)S(1)} %get-tuple-element.190), kind=kOutput, calls=%fused_computation.140 | convolution fusion | flops 6450839552 | bytes 67108864 | tf_op jit(solution)/shard_map/ecf,edf->ecd/dot_general | solution.py:165
  936.0 49.2 %gather_fusion.6 = f32[5120,1536]{1,0:T(8,128)} fusion(f32[8192,1536]{1,0:T(8,128)} %bitcast.321, s32[5120]{0:T(1024)S(1)} %copy-done.99), kind=kCustom, calls=%fused_computation.6 | custom fusion | bytes 62935040 | tf_op jit(solution)/shard_map/gather | solution.py:169
  985.3 16.3 bitcast_reduce_fusion.1
  1003.2 22.7 %fusion.225 = f32[16,512,1536]{2,1,0:T(8,128)} fusion(bf16[16,512,128]{1,2,0:T(8,128)(2,1)S(1)} %copy-done.21, bf16[16,128,1536]{2,1,0:T(8,128)(2,1)} %copy.297), kind=kOutput, calls=%fused_computation.376 | convolution fusion | flops 3221225472 | bytes 58720256 | tf_op jit(solution)/shard_map/ecf,efd->ecd/dot_general | solution.py:139
  1025.9 49.3 %gather_fusion.3 = f32[5120,1536]{1,0:T(8,128)} fusion(f32[8192,1536]{1,0:T(8,128)} %bitcast.320, s32[5120]{0:T(1024)S(1)} %copy-done.101), kind=kCustom, calls=%fused_computation.3 | custom fusion | bytes 62935040 | tf_op jit(solution)/shard_map/gather | solution.py:140
  1075.1 15.5 fusion.3
  1090.7 22.5 fusion.221
  1113.2 49.3 %gather_fusion.1 = f32[5120,1536]{1,0:T(8,128)} fusion(f32[8192,1536]{1,0:T(8,128)} %bitcast.319, s32[5120]{0:T(1024)S(1)} %copy-done.99), kind=kCustom, calls=%fused_computation.1 | custom fusion | bytes 62935040 | tf_op jit(solution)/shard_map/gather | solution.py:140
  1178.1 25.5 %all-reduce = (f32[640,8]{0,1:T(8,128)S(1)}, f32[640,8]{0,1:T(8,128)S(1)}) all-reduce(f32[640,8]{0,1:T(8,128)S(1)} %copy.321, f32[640,8]{0,1:T(8,128)S(1)} %copy.312), channel_id=1, replica_groups=mesh['dp'=8,'tensor'=4] {'tensor'}, use_global_device_ids=true, to_apply=%region_45.46 | all-reduce | flops 10240 | bytes 81920 | tf_op jit(solution)/shard_map/psum | solution.py:148
  1203.9 73.4 %all-reduce.8.cloned.1.call-done = (f32[640,1536]{1,0:T(8,128)}, f32[640,1536]{1,0:T(8,128)}) async-done(((f32[640,1536]{1,0:T(8,128)}, f32[640,1536]{1,0:T(8,128)}), (f32[640,1536]{1,0:T(8,128)}, f32[640,1536]{1,0:T(8,128)})) %all-reduce.8.cloned.1.call-update) | async-done | bytes 7864336 | tf_op jit(solution)/shard_map/psum | solution.py:177
  1303.0 18.3 fusion.6
  1332.2 15.4 fusion.9
  1347.6 15.7 fusion.8
  1368.6 20.5 fusion.11
  1419.2 20.7 reduce-scatter.17.cloned.1.call-done
  1441.2 36.5 %reduce-scatter.23.cloned.1.call-done = f32[128,2,64]{0,2,1:T(8,128)} async-done(((f32[1024,2,64]{0,2,1:T(8,128)}), f32[128,2,64]{0,2,1:T(8,128)}) %reduce-scatter.23.cloned.1.call-update) | async-done | bytes 65552 | tf_op jit(solution)/shard_map/reduce_scatter | solution.py:213
  1481.8 34.0 %reduce-scatter.19.cloned.1.call-done = f32[128,2,64]{0,2,1:T(8,128)} async-done(((f32[1024,2,64]{0,2,1:T(8,128)}), f32[128,2,64]{0,2,1:T(8,128)}) %reduce-scatter.19.cloned.1.call-update) | async-done | bytes 65552 | tf_op jit(solution)/shard_map/reduce_scatter | solution.py:213
  1549.7 23.3 %fusion.20 = f32[16,128,1536]{1,2,0:T(8,128)} fusion(bf16[16,512,128]{1,2,0:T(8,128)(2,1)S(1)} %copy-done.20, f32[16,512,1536]{1,2,0:T(8,128)} %copy.308, f32[16,512]{1,0:T(8,128)S(1)} %copy-done.48), kind=kOutput, calls=%fused_computation.53 | convolution fusion | flops 3246391296 | bytes 65044480 | tf_op jit(solution)/shard_map/ecf,ecd->efd/dot_general | solution.py:158
  1573.0 221.7 %all-reduce.12.cloned.1.call-done = (bf16[640,1536]{1,0:T(8,128)(2,1)}, bf16[640,1536]{1,0:T(8,128)(2,1)}, bf16[640,1536]{1,0:T(8,128)(2,1)}, bf16[640,1536]{1,0:T(8,128)(2,1)}) async-done(((bf16[640,1536]{1,0:T(8,128)(2,1)}, bf16[640,1536]{1,0:T(8,128)(2,1)}, bf16[640,1536]{1,0:T(8,128)(2,1)}, bf16[640,1536]{1,0:T(8,128)(2,1)}), (bf16[640,1536]{1,0:T(8,128)(2,1)}, bf16[640,1536]{1,0:T(8,128)(2,1)}, ...) | async-done | bytes 7864336 | tf_op jit(solution)/shard_map/psum | solution.py:144
  1801.5 26.6 %fusion.24 = f32[16,128,1536]{1,2,0:T(8,128)} fusion(f32[16,128,1536]{1,2,0:T(8,128)} %fusion.20, bf16[16,512,128]{1,2,0:T(8,128)(2,1)S(1)} %copy-done.22, f32[16,512,1536]{1,2,0:T(8,128)} %copy.317, f32[16,512]{1,0:T(8,128)S(1)} %copy-done.62), kind=kOutput, calls=%fused_computation.58 | convolution fusion | flops 3249537024 | bytes 77627392 | tf_op jit(solution)/shard_map/ecf,ecd->efd/dot_general | solution.py:158
  1828.2 17.8 fusion.65
  1846.0 27.2 %convolution_add_fusion = f32[16,1536,256]{1,2,0:T(8,128)} fusion(f32[16,1536,256]{1,2,0:T(8,128)} %fusion.65, bf16[16,512,1536]{2,1,0:T(8,128)(2,1)} %bitcast.333, bf16[16,512,128]{1,2,0:T(8,128)(2,1)} %get-tuple-element.193, bf16[16,512,128]{1,2,0:T(8,128)(2,1)S(1)} %copy-done.24), kind=kOutput, calls=%fused_computation.42 | convolution fusion | flops 6457131008 | bytes 79691776 | tf_op jit(solution)/shard_map/ecd,ecf->edf/dot_general | solution.py:162
  1873.2 25.5 %copy.332 = f32[16,1536,2,128]{3,0,2,1:T(8,128)} copy(f32[16,1536,2,128]{1,3,2,0:T(8,128)} %bitcast.331) | data formatting | bytes 50331648 | tf_op jit(solution)/shard_map/add | solution.py:311
  1903.3 33.4 %reduce-scatter.25.cloned.1.call-done = f32[192,2,320]{2,0,1:T(8,128)} async-done(((f32[1536,2,320]{2,0,1:T(8,128)}), f32[192,2,320]{2,0,1:T(8,128)}) %reduce-scatter.25.cloned.1.call-update) | async-done | bytes 491536 | tf_op jit(solution)/shard_map/reduce_scatter | solution.py:315
  1959.1 16.1 reduce-scatter.35.cloned.1.call-done
  1976.8 94.2 %reduce-scatter.29.cloned.1.call-done = f32[16,128,192]{1,2,0:T(8,128)} async-done(((f32[16,128,1536]{1,2,0:T(8,128)}), f32[16,128,192]{1,2,0:T(8,128)}) %reduce-scatter.29.cloned.1.call-update) | async-done | bytes 1572880 | tf_op jit(solution)/shard_map/reduce_scatter | solution.py:318
  2076.9 154.5 %reduce-scatter.27.cloned.1.call-done = f32[16,192,2,128]{3,0,2,1:T(8,128)} async-done(((f32[16,1536,2,128]{3,0,2,1:T(8,128)}), f32[16,192,2,128]{3,0,2,1:T(8,128)}) %reduce-scatter.27.cloned.1.call-update) | async-done | bytes 3145744 | tf_op jit(solution)/shard_map/reduce_scatter | solution.py:317
  (539 shorter events, 394.3 us)
Async XLA Ops:
  7.2 31.8 %all-gather.9.cloned.1.call-start = ((), (), s32[]{:S(2)}) async-start(), calls=%async_computation.11 | async-start | bytes 1769472 | tf_op jit(solution)/shard_map/all_gather | solution.py:267
  9.2 61.3 %all-gather.7.cloned.1.call-start = ((), (), s32[]{:S(2)}) async-start(), calls=%async_computation.10 | async-start | bytes 2654208 | tf_op jit(solution)/shard_map/all_gather | solution.py:266
  11.2 493.7 %all-gather.13.cloned.1.call-start = ((), (), s32[]{:S(2)}) async-start(), calls=%async_computation.13 | async-start | bytes 7077888 | tf_op jit(solution)/shard_map/all_gather | solution.py:269
  14.5 499.5 %all-reduce.10.cloned.1.call-start = ((), (), s32[]{:S(2)}) async-start(), calls=%async_computation.25 | async-start | bytes 15728640 | tf_op jit(solution)/shard_map/psum | solution.py:118
  28.7 52.4 %copy-start.130 = (f32[1536]{0:T(1024)}, f32[1536]{0:T(1024)S(1)}, u32[]{:S(2)}) copy-start(f32[1536]{0:T(1024)S(1)} %get-tuple-element.157) | copy-start | bytes 18436
  28.7 47.6 %copy-start.145 = (f32[640]{0:T(1024)}, f32[640]{0:T(1024)S(1)}, u32[]{:S(2)}) copy-start(f32[640]{0:T(1024)S(1)} %get-tuple-element.257) | copy-start | bytes 7684
  28.7 52.4 %copy-start.143 = (f32[640]{0:T(1024)}, f32[640]{0:T(1024)S(1)}, u32[]{:S(2)}) copy-start(f32[640]{0:T(1024)S(1)} %get-tuple-element.256) | copy-start | bytes 7684
  29.7 75.7 %copy-start.71 = (f32[640,32]{0,1:T(8,128)}, f32[640,32]{0,1:T(8,128)S(1)}, u32[]{:S(2)}) copy-start(f32[640,32]{0,1:T(8,128)S(1)} %get-tuple-element.241) | copy-start | bytes 245764
  29.7 95.2 %copy-start.39 = (f32[640,32]{0,1:T(8,128)}, f32[640,32]{0,1:T(8,128)S(1)}, u32[]{:S(2)}) copy-start(f32[640,32]{0,1:T(8,128)S(1)} %get-tuple-element.242) | copy-start | bytes 245764
  42.5 135.1 %copy-start.17 = (bf16[2,192,1536]{2,1,0:T(8,128)(2,1)}, bf16[2,192,1536]{2,1,0:T(8,128)(2,1)S(1)}, u32[]{:S(2)}) copy-start(bf16[2,192,1536]{2,1,0:T(8,128)(2,1)S(1)} %copy.291) | copy-start | bytes 3538948
  181.5 527.3 %all-gather.11.cloned.1.call-start = ((), (), s32[]{:S(2)}) async-start(), calls=%async_computation.12 | async-start | bytes 14155776 | tf_op jit(solution)/shard_map/all_gather | solution.py:268
  185.9 1091.4 %all-reduce.8.cloned.1.call-start = ((), (), s32[]{:S(2)}) async-start(), calls=%async_computation.24 | async-start | bytes 15728640 | tf_op jit(solution)/shard_map/psum | solution.py:177
  208.2 86.1 %copy-start.126 = (s32[5120,1]{0,1:T(1,128)}, s32[5120,1]{0,1:T(1,128)S(1)}, u32[]{:S(2)}) copy-start(s32[5120,1]{0,1:T(1,128)S(1)} %compare_select_fusion.1) | copy-start | bytes 61444
  349.8 48.9 %copy-start.106 = (s32[8192]{0:T(1024)S(1)}, s32[8192]{0:T(1024)}, u32[]{:S(2)}) copy-start(s32[8192]{0:T(1024)} %scatter_custom_fusion) | copy-start | bytes 98308
  454.3 49.4 %copy-start.127 = (s32[5120,1]{0,1:T(1,128)S(1)}, s32[5120,1]{0,1:T(1,128)}, u32[]{:S(2)}) copy-start(s32[5120,1]{0,1:T(1,128)} %copy-done.126) | copy-start | bytes 61444
  454.3 50.0 %copy-start.129 = (s32[5120,1]{0,1:T(1,128)S(1)}, s32[5120,1]{0,1:T(1,128)}, u32[]{:S(2)}) copy-start(s32[5120,1]{0,1:T(1,128)} %copy-done.128) | copy-start | bytes 61444
  523.4 91.5 %copy-start = (bf16[640,1536]{1,0:T(8,128)(2,1)}, bf16[640,1536]{1,0:T(8,128)(2,1)S(1)}, u32[]{:S(2)}) copy-start(bf16[640,1536]{1,0:T(8,128)(2,1)S(1)} %get-tuple-element.239) | copy-start | bytes 5898244
  523.4 51.9 %copy-start.91 = (s32[8192]{0:T(1024)S(1)}, s32[8192]{0:T(1024)}, u32[]{:S(2)}) copy-start(s32[8192]{0:T(1024)} %copy-done.90) | copy-start | bytes 98308
  614.9 47.4 %copy-start.72 = (f32[640,8]{0,1:T(8,128)}, f32[640,8]{0,1:T(8,128)S(1)}, u32[]{:S(2)}) copy-start(f32[640,8]{0,1:T(8,128)S(1)} %select_reduce_fusion.3) | copy-start | bytes 61444
  614.9 47.4 %copy-start.114 = (f32[640]{0:T(1024)}, f32[640]{0:T(1024)S(1)}, u32[]{:S(2)}) copy-start(f32[640]{0:T(1024)S(1)} %reduce_max.37) | copy-start | bytes 7684
  615.6 46.5 %copy-start.116 = (f32[640]{0:T(1024)}, f32[640]{0:T(1024)S(1)}, u32[]{:S(2)}) copy-start(f32[640]{0:T(1024)S(1)} %reduce_max.39) | copy-start | bytes 7684
  615.7 46.5 %copy-start.134 = (f32[640]{0:T(1024)}, f32[640]{0:T(1024)S(1)}, u32[]{:S(2)}) copy-start(f32[640]{0:T(1024)S(1)} %fusion.149) | copy-start | bytes 7684
  616.6 46.1 %copy-start.112 = (s32[8192]{0:T(1024)S(1)}, s32[8192]{0:T(1024)}, u32[]{:S(2)}) copy-start(s32[8192]{0:T(1024)} %get-tuple-element.232) | copy-start | bytes 98308
  662.2 113.6 %copy-start.61 = (f32[16,512]{1,0:T(8,128)}, f32[16,512]{1,0:T(8,128)S(1)}, u32[]{:S(2)}) copy-start(f32[16,512]{1,0:T(8,128)S(1)} %mul.945) | copy-start | bytes 98308
  662.3 45.9 %copy-start.136 = (f32[640]{0:T(1024)}, f32[640]{0:T(1024)S(1)}, u32[]{:S(2)}) copy-start(f32[640]{0:T(1024)S(1)} %fusion.147) | copy-start | bytes 7684
  1001.6 417.6 %reduce-scatter.21.cloned.1.call-start = ((), (), s32[]{:S(2)}) async-start(), calls=%async_computation.16 | async-start | bytes 589824 | tf_op jit(solution)/shard_map/reduce_scatter | solution.py:212
  1025.8 49.3 %copy-start.31 = (f32[640,8]{1,0:T(8,128)S(1)}, f32[640,8]{1,0:T(8,128)}, u32[]{:S(2)}) copy-start(f32[640,8]{1,0:T(8,128)} %copy-done.30) | copy-start | bytes 61444
  1113.2 49.4 %copy-start.33 = (f32[640,8]{1,0:T(8,128)S(1)}, f32[640,8]{1,0:T(8,128)}, u32[]{:S(2)}) copy-start(f32[640,8]{1,0:T(8,128)} %copy-done.32) | copy-start | bytes 61444
  1162.6 114.6 %copy-start.46 = (bf16[1536,16]{0,1:T(8,128)(2,1)S(1)}, bf16[1536,16]{0,1:T(8,128)(2,1)}, u32[]{:S(2)}) copy-start(bf16[1536,16]{0,1:T(8,128)(2,1)} %reshape.717) | copy-start | bytes 147460
  1203.8 76.5 %copy-start.97 = (bf16[640,16]{0,1:T(8,128)(2,1)}, bf16[640,16]{0,1:T(8,128)(2,1)S(1)}, u32[]{:S(2)}) copy-start(bf16[640,16]{0,1:T(8,128)(2,1)S(1)} %select_reduce_fusion) | copy-start | bytes 61444
  1203.9 76.4 %copy-start.95 = (bf16[640,16]{0,1:T(8,128)(2,1)}, bf16[640,16]{0,1:T(8,128)(2,1)S(1)}, u32[]{:S(2)}) copy-start(bf16[640,16]{0,1:T(8,128)(2,1)S(1)} %select_reduce_fusion.1) | copy-start | bytes 61444
  1303.0 86.9 %copy-start.77 = (f32[1536,2,64]{0,2,1:T(8,128)}, f32[1536,2,64]{0,2,1:T(8,128)S(1)}, u32[]{:S(2)}) copy-start(f32[1536,2,64]{0,2,1:T(8,128)S(1)} %fusion.70) | copy-start | bytes 2359300
  1332.2 56.9 %copy-start.78 = (f32[1536,2,64]{0,2,1:T(8,128)}, f32[1536,2,64]{0,2,1:T(8,128)S(1)}, u32[]{:S(2)}) copy-start(f32[1536,2,64]{0,2,1:T(8,128)S(1)} %fusion.67) | copy-start | bytes 2359300
  1368.5 71.4 %reduce-scatter.17.cloned.1.call-start = ((), (), s32[]{:S(2)}) async-start(), calls=%async_computation.14 | async-start | bytes 589824 | tf_op jit(solution)/shard_map/reduce_scatter | solution.py:212
  1399.7 78.0 %reduce-scatter.23.cloned.1.call-start = ((), (), s32[]{:S(2)}) async-start(), calls=%async_computation.17 | async-start | bytes 589824 | tf_op jit(solution)/shard_map/reduce_scatter | solution.py:213
  1406.3 109.4 %reduce-scatter.19.cloned.1.call-start = ((), (), s32[]{:S(2)}) async-start(), calls=%async_computation.15 | async-start | bytes 589824 | tf_op jit(solution)/shard_map/reduce_scatter | solution.py:213
  1413.0 381.6 %all-reduce.12.cloned.1.call-start = ((), (), s32[]{:S(2)}) async-start(), calls=%async_computation.26 | async-start | bytes 15728640 | tf_op jit(solution)/shard_map/psum | solution.py:144
  1414.3 63.5 %copy-start.41 = (bf16[1536,2,320]{0,2,1:T(8,128)(2,1)S(1)}, bf16[1536,2,320]{0,2,1:T(8,128)(2,1)}, u32[]{:S(2)}) copy-start(bf16[1536,2,320]{0,2,1:T(8,128)(2,1)} %copy-done.40) | copy-start | bytes 5898244
  1419.2 62.6 %copy-start.80 = (bf16[640,2,3,64]{0,3,2,1:T(8,128)(2,1)}, bf16[640,2,3,64]{0,3,2,1:T(8,128)(2,1)S(1)}, u32[]{:S(2)}) copy-start(bf16[640,2,3,64]{0,3,2,1:T(8,128)(2,1)S(1)} %pad_maximum_fusion.9) | copy-start | bytes 1474564
  1441.2 74.5 %copy-start.122 = (bf16[640,2,32]{0,2,1:T(8,128)(2,1)}, bf16[640,2,32]{0,2,1:T(8,128)(2,1)S(1)}, u32[]{:S(2)}) copy-start(bf16[640,2,32]{0,2,1:T(8,128)(2,1)S(1)} %get-tuple-element.216) | copy-start | bytes 245764
  1441.2 74.5 %copy-start.124 = (bf16[640,2,32]{0,2,1:T(8,128)(2,1)}, bf16[640,2,32]{0,2,1:T(8,128)(2,1)S(1)}, u32[]{:S(2)}) copy-start(bf16[640,2,32]{0,2,1:T(8,128)(2,1)S(1)} %get-tuple-element.217) | copy-start | bytes 245764
  1519.7 379.2 %reduce-scatter.33.cloned.1.call-start = ((), (), s32[]{:S(2)}) async-start(), calls=%async_computation.22 | async-start | bytes 884736
  1523.9 376.7 %reduce-scatter.31.cloned.1.call-start = ((), (), s32[]{:S(2)}) async-start(), calls=%async_computation.21 | async-start | bytes 2654208
  1539.3 397.3 %reduce-scatter.25.cloned.1.call-start = ((), (), s32[]{:S(2)}) async-start(), calls=%async_computation.18 | async-start | bytes 5308416 | tf_op jit(solution)/shard_map/reduce_scatter | solution.py:315
  1548.1 427.1 %reduce-scatter.35.cloned.1.call-start = ((), (), s32[]{:S(2)}) async-start(), calls=%async_computation.23 | async-start | bytes 884736
  1801.2 269.8 %reduce-scatter.29.cloned.1.call-start = ((), (), s32[]{:S(2)}) async-start(), calls=%async_computation.20 | async-start | bytes 14155776 | tf_op jit(solution)/shard_map/reduce_scatter | solution.py:318
  1828.1 403.3 %reduce-scatter.27.cloned.1.call-start = ((), (), s32[]{:S(2)}) async-start(), calls=%async_computation.19 | async-start | bytes 28311552 | tf_op jit(solution)/shard_map/reduce_scatter | solution.py:317
  1976.8 254.6 %copy-start.27 = (f32[16,192,2,128]{3,2,1,0:T(2,128)S(1)}, f32[16,192,2,128]{3,2,1,0:T(2,128)}, u32[]{:S(2)}) copy-start(f32[16,192,2,128]{3,2,1,0:T(2,128)} %param.30) | copy-start | bytes 9437188
  (130 other events, 1817.0 us)
Sparse Core Ops, SparseCore 0:
  10.5 28.4 all-gather.8
  41.4 29.0 all-gather.6
  72.9 48.3 all-gather.12
  181.6 274.1 all-reduce.9
  458.2 70.9 all-gather.10
  1001.7 275.5 all-reduce.7
  1368.7 33.1 reduce-scatter.20
  1405.7 34.1 reduce-scatter.16
  1443.6 34.1 reduce-scatter.22
  1481.6 34.1 reduce-scatter.18
  1519.8 274.8 all-reduce.11
  1798.2 33.7 reduce-scatter.32
  1835.9 42.5 reduce-scatter.30
  1882.8 53.8 reduce-scatter.24
  1940.2 34.9 reduce-scatter.34
  1978.6 92.3 reduce-scatter.28
  2074.5 156.8 reduce-scatter.26
where the time goes:
time: 2270 us; the launch traced here: 2260 us
  local copies, waits for them, and re-layouts  807 us (36%)
  waiting for transfers between devices  720 us (32%)
  matrix products  446 us (20%)
  other arithmetic  183 us (8%)
  blocking collectives  84.7 us (4%)
    psum x1, waiting for transfers between devices, micro_step(): lax.psum(jnp.sum(picked * gates[..., None], axis=1).astype(jnp.bfloat16),...  222 us
    gather x4, local copies, waits for them, and re-layouts, micro_step(): outgrad[token_of_slot]  209 us
    reduce_scatter x1, waiting for transfers between devices, shards(): lax.psum_scatter(totals[2], 'dp', scatter_dimension=1, tiled=True)  154 us
    gather x2, local copies, waits for them, and re-layouts, micro_step(): result.reshape(EXPERTS * CAP, model_width)[destination]  98.6 us
    gather x2, local copies, waits for them, and re-layouts, micro_step(): rows_grad.reshape(EXPERTS * CAP, model_width)[destination]  98.4 us
    reduce_scatter x1, waiting for transfers between devices, shards(): lax.psum_scatter(totals[3], 'dp', scatter_dimension=2, tiled=True)  94.2 us
    gather x2, local copies, waits for them, and re-layouts, micro_step(): slot_gate = gates.reshape(-1)[source] * filled  91.1 us
    gather x2, local copies, waits for them, and re-layouts, micro_step(): expert_rows = normed_own[token_of_slot].reshape(EXPERTS, CAP, model_width)  89.1 us
  transfers between devices with their start and end apart: 17, of which 11 were waited for; matrix products, arithmetic and copies ran while one was open for 45% of the time, Pallas kernels for 0%

commit v1 on v0

v1 whole, which is shorter than its diff:
```python
import functools

import jax
import jax.numpy as jnp
from jax import lax
from jax.experimental import pallas as pl
from jax.experimental.pallas import tpu as pltpu
from jax.sharding import PartitionSpec as P

HEAD_DIM = 64
TOPK = 8
EXPERTS = 16
PROMPT_DEV = 128
CONT = 512
MICRO = 2
STEP = 10
GROUP = 3
TOK_MB = 640

eps_norm = 1e-05
beta_first = 0.9
beta_second = 0.95
adam_eps = 1e-08
weight_decay = 0.1
bf16 = jnp.bfloat16
f32 = jnp.float32
MESH = pl.DeviceIdType.MESH


def angles_for(positions, head_size):
    half_dim = head_size // 2
    freqs = 10000.0 ** (-2.0 * jnp.arange(half_dim, dtype=f32) / head_size)
    angles = positions.astype(f32)[..., None] * freqs
    return (jnp.cos(angles), jnp.sin(angles))


def rotate(values, cosine, sine):
    half_dim = values.shape[-1] // 2
    first_half = values[..., :half_dim]
    second_half = values[..., half_dim:]
    return jnp.concatenate(
        [first_half * cosine - second_half * sine, second_half * cosine + first_half * sine],
        axis=-1,
    )


def adam_update(weight, moment_one, moment_two, gradient, decay_rate, learn_rate):
    first_next = beta_first * moment_one + (1.0 - beta_first) * gradient
    second_next = beta_second * moment_two + (1.0 - beta_second) * gradient * gradient
    corr_first = 1.0 - beta_first**STEP
    corr_second = 1.0 - beta_second**STEP
    update = first_next / corr_first / (jnp.sqrt(second_next / corr_second) + adam_eps)
    return (weight - learn_rate * (update + decay_rate * weight), first_next, second_next)


def line_sum_kernel(n, chunks, x_ref, o_ref, held, send_red, recv_red, send_out, recv_out):
    me = lax.axis_index("tensor")
    rows = x_ref.shape[0] // (2 * chunks)
    low, high = me - 1, me + 1

    barrier = pltpu.get_barrier_semaphore()

    @pl.when(me > 0)
    def _():
        pl.semaphore_signal(barrier, inc=1, device_id={"tensor": low}, device_id_type=MESH)

    @pl.when(me < n - 1)
    def _():
        pl.semaphore_signal(barrier, inc=1, device_id={"tensor": high}, device_id_type=MESH)

    pl.semaphore_wait(barrier, jnp.where((me > 0) & (me < n - 1), 2, 1))

    def part(half, c):
        return pl.ds(pl.multiple_of((half * chunks + c) * rows, 16), rows)

    def reduce_copy(half, c, src):
        to = low if half == 0 else high
        return pltpu.make_async_remote_copy(
            src_ref=src.at[part(half, c)],
            dst_ref=held.at[part(half, c)],
            send_sem=send_red.at[half, c],
            recv_sem=recv_red.at[half, c],
            device_id={"tensor": to},
            device_id_type=MESH,
        )

    def out_copy(half, c):
        to = high if half == 0 else low
        return pltpu.make_async_remote_copy(
            src_ref=o_ref.at[part(half, c)],
            dst_ref=o_ref.at[part(half, c)],
            send_sem=send_out.at[half, c],
            recv_sem=recv_out.at[half, c],
            device_id={"tensor": to},
            device_id_type=MESH,
        )

    def place(half):
        return n - 1 - me if half == 0 else me

    def step(s, carry):
        for half in (0, 1):
            at = place(half)

            @pl.when(s < chunks)
            def _():
                @pl.when(at == 0)
                def _():
                    reduce_copy(half, s, x_ref).start()

                @pl.when(at > 0)
                def _():
                    reduce_copy(half, s, held).wait_recv()
                    total = x_ref[part(half, s)].astype(f32) + held[part(half, s)].astype(f32)

                    @pl.when(at < n - 1)
                    def _():
                        held[part(half, s)] = total.astype(held.dtype)
                        reduce_copy(half, s, held).start()

                    @pl.when(at == n - 1)
                    def _():
                        o_ref[part(half, s)] = total.astype(o_ref.dtype)
                        out_copy(half, s).start()

            c = s - 2 * (n - 1 - at)

            @pl.when((at < n - 1) & (c >= 0) & (c < chunks))
            def _():
                out_copy(half, c).wait_recv()

                @pl.when(at > 0)
                def _():
                    out_copy(half, c).start()

        return carry

    lax.fori_loop(0, chunks + 2 * (n - 1), step, 0)

    def finish(c, carry):
        for half in (0, 1):
            at = place(half)

            @pl.when(at < n - 1)
            def _():
                reduce_copy(half, c, held).wait_send()

            @pl.when(at > 0)
            def _():
                out_copy(half, c).wait_send()

        return carry

    lax.fori_loop(0, chunks, finish, 0)


def line_sum(x, n, barrier_id):
    rows, width = x.shape
    chunks = 8
    return pl.pallas_call(
        functools.partial(line_sum_kernel, n, chunks),
        out_shape=jax.ShapeDtypeStruct(x.shape, x.dtype),
        in_specs=[pl.BlockSpec(memory_space=pltpu.VMEM)],
        out_specs=pl.BlockSpec(memory_space=pltpu.VMEM),
        scratch_shapes=[pltpu.VMEM(x.shape, x.dtype)]
        + [pltpu.SemaphoreType.DMA((2, chunks)) for _ in range(4)],
        compiler_params=pltpu.CompilerParams(
            collective_id=barrier_id, has_side_effects=True, vmem_limit_bytes=24 * 2**20
        ),
        cost_estimate=pl.CostEstimate(
            flops=rows * width, bytes_accessed=100 * rows * width, transcendentals=0
        ),
    )(x)


def expert_kernel(group, rows_ref, outgrad_ref, gates_ref, gu_ref, down_ref,
                  active_ref, hidden_ref, gate_grad_ref):
    step = pl.program_id(0)
    tile = 256
    width = gu_ref.shape[1] // 2
    hidden = width // group
    lane = lax.broadcasted_iota(jnp.int32, (tile, 128), 1)
    column = lax.broadcasted_iota(jnp.int32, (tile, width), 1)

    @pl.when(step == 0)
    def _():
        gate_grad_ref[...] = jnp.zeros_like(gate_grad_ref)

    def one(t, carry):
        at = pl.ds(pl.multiple_of(t * tile, tile), tile)
        h = jnp.dot(rows_ref[at], gu_ref[...], preferred_element_type=f32)
        back = jnp.dot(outgrad_ref[at], down_ref[...], preferred_element_type=f32)
        gates = gates_ref[at]
        wide = jnp.zeros((tile, width), f32)
        for j in range(group):
            g = jnp.sum(jnp.where(lane == step * group + j, gates, 0.0), axis=1, keepdims=True)
            wide = g + wide if group == 1 else jnp.where(column // hidden == j, g, wide)
        gate, up = h[:, :width], h[:, width:]
        sig = 1.0 / (1.0 + jnp.exp(-gate))
        silu = gate * sig
        active = (silu * up).astype(bf16).astype(f32)
        active_ref[at] = (active * wide).astype(bf16)
        product = active * back
        grads = gate_grad_ref[at]
        for j in range(group):
            s = jnp.sum(jnp.where(column // hidden == j, product, 0.0), axis=1, keepdims=True)
            grads = jnp.where(lane == step * group + j, s, grads)
        gate_grad_ref[at] = grads
        back = back * wide
        hidden_ref[at, :width] = (back * up * sig * (1.0 + gate * (1.0 - sig))).astype(bf16)
        hidden_ref[at, width:] = (back * silu).astype(bf16)
        return carry

    lax.fori_loop(0, rows_ref.shape[0] // tile, one, 0)


def expert_call(rows, outgrad, gates, gu, down, group):
    tokens, model = rows.shape
    width = gu.shape[1] // (EXPERTS // group)
    steps = EXPERTS // group
    return pl.pallas_call(
        functools.partial(expert_kernel, group),
        grid=(steps,),
        in_specs=[
            pl.BlockSpec((tokens, model), lambda p: (0, 0)),
            pl.BlockSpec((tokens, model), lambda p: (0, 0)),
            pl.BlockSpec((tokens, 128), lambda p: (0, 0)),
            pl.BlockSpec((model, width), lambda p: (0, p)),
            pl.BlockSpec((model, width // 2), lambda p: (0, p)),
        ],
        out_specs=[
            pl.BlockSpec((tokens, width // 2), lambda p: (0, p)),
            pl.BlockSpec((tokens, width), lambda p: (0, p)),
            pl.BlockSpec((tokens, 128), lambda p: (0, 0)),
        ],
        out_shape=[
            jax.ShapeDtypeStruct((tokens, steps * width // 2), bf16),
            jax.ShapeDtypeStruct((tokens, steps * width), bf16),
            jax.ShapeDtypeStruct((tokens, 128), f32),
        ],
        compiler_params=pltpu.CompilerParams(vmem_limit_bytes=48 * 2**20),
        cost_estimate=pl.CostEstimate(
            flops=2 * tokens * model * steps * width * 3 // 2,
            bytes_accessed=2 * (model * steps * width * 3 // 2 + tokens * steps * width * 3 // 2),
            transcendentals=tokens * steps * width // 2,
        ),
    )(rows, outgrad, gates, gu, down)


def attend(queries, keys_all, values_all, allowed):
    factor = HEAD_DIM ** (-0.5)
    scores = jnp.einsum("tkgd,skd->kgts", queries, keys_all, preferred_element_type=f32) * factor
    scores = jnp.where(allowed, scores, -1e30)
    row_max = jnp.max(scores, axis=-1, keepdims=True)
    exponent = jnp.exp(scores - row_max)
    softened = exponent / jnp.sum(exponent, axis=-1, keepdims=True)
    soft_low = softened.astype(bf16)
    attended = jnp.einsum("kgts,skd->tkgd", soft_low, values_all, preferred_element_type=f32)
    return attended.astype(bf16), softened, soft_low


def attend_back(queries, keys_all, values_all, softened, soft_low, attended_grad):
    factor = HEAD_DIM ** (-0.5)
    soft_grad = jnp.einsum("tkgd,skd->kgts", attended_grad, values_all, preferred_element_type=f32)
    values_grad = jnp.einsum("kgts,tkgd->skd", soft_low, attended_grad, preferred_element_type=f32)
    row_delta = jnp.sum(softened * soft_grad, axis=-1, keepdims=True)
    scores_grad = (softened * (soft_grad - row_delta)).astype(bf16)
    queries_grad = (
        jnp.einsum("kgts,skd->tkgd", scores_grad, keys_all, preferred_element_type=f32) * factor
    )
    keys_grad = (
        jnp.einsum("kgts,tkgd->skd", scores_grad, queries, preferred_element_type=f32) * factor
    )
    return queries_grad, keys_grad, values_grad


def shards(
    tokens, cotangent, routes,
    inproj_weight, inproj_first, inproj_second,
    outproj_weight, outproj_first, outproj_second,
    gateup_weight, gateup_first, gateup_second,
    down_weight, down_first, down_second,
    router_weight, router_first, router_second,
    gains, gains_first, gains_second,
):
    n_dp = lax.axis_size("dp")
    n_tensor = lax.axis_size("tensor")
    depth = inproj_weight.shape[0]
    kv_local = inproj_weight.shape[1]
    hidden = down_weight.shape[1]
    group = max(1, 256 // hidden)
    groups = EXPERTS // group
    in_width = inproj_weight.shape[1] * inproj_weight.shape[2]
    out_width = outproj_weight.shape[0] * outproj_weight.shape[1]
    prompt_total = PROMPT_DEV * n_dp
    count = tokens.shape[0]

    def gateup_flat(w):
        w = w.reshape(groups, group, depth, 2, hidden)
        return w.transpose(2, 0, 3, 1, 4).reshape(depth, 2 * EXPERTS * hidden)

    def gateup_back(w):
        w = w.reshape(depth, groups, 2, group, hidden)
        return w.transpose(1, 3, 0, 2, 4).reshape(EXPERTS, depth, 2, hidden)

    gains_high = gains.astype(bf16)
    gains_low = (gains - gains_high.astype(f32)).astype(bf16)
    attn_local = jnp.concatenate(
        [
            inproj_weight.reshape(depth, in_width).astype(bf16),
            outproj_weight.reshape(out_width, depth).T.astype(bf16),
            jnp.concatenate(
                [
                    router_weight.astype(bf16),
                    gains_high.T,
                    gains_low.T,
                    jnp.zeros((depth, 128 - EXPERTS - 4), bf16),
                ],
                axis=1,
            ),
        ],
        axis=1,
    )
    attn_full = lax.all_gather(attn_local, "dp", axis=0, tiled=True)
    gu_full = lax.all_gather(gateup_flat(gateup_weight.astype(bf16)), "dp", axis=0, tiled=True)
    down_full = lax.all_gather(
        down_weight.reshape(EXPERTS * hidden, depth).T.astype(bf16), "dp", axis=0, tiled=True
    )
    inproj_full = attn_full[:, :in_width]
    outproj_full = attn_full[:, in_width : in_width + out_width]
    small_full = attn_full[:, in_width + out_width :]
    router_full = small_full[:, :EXPERTS]
    small_t = small_full[:, EXPERTS : EXPERTS + 4].astype(f32).T
    gain_first = small_t[0:1] + small_t[2:3]
    gain_second = small_t[1:2] + small_t[3:4]

    device_index = lax.axis_index("dp")
    inner = jnp.arange(TOK_MB, dtype=jnp.int32)
    positions = jnp.where(
        inner < PROMPT_DEV, device_index * PROMPT_DEV + inner, prompt_total + inner - PROMPT_DEV
    )
    cosine, sine = angles_for(positions, HEAD_DIM)
    cosine = jnp.tile(cosine, (MICRO, 1))
    sine = jnp.tile(sine, (MICRO, 1))
    key_index = jnp.arange(prompt_total + CONT, dtype=jnp.int32)
    allowed = (key_index[None, :] <= positions[:, None]) & (
        (key_index[None, :] < prompt_total) | (inner[:, None] >= PROMPT_DEV)
    )
    query_width = GROUP * HEAD_DIM
    cos_query, sin_query = cosine[:, None, None, :], sine[:, None, None, :]
    cos_key, sin_key = cosine[:, None, :], sine[:, None, :]

    inputs = tokens.astype(f32)
    inverse_first = lax.rsqrt(jnp.mean(inputs * inputs, axis=-1, keepdims=True) + eps_norm)
    norm_first = inputs * inverse_first
    normed_first = (norm_first * gain_first).astype(bf16)
    mixed = jnp.dot(normed_first, inproj_full, preferred_element_type=f32).reshape(
        count, kv_local, -1
    )
    queries = rotate(
        mixed[..., :query_width].reshape(count, kv_local, GROUP, HEAD_DIM), cos_query, sin_query
    ).astype(bf16)
    keys = rotate(mixed[..., query_width : query_width + HEAD_DIM], cos_key, sin_key)
    both = jnp.concatenate([keys, mixed[..., query_width + HEAD_DIM :]], axis=-1).astype(bf16)
    both = both.reshape(MICRO, TOK_MB, kv_local * 2 * HEAD_DIM)
    prompt_both = lax.all_gather(both[:, :PROMPT_DEV], "dp", axis=1, tiled=True)
    both_all = jnp.concatenate([prompt_both, both[:, PROMPT_DEV:]], axis=1).reshape(
        MICRO, prompt_total + CONT, kv_local, 2 * HEAD_DIM
    )
    kept = []
    attended = []
    for m in range(MICRO):
        q = queries[m * TOK_MB : (m + 1) * TOK_MB]
        k, v = both_all[m, :, :, :HEAD_DIM], both_all[m, :, :, HEAD_DIM:]
        out, softened, soft_low = attend(q, k, v, allowed)
        attended.append(out.reshape(TOK_MB, -1))
        kept.append((q, k, v, softened, soft_low))
    attended = jnp.concatenate(attended, axis=0)
    branch = lax.dot_general(
        attended, outproj_full, (((1,), (1,)), ((), ())), preferred_element_type=f32
    ).astype(bf16)
    branch = line_sum(branch, n_tensor, 1)

    middle = inputs + branch.astype(f32)
    inverse_second = lax.rsqrt(jnp.mean(middle * middle, axis=-1, keepdims=True) + eps_norm)
    norm_second = middle * inverse_second
    normed_second = (norm_second * gain_second).astype(bf16)
    logits = jnp.dot(normed_second, router_full, preferred_element_type=f32)
    named = jnp.any(routes[:, :, None] == jnp.arange(EXPERTS, dtype=jnp.int32), axis=1)
    top = jnp.max(jnp.where(named, logits, -jnp.inf), axis=-1, keepdims=True)
    weights = jnp.where(named, jnp.exp(jnp.where(named, logits, top) - top), 0.0)
    gates = weights / jnp.sum(weights, axis=-1, keepdims=True)
    gates_wide = jnp.pad(gates, ((0, 0), (0, 128 - EXPERTS)))
    active, hidden_grad, gate_grad = expert_call(
        normed_second, cotangent, gates_wide, gu_full, down_full, group
    )
    contract_last = (((1,), (1,)), ((), ()))
    rows_grad = lax.dot_general(
        hidden_grad, gu_full, contract_last, preferred_element_type=f32
    ).astype(bf16)
    summed = line_sum(jnp.concatenate([rows_grad, gate_grad.astype(bf16)], axis=1), n_tensor, 2)
    mixture = lax.dot_general(active, down_full, contract_last, preferred_element_type=f32).astype(
        bf16
    )
    mixture = line_sum(mixture, n_tensor, 1)
    block_out = (middle + mixture.astype(f32)).astype(bf16)
    contract_first = (((0,), (0,)), ((), ()))
    down_grad = lax.dot_general(
        cotangent, active, contract_first, preferred_element_type=f32
    ).astype(bf16)
    gateup_grad = lax.dot_general(
        normed_second, hidden_grad, contract_first, preferred_element_type=f32
    ).astype(bf16)
    down_grad = lax.psum_scatter(down_grad, "dp", scatter_dimension=0, tiled=True)
    gateup_grad = lax.psum_scatter(gateup_grad, "dp", scatter_dimension=0, tiled=True)

    model = tokens.shape[1]
    gate_grad = summed[:, model : model + EXPERTS].astype(f32)
    outgrad = cotangent.astype(f32)
    chosen_grad = gates * (gate_grad - jnp.sum(gates * gate_grad, axis=-1, keepdims=True))
    logits_grad = chosen_grad.astype(bf16)
    router_grad = lax.dot_general(
        normed_second, logits_grad, contract_first, preferred_element_type=f32
    )
    normed_second_grad = summed[:, :model].astype(f32) + lax.dot_general(
        logits_grad, router_full, contract_last, preferred_element_type=f32
    )
    norm_second_grad = normed_second_grad * gain_second
    gain_second_grad = jnp.sum(normed_second_grad * norm_second, axis=0)
    middle_grad = outgrad + inverse_second * (
        norm_second_grad
        - norm_second * jnp.mean(norm_second_grad * norm_second, axis=-1, keepdims=True)
    )

    branch_own = middle_grad.astype(bf16)
    outproj_grad = lax.dot_general(
        branch_own, attended, contract_first, preferred_element_type=f32
    )
    attended_grad = (
        jnp.dot(branch_own, outproj_full, preferred_element_type=f32)
        .astype(bf16)
        .reshape(count, kv_local, GROUP, HEAD_DIM)
    )
    queries_grad, both_grad = [], []
    for m in range(MICRO):
        q, k, v, softened, soft_low = kept[m]
        dq, dk, dv = attend_back(
            q, k, v, softened, soft_low, attended_grad[m * TOK_MB : (m + 1) * TOK_MB]
        )
        queries_grad.append(dq)
        both_grad.append(
            jnp.concatenate([dk, dv], axis=-1).reshape(
                prompt_total + CONT, kv_local * 2 * HEAD_DIM
            )
        )
    queries_grad = jnp.concatenate(queries_grad, axis=0)
    both_grad = jnp.stack(both_grad)
    prompt_grad = lax.psum_scatter(
        both_grad[:, :prompt_total].astype(bf16), "dp", scatter_dimension=1, tiled=True
    ).astype(f32)
    both_grad = jnp.concatenate([prompt_grad, both_grad[:, prompt_total:]], axis=1).reshape(
        count, kv_local, 2 * HEAD_DIM
    )
    keys_grad, values_grad = both_grad[..., :HEAD_DIM], both_grad[..., HEAD_DIM:]
    queries_raw_grad = rotate(queries_grad, cos_query, -sin_query).reshape(count, kv_local, -1)
    keys_raw_grad = rotate(keys_grad, cos_key, -sin_key)
    mixed_grad = (
        jnp.concatenate([queries_raw_grad, keys_raw_grad, values_grad], axis=-1)
        .astype(bf16)
        .reshape(count, -1)
    )
    normed_first_grad = lax.dot_general(
        mixed_grad, inproj_full, contract_last, preferred_element_type=f32
    ).astype(bf16)
    normed_first_grad = line_sum(normed_first_grad, n_tensor, 1).astype(f32)
    inproj_grad = lax.dot_general(
        normed_first, mixed_grad, contract_first, preferred_element_type=f32
    )
    norm_first_grad = normed_first_grad * gain_first
    gain_first_grad = jnp.sum(normed_first_grad * norm_first, axis=0)
    tokens_grad = middle_grad + inverse_first * (
        norm_first_grad
        - norm_first * jnp.mean(norm_first_grad * norm_first, axis=-1, keepdims=True)
    )

    attn_grad = lax.psum_scatter(
        jnp.concatenate([inproj_grad, outproj_grad], axis=1).astype(bf16),
        "dp",
        scatter_dimension=0,
        tiled=True,
    ).astype(f32)
    small_grad = lax.psum_scatter(
        jnp.concatenate(
            [router_grad, gain_first_grad[:, None], gain_second_grad[:, None]], axis=1
        ),
        "dp",
        scatter_dimension=0,
        tiled=True,
    )
    reduced = (
        attn_grad[:, :in_width].reshape(inproj_weight.shape),
        attn_grad[:, in_width:].T.reshape(outproj_weight.shape),
        gateup_back(gateup_grad).astype(f32),
        down_grad.T.reshape(down_weight.shape).astype(f32),
        small_grad[:, :EXPERTS],
        small_grad[:, EXPERTS:].T,
    )
    triples = (
        (inproj_weight, inproj_first, inproj_second, weight_decay, 0.05),
        (outproj_weight, outproj_first, outproj_second, weight_decay, 0.3),
        (gateup_weight, gateup_first, gateup_second, weight_decay, 0.05),
        (down_weight, down_first, down_second, weight_decay, 0.05),
        (router_weight, router_first, router_second, weight_decay, 0.05),
        (gains, gains_first, gains_second, 0.0, 0.4),
    )
    results = [block_out, tokens_grad]
    for (weight, first, second, decay, rate), gradient in zip(triples, reduced):
        results.extend(adam_update(weight, first, second, gradient, decay, rate))
    return tuple(results)


def solution(mesh):
    row = P("dp", None)
    inproj = P("dp", "tensor", None)
    outproj = P("tensor", None, "dp")
    gateup = P(None, "dp", None, "tensor")
    down = P(None, "tensor", "dp")
    gain = P(None, "dp")
    weights = (inproj,) * 3 + (outproj,) * 3 + (gateup,) * 3 + (down,) * 3 + (row,) * 3 + (gain,) * 3
    return jax.shard_map(
        shards,
        mesh=mesh,
        in_specs=(row, row, row) + weights,
        out_specs=(row, row) + weights,
        check_vma=False,
    )
```

time: 2270 us -> 2040 us (0.90)
  Pallas kernels: 0 us -> 1370 us
  local copies, waits for them, and re-layouts: 807 us -> 69 us
  waiting for transfers between devices: 720 us -> 231 us
  matrix products: 446 us -> 235 us
  blocking collectives: 84.7 us -> 0 us
  other arithmetic: 183 us -> 115 us
    pallas_call x0 -> x5, Pallas kernels: none -> 1370 us  [the longest x4 1330 us: line_sum(): pl.pallas_call(functools.partial(line_sum_kernel, n, chunks), out_shape=j...]
    gather x12 -> x0, local copies, waits for them, and re-layouts: 586 us -> none  [the longest x4 209 us: micro_step(): outgrad[token_of_slot]]
    psum x3 -> x0, waiting for transfers between devices: 295 us -> none  [the longest x1 222 us: micro_step(): lax.psum(jnp.sum(picked * gates[..., None], axis=1).astype(jnp.bfloat16),...]
    reduce_scatter x7 -> x1, waiting for transfers between devices: 373 us -> 86.2 us  [shards(): lax.psum_scatter(gateup_grad, 'dp', scatter_dimension=0, tiled=True)]
    dot_general x40 -> x23, matrix products: 419 us -> 206 us  [the longest x2 30.4 us: attend_back(): jnp.einsum('tkgd,skd->kgts', attended_grad, values_all, preferred_element...]
    unnamed x20 -> x13, waiting for transfers between devices: 16.4 us -> 98 us
    scatter x4 -> x0, local copies, waits for them, and re-layouts: 78.7 us -> none  [the longest x2 39.6 us: expert_slots(): filled = jnp.zeros((EXPERTS * CAP,), jnp.float32).at[destination].set(1.0)]
    reduce_sum x17 -> x5, other arithmetic: 77.9 us -> 7.99 us  [the longest x1 2.95 us: shards(): jnp.mean(inputs * inputs, axis=-1, keepdims=True) + eps_norm]
  transfers between devices with their start and end apart: 17 -> 9, of which waited for: 11 -> 6; matrix products, arithmetic and copies ran while one was open for 45% -> 9% of each run, Pallas kernels for 0% -> 16%
where the time goes in v1:
time: 2040 us; the launch traced here: 2030 us
  Pallas kernels  1370 us (67%)
  matrix products  235 us (12%)
  waiting for transfers between devices  231 us (11%)
  other arithmetic  115 us (6%)
  local copies, waits for them, and re-layouts  69 us (3%)
    pallas_call x4, Pallas kernels, line_sum(): pl.pallas_call(functools.partial(line_sum_kernel, n, chunks), out_shape=j...  1330 us
    unnamed x13, waiting for transfers between devices  98 us
    reduce_scatter x1, waiting for transfers between devices, shards(): lax.psum_scatter(gateup_grad, 'dp', scatter_dimension=0, tiled=True)  86.2 us
    pallas_call x1, Pallas kernels, expert_call(): pl.pallas_call(functools.partial(expert_kernel, group), grid=(steps,), in...  41.2 us
  transfers between devices with their start and end apart: 9, of which 6 were waited for; matrix products, arithmetic and copies ran while one was open for 9% of the time, Pallas kernels for 16%

profile of v1, /device:TPU:0, one launch (start us, length us, event | category | flops | bytes accessed | tf_op | source)
XLA Modules:
  0.0 2034.3 jit_solution(17948652365698061453)
XLA Ops:
  13.4 2.9 fusion.26
  16.4 33.2 %all-gather.5.cloned.1.call-done = bf16[1536,1152]{1,0:T(8,128)(2,1)} async-done(((bf16[192,1152]{1,0:T(8,128)(2,1)}), bf16[1536,1152]{1,0:T(8,128)(2,1)}) %all-gather.5.cloned.1.call-update) | async-done | bytes 3538960 | tf_op jit(solution)/shard_map/all_gather | solution.py:324
  52.1 4.9 fusion.59
  78.1 14.0 all-gather.7.cloned.1.call-done
  92.1 2.6 pad_maximum_fusion.3
  94.9 14.2 fusion.119
  109.1 14.4 fusion.120
  123.5 19.6 fusion.65
  143.2 10.1 fusion.68
  153.3 3.7 convolution_convert_fusion.4.x_ref
  157.1 326.3 %shard_map.356 = bf16[1280,1536]{1,0:T(8,128)(2,1)S(1)} custom-call(bf16[1280,1536]{1,0:T(8,128)(2,1)S(1)} %convolution_convert_fusion.4.x_ref), custom_call_target="tpu_custom_call" | custom-call | flops 1966080 | bytes 196608000 | tf_op jit(solution)/shard_map/pallas_call | solution.py:160
  494.7 41.2 %shard_map.357 = (bf16[1280,2048]{1,0:T(8,128)(2,1)}, bf16[1280,4096]{1,0:T(8,128)(2,1)}, f32[1280,128]{1,0:T(8,128)S(1)}) custom-call(bf16[1280,1536]{1,0:T(8,128)(2,1)S(1)} %copy-done.3, bf16[1280,1536]{1,0:T(8,128)(2,1)} %outgrad_ref.1, f32[1280,128]{1,0:T(8,128)S(1)} %pad.4.gates_ref, bf16[1536,4096]{1,0:T(8,128)(2,1)} %all-gather.9.cloned.1.call-done.gu_ref, ...), custom_call_target="tpu_custom_call" | custom-call | flops 24159191040 | bytes 34603008 | tf_op jit(solution)/shard_map/pallas_call | solution.py:221
  536.0 22.2 %convolution_convert_fusion.3 = bf16[1280,1536]{1,0:T(8,128)(2,1)S(1)} fusion(bf16[1280,4096]{1,0:T(8,128)(2,1)} %get-tuple-element.24, bf16[1536,4096]{1,0:T(8,128)(2,1)} %all-gather.9.cloned.1.call-done.gu_ref), kind=kOutput, calls=%fused_computation.51 | convolution fusion | flops 16108093440 | bytes 27000832 | tf_op jit(solution)/shard_map/dot_general | solution.py:398
  558.6 355.6 %shard_map.359 = bf16[1280,1664]{1,0:T(8,128)(2,1)S(1)} custom-call(bf16[1280,1664]{1,0:T(8,128)(2,1)S(1)} %pad_maximum_fusion.x_ref), custom_call_target="tpu_custom_call" | custom-call | flops 2129920 | bytes 212992000 | tf_op jit(solution)/shard_map/pallas_call | solution.py:160
  914.2 8.7 convolution_convert_fusion.5.x_ref
  922.9 320.2 %shard_map.358 = bf16[1280,1536]{1,0:T(8,128)(2,1)S(1)} custom-call(bf16[1280,1536]{1,0:T(8,128)(2,1)S(1)} %convolution_convert_fusion.5.x_ref), custom_call_target="tpu_custom_call" | custom-call | flops 1966080 | bytes 196608000 | tf_op jit(solution)/shard_map/pallas_call | solution.py:160
  1243.5 7.7 multiply_reduce_fusion
  1251.2 8.4 multiply_add_fusion
  1259.6 5.2 convolution_convert_fusion.8
  1264.9 12.3 fusion.44
  1277.2 15.2 fusion.5
  1292.4 15.7 fusion.7
  1308.2 3.7 fusion.53
  1311.8 3.1 fusion.63
  1315.0 12.3 fusion.47
  1327.3 15.2 fusion.2
  1342.5 15.2 fusion.4
  1357.8 3.1 fusion.62
  1360.9 3.7 fusion.51
  1367.1 4.0 copy.238
  1379.3 6.2 convolution_convert_fusion.7
  1385.6 21.9 %reduce-scatter.16.cloned.1.call-done = bf16[128,512]{1,0:T(8,128)(2,1)} async-done(((bf16[1024,512]{1,0:T(8,128)(2,1)}), bf16[128,512]{1,0:T(8,128)(2,1)}) %reduce-scatter.16.cloned.1.call-update) | async-done | bytes 131088
  1425.6 4.1 convolution_convert_fusion.6
  1429.8 3.5 convolution_convert_fusion.2.x_ref
  1433.3 324.9 %shard_map.360 = bf16[1280,1536]{1,0:T(8,128)(2,1)S(1)} custom-call(bf16[1280,1536]{1,0:T(8,128)(2,1)S(1)} %convolution_convert_fusion.2.x_ref), custom_call_target="tpu_custom_call" | custom-call | flops 1966080 | bytes 196608000 | tf_op jit(solution)/shard_map/pallas_call | solution.py:160
  1758.2 2.9 fusion.25
  1764.6 2.9 copy.240
  1767.5 13.5 fusion.28
  1781.0 8.7 copy.242
  1789.8 23.5 %convolution_convert_fusion = bf16[1536,4096]{1,0:T(8,128)(2,1)} fusion(bf16[1280,1536]{1,0:T(8,128)(2,1)} %copy-done.2, bf16[1280,4096]{1,0:T(8,128)(2,1)} %get-tuple-element.24), kind=kOutput, calls=%fused_computation.18 | convolution fusion | flops 16112418816 | bytes 27000832 | tf_op jit(solution)/shard_map/dot_general | solution.py:411
  1813.5 8.9 fusion.22
  1825.8 19.5 reduce-scatter.18.cloned.1.call-done
  1850.2 4.2 multiply_subtract_fusion.2
  1854.4 56.4 %reduce-scatter.20.cloned.1.call-done = bf16[192,2048]{1,0:T(8,128)(2,1)} async-done(((bf16[1536,2048]{1,0:T(8,128)(2,1)}), bf16[192,2048]{1,0:T(8,128)(2,1)}) %reduce-scatter.20.cloned.1.call-update) | async-done | bytes 786448
  1914.3 6.2 multiply_subtract_fusion.1
  1920.6 86.2 %reduce-scatter.14.cloned.1.call-done = bf16[192,4096]{1,0:T(8,128)(2,1)} async-done(((bf16[1536,4096]{1,0:T(8,128)(2,1)}), bf16[192,4096]{1,0:T(8,128)(2,1)}) %reduce-scatter.14.cloned.1.call-update) | async-done | bytes 1572880 | tf_op jit(solution)/shard_map/reduce_scatter | solution.py:415
  2006.8 4.2 reshape.261
  2013.8 13.7 multiply_subtract_fusion
  (228 shorter events, 88.5 us)
Async XLA Ops:
  7.2 42.4 %all-gather.5.cloned.1.call-start = ((), (), s32[]{:S(2)}) async-start(), calls=%async_computation.5 | async-start | bytes 3981312 | tf_op jit(solution)/shard_map/all_gather | solution.py:324
  12.8 79.3 %all-gather.7.cloned.1.call-start = ((), (), s32[]{:S(2)}) async-start(), calls=%async_computation.6 | async-start | bytes 1179648 | tf_op jit(solution)/shard_map/all_gather | solution.py:366
  13.3 64.5 %copy-start.19 = (f32[4,8,2,640]{3,1,2,0:T(8,128)}, f32[4,8,2,640]{3,1,2,0:T(8,128)S(1)}, u32[]{:S(2)}) copy-start(f32[4,8,2,640]{3,1,2,0:T(8,128)S(1)} %copy.251) | copy-start | bytes 491524
  16.4 40.6 %copy-start.34 = (f32[1280]{0:T(1024)}, f32[1280]{0:T(1024)S(1)}, u32[]{:S(2)}) copy-start(f32[1280]{0:T(1024)S(1)} %add_rsqrt_fusion.1) | copy-start | bytes 15364
  52.0 5.0 copy-start.32
  57.0 9.7 copy-start.11
  63.9 428.5 %all-gather.11.cloned.1.call-start = ((), (), s32[]{:S(2)}) async-start(), calls=%async_computation.8 | async-start | bytes 7077888 | tf_op jit(solution)/shard_map/all_gather | solution.py:326
  66.4 426.1 %all-gather.9.cloned.1.call-start = ((), (), s32[]{:S(2)}) async-start(), calls=%async_computation.7 | async-start | bytes 14155776 | tf_op jit(solution)/shard_map/all_gather | solution.py:325
  68.0 5.6 copy-start.37
  72.9 1334.6 %reduce-scatter.16.cloned.1.call-start = ((), (), s32[]{:S(2)}) async-start(), calls=%async_computation.10 | async-start | bytes 1179648
  76.1 16.0 slice-start
  78.1 31.0 %copy-start.15 = (bf16[1280,2,3,32]{0,3,2,1:T(8,128)(2,1)}, bf16[1280,2,3,32]{0,3,2,1:T(8,128)(2,1)S(1)}, u32[]{:S(2)}) copy-start(bf16[1280,2,3,32]{0,3,2,1:T(8,128)(2,1)S(1)} %get-tuple-element.58) | copy-start | bytes 1474564
  78.1 31.0 %copy-start.17 = (bf16[1280,2,3,32]{0,3,2,1:T(8,128)(2,1)}, bf16[1280,2,3,32]{0,3,2,1:T(8,128)(2,1)S(1)}, u32[]{:S(2)}) copy-start(bf16[1280,2,3,32]{0,3,2,1:T(8,128)(2,1)S(1)} %get-tuple-element.59) | copy-start | bytes 1474564
  109.1 34.1 %copy-start.40 = (f32[2,3,640]{2,1,0:T(4,128)}, f32[2,3,640]{2,1,0:T(4,128)S(1)}, u32[]{:S(2)}) copy-start(f32[2,3,640]{2,1,0:T(4,128)S(1)} %get-tuple-element.68) | copy-start | bytes 46084
  143.2 10.2 copy-start.48
  153.3 3.8 copy-start.50
  157.1 326.3 %copy-start.8 = (bf16[1280,1536]{1,0:T(8,128)(2,1)S(1)}, bf16[1280,1536]{1,0:T(8,128)(2,1)}, u32[]{:S(2)}) copy-start(bf16[1280,1536]{1,0:T(8,128)(2,1)} %param.21) | copy-start | bytes 11796484
  492.4 751.1 %copy-start.13 = (f32[1280,16]{1,0:T(8,128)}, f32[1280,16]{1,0:T(8,128)S(1)}, u32[]{:S(2)}) copy-start(f32[1280,16]{1,0:T(8,128)S(1)} %fusion.84) | copy-start | bytes 245764
  558.2 355.9 %slice-start.1 = ((s8[6291456]{0:T(1024)(128)(4,1)}), s8[4194304]{0:T(1024)(128)(4,1)S(1)}, s32[]{:S(2)}) async-start(s8[6291456]{0:T(1024)(128)(4,1)} %bitcast.263), calls=%async_computation.15 | async-start | bytes 8388608
  558.6 355.6 %slice-start.2 = ((s8[6291456]{0:T(1024)(128)(4,1)}), s8[2097152]{0:T(1024)(128)(4,1)S(1)}, s32[]{:S(2)}) async-start(s8[6291456]{0:T(1024)(128)(4,1)} %bitcast.263), calls=%async_computation.16 | async-start | bytes 4194304
  558.6 355.6 %copy-start.52 = (bf16[1280,2048]{1,0:T(8,128)(2,1)S(1)}, bf16[1280,2048]{1,0:T(8,128)(2,1)}, u32[]{:S(2)}) copy-start(bf16[1280,2048]{1,0:T(8,128)(2,1)} %get-tuple-element.23) | copy-start | bytes 15728644
  914.2 329.3 %copy-start.6 = (bf16[1280,1664]{1,0:T(8,128)(2,1)}, bf16[1280,1664]{1,0:T(8,128)(2,1)S(1)}, u32[]{:S(2)}) copy-start(bf16[1280,1664]{1,0:T(8,128)(2,1)S(1)} %shard_map.359) | copy-start | bytes 12779524
  922.9 320.5 %copy-start.1 = (bf16[1280,1536]{1,0:T(8,128)(2,1)S(1)}, bf16[1280,1536]{1,0:T(8,128)(2,1)}, u32[]{:S(2)}) copy-start(bf16[1280,1536]{1,0:T(8,128)(2,1)} %copy-done) | copy-start | bytes 11796484
  922.9 320.5 %copy-start.9 = (bf16[1280,1536]{1,0:T(8,128)(2,1)S(1)}, bf16[1280,1536]{1,0:T(8,128)(2,1)}, u32[]{:S(2)}) copy-start(bf16[1280,1536]{1,0:T(8,128)(2,1)} %param.21) | copy-start | bytes 11796484
  1243.5 7.7 copy-start.38
  1243.5 7.7 copy-start.21
  1292.4 15.7 copy-start.16
  1292.4 15.7 copy-start.18
  1366.0 7.7 copy-start.20
  1366.0 7.7 copy-start.27
  1371.2 5.8 copy-start.39
  1373.6 448.7 %reduce-scatter.22.cloned.1.call-start = ((), (), s32[]{:S(2)}) async-start(), calls=%async_computation.13 | async-start | bytes 884736
  1419.2 5.4 copy-start.22
  1420.6 4.1 copy-start.33
  1420.7 4.1 copy-start.35
  1425.6 4.1 copy-start.31
  1762.4 82.9 %reduce-scatter.18.cloned.1.call-start = ((), (), s32[]{:S(2)}) async-start(), calls=%async_computation.11 | async-start | bytes 3538944
  1767.5 143.4 %reduce-scatter.20.cloned.1.call-start = ((), (), s32[]{:S(2)}) async-start(), calls=%async_computation.12 | async-start | bytes 7077888
  1789.8 217.0 %reduce-scatter.14.cloned.1.call-start = ((), (), s32[]{:S(2)}) async-start(), calls=%async_computation.9 | async-start | bytes 14155776 | tf_op jit(solution)/shard_map/reduce_scatter | solution.py:415
  1813.4 11.2 copy-start.45
  1813.4 11.1 copy-start.46
  1813.4 11.1 copy-start.47
  1813.4 11.7 copy-start.36
  1813.4 11.7 copy-start.42
  1813.4 11.7 copy-start.43
  1822.4 25.6 %copy-start.26 = (f32[2,192,192]{2,1,0:T(8,128)S(1)}, f32[2,192,192]{2,1,0:T(8,128)}, u32[]{:S(2)}) copy-start(f32[2,192,192]{2,1,0:T(8,128)} %param.27) | copy-start | bytes 884740
  1823.4 26.9 %copy-start.25 = (f32[192,2,320]{2,1,0:T(2,128)S(1)}, f32[192,2,320]{2,1,0:T(2,128)}, u32[]{:S(2)}) copy-start(f32[192,2,320]{2,1,0:T(2,128)} %param.24) | copy-start | bytes 1474564
  1823.4 26.9 %copy-start.29 = (f32[192,2,320]{2,1,0:T(2,128)S(1)}, f32[192,2,320]{2,1,0:T(2,128)}, u32[]{:S(2)}) copy-start(f32[192,2,320]{2,1,0:T(2,128)} %param.25) | copy-start | bytes 1474564
  (17 other events, 46.9 us)
Sparse Core Ops, SparseCore 0:
  12.9 36.6 all-gather.4
  64.0 28.0 all-gather.6
  94.6 45.5 all-gather.10
  142.4 72.1 all-gather.8
  1373.8 33.7 reduce-scatter.15
  1762.5 32.4 reduce-scatter.21
  1799.0 46.2 reduce-scatter.17
  1849.0 61.7 reduce-scatter.19
  1914.3 92.3 reduce-scatter.13

commit v2 on v1

--- a/solution.py
+++ b/solution.py
@@ -24,6 +24,7 @@
 weight_decay = 0.1
 bf16 = jnp.bfloat16
 f32 = jnp.float32
+line_chunks = 10
 MESH = pl.DeviceIdType.MESH
 
 
@@ -98,32 +99,35 @@
     def place(half):
         return n - 1 - me if half == 0 else me
 
-    def step(s, carry):
+    def step(t, carry):
         for half in (0, 1):
             at = place(half)
-
-            @pl.when(s < chunks)
+            c = t - at
+
+            @pl.when((c >= 0) & (c < chunks))
             def _():
                 @pl.when(at == 0)
                 def _():
-                    reduce_copy(half, s, x_ref).start()
+                    reduce_copy(half, c, x_ref).start()
 
                 @pl.when(at > 0)
                 def _():
-                    reduce_copy(half, s, held).wait_recv()
-                    total = x_ref[part(half, s)].astype(f32) + held[part(half, s)].astype(f32)
+                    reduce_copy(half, c, held).wait_recv()
+                    total = x_ref[part(half, c)].astype(f32) + held[part(half, c)].astype(f32)
 
                     @pl.when(at < n - 1)
                     def _():
-                        held[part(half, s)] = total.astype(held.dtype)
-                        reduce_copy(half, s, held).start()
+                        held[part(half, c)] = total.astype(held.dtype)
+                        reduce_copy(half, c, held).start()
 
                     @pl.when(at == n - 1)
                     def _():
-                        o_ref[part(half, s)] = total.astype(o_ref.dtype)
-                        out_copy(half, s).start()
-
-            c = s - 2 * (n - 1 - at)
+                        o_ref[part(half, c)] = total.astype(o_ref.dtype)
+                        out_copy(half, c).start()
+
+        for half in (0, 1):
+            at = place(half)
+            c = t - 2 * (n - 1) + at
 
             @pl.when((at < n - 1) & (c >= 0) & (c < chunks))
             def _():
@@ -156,7 +160,7 @@
 
 def line_sum(x, n, barrier_id):
     rows, width = x.shape
-    chunks = 8
+    chunks = line_chunks
     return pl.pallas_call(
         functools.partial(line_sum_kernel, n, chunks),
         out_shape=jax.ShapeDtypeStruct(x.shape, x.dtype),
@@ -247,6 +251,285 @@
     )(rows, outgrad, gates, gu, down)
 
 
+def turn(u, cosine, sine):
+    lane = lax.broadcasted_iota(jnp.int32, u.shape, 1) % HEAD_DIM
+    other = jnp.where(lane < HEAD_DIM // 2, pltpu.roll(u, 96, 1), pltpu.roll(u, 32, 1))
+    return u * cosine + other * sine
+
+
+def project_kernel(x_ref, gain_ref, w_ref, cos_ref, sin_ref, normed_ref, q_ref, kv_ref):
+    x = x_ref[...].astype(f32)
+    inverse = lax.rsqrt(jnp.mean(x * x, axis=-1, keepdims=True) + eps_norm)
+    normed = (x * inverse * gain_ref[0:1]).astype(bf16)
+    normed_ref[...] = normed
+    mixed = jnp.dot(normed, w_ref[...], preferred_element_type=f32)
+    cosine, sine = cos_ref[...], sin_ref[...]
+    turned = q_ref.shape[1] // 128
+    for c in range(turned):
+        q_ref[:, c * 128 : (c + 1) * 128] = turn(
+            mixed[:, c * 128 : (c + 1) * 128], cosine, sine
+        ).astype(bf16)
+    start = turned * 128
+    kv_ref[:, :128] = turn(mixed[:, start : start + 128], cosine, sine).astype(bf16)
+    kv_ref[:, 128:] = mixed[:, start + 128 :].astype(bf16)
+
+
+def project_call(tokens, gain, w, cosine, sine):
+    count, model = tokens.shape
+    tile = 256
+    width = w.shape[1]
+    row = lambda n: pl.BlockSpec((tile, n), lambda i: (i, 0))
+    return pl.pallas_call(
+        project_kernel,
+        grid=(count // tile,),
+        in_specs=[
+            row(model),
+            pl.BlockSpec((8, model), lambda i: (0, 0)),
+            pl.BlockSpec((model, width), lambda i: (0, 0)),
+            row(128),
+            row(128),
+        ],
+        out_specs=[row(model), row(width - 256), row(256)],
+        out_shape=[
+            jax.ShapeDtypeStruct((count, model), bf16),
+            jax.ShapeDtypeStruct((count, width - 256), bf16),
+            jax.ShapeDtypeStruct((count, 256), bf16),
+        ],
+        compiler_params=pltpu.CompilerParams(vmem_limit_bytes=32 * 2**20),
+        cost_estimate=pl.CostEstimate(
+            flops=2 * count * model * width, bytes_accessed=6 * count * model, transcendentals=count
+        ),
+    )(tokens, gain, w, cosine, sine)
+
+
+def head_places(heads):
+    return [(h // GROUP, h % 2, h // 2) for h in range(heads)]
+
+
+def spread(kv, scale):
+    lane = lax.broadcasted_iota(jnp.int32, kv.shape, 1)
+    kv = kv * scale
+    turned = pltpu.roll(kv, HEAD_DIM, 1)
+    first = lane < HEAD_DIM
+    zero = jnp.zeros_like(kv)
+    return {
+        (0, 0): jnp.where(first, kv, zero).astype(bf16),
+        (0, 1): jnp.where(first, zero, turned).astype(bf16),
+        (1, 0): jnp.where(first, turned, zero).astype(bf16),
+        (1, 1): jnp.where(first, zero, kv).astype(bf16),
+    }
+
+
+def row_tiles(prompt_total):
+    tiles = [(0, PROMPT_DEV, prompt_total)]
+    for start in range(0, CONT, 256):
+        tiles.append((PROMPT_DEV + start, 256, prompt_total + start + 256))
+    return tiles
+
+
+nt = (((1,), (1,)), ((), ()))
+
+
+def attention_kernel(heads, dp, q_ref, kv_ref, o_ref, lse_ref, k_ref, v_ref):
+    prompt_total = kv_ref.shape[1] - CONT
+    me = lax.axis_index(dp)
+    keys = spread(kv_ref[0, :, :128].astype(f32), HEAD_DIM**-0.5)
+    values = spread(kv_ref[0, :, 128:].astype(f32), 1.0)
+    for i, place in enumerate(keys):
+        k_ref[i] = keys[place]
+        v_ref[i] = values[place]
+    index = {place: i for i, place in enumerate(keys)}
+    lane = lax.broadcasted_iota(jnp.int32, (1, 128), 1)
+    for start, rows, length in row_tiles(prompt_total):
+        row = lax.broadcasted_iota(jnp.int32, (rows, 1), 0)
+        if start == 0:
+            masked = 0
+            reach = row + me * PROMPT_DEV
+        else:
+            masked = length - 256
+            reach = row
+        column = lax.broadcasted_iota(jnp.int32, (rows, length - masked), 1)
+        lse = jnp.zeros((rows, 128), f32)
+        pair_out = None
+        for h, (kv, half, pair) in enumerate(head_places(heads)):
+            q = q_ref[start : start + rows, pair * 128 : (pair + 1) * 128]
+            i = index[kv, half]
+            tail = lax.dot_general(q, k_ref[i, masked:length], nt, preferred_element_type=f32)
+            tail = jnp.where(column <= reach, tail, -1e30)
+            top = jnp.max(tail, axis=1, keepdims=True)
+            if masked:
+                head = lax.dot_general(q, k_ref[i, :masked], nt, preferred_element_type=f32)
+                top = jnp.maximum(top, jnp.max(head, axis=1, keepdims=True))
+                p_head = jnp.exp(head - top)
+            p_tail = jnp.exp(tail - top)
+            total = jnp.sum(p_tail, axis=1, keepdims=True)
+            out = jnp.dot(
+                p_tail.astype(bf16), v_ref[i, masked:length], preferred_element_type=f32
+            )
+            if masked:
+                total = total + jnp.sum(p_head, axis=1, keepdims=True)
+                out = out + jnp.dot(
+                    p_head.astype(bf16), v_ref[i, :masked], preferred_element_type=f32
+                )
+            out = out / total
+            lse = jnp.where(lane == h, top + jnp.log(total), lse)
+            if half == 0:
+                pair_out = out
+            else:
+                o_ref[start : start + rows, pair * 128 : (pair + 1) * 128] = (
+                    pair_out + out
+                ).astype(bf16)
+        lse_ref[start : start + rows] = lse
+
+
+def attention_call(q, kv, dp):
+    count, width = q.shape
+    keys = kv.shape[1]
+    heads = width // HEAD_DIM
+    return pl.pallas_call(
+        functools.partial(attention_kernel, heads, dp),
+        grid=(MICRO,),
+        in_specs=[
+            pl.BlockSpec((TOK_MB, width), lambda m: (m, 0)),
+            pl.BlockSpec((1, keys, 256), lambda m: (m, 0, 0)),
+        ],
+        out_specs=[
+            pl.BlockSpec((TOK_MB, width), lambda m: (m, 0)),
+            pl.BlockSpec((TOK_MB, 128), lambda m: (m, 0)),
+        ],
+        out_shape=[
+            jax.ShapeDtypeStruct((count, width), bf16),
+            jax.ShapeDtypeStruct((count, 128), f32),
+        ],
+        scratch_shapes=[pltpu.VMEM((4, keys, 128), bf16), pltpu.VMEM((4, keys, 128), bf16)],
+        compiler_params=pltpu.CompilerParams(vmem_limit_bytes=48 * 2**20),
+        cost_estimate=pl.CostEstimate(
+            flops=16 * count * keys * width,
+            bytes_accessed=8 * count * width,
+            transcendentals=count * keys * heads,
+        ),
+    )(q, kv)
+
+
+def attention_back_kernel(
+    heads, dp, q_ref, kv_ref, do_ref, o_ref, lse_ref, cos_ref, sin_ref, row_cos_ref, row_sin_ref,
+    dq_ref, dkv_ref, k_ref, v_ref, kt_ref, dk_ref, dv_ref,
+):
+    prompt_total = kv_ref.shape[1] - CONT
+    me = lax.axis_index(dp)
+    keys = spread(kv_ref[0, :, :128].astype(f32), HEAD_DIM**-0.5)
+    values = spread(kv_ref[0, :, 128:].astype(f32), 1.0)
+    for i, place in enumerate(keys):
+        k_ref[i] = keys[place]
+        v_ref[i] = values[place]
+        kt_ref[i] = keys[place].astype(f32).T.astype(bf16)
+    index = {place: i for i, place in enumerate(keys)}
+    dk_ref[...] = jnp.zeros_like(dk_ref)
+    dv_ref[...] = jnp.zeros_like(dv_ref)
+    half_rows = (
+        lax.broadcasted_iota(jnp.int32, (8, 128), 1) // HEAD_DIM
+        == lax.broadcasted_iota(jnp.int32, (8, 128), 0)
+    ).astype(f32)
+    for start, rows, length in row_tiles(prompt_total):
+        at = slice(start, start + rows)
+        column = lax.broadcasted_iota(jnp.int32, (1, rows), 1)
+        if start == 0:
+            masked = 0
+            reach = column + me * PROMPT_DEV
+        else:
+            masked = length - 256
+            reach = column
+        key = lax.broadcasted_iota(jnp.int32, (length - masked, rows), 0)
+        back = None
+        for h, (kv, half, pair) in enumerate(head_places(heads)):
+            lanes = slice(pair * 128, (pair + 1) * 128)
+            i = index[kv, half]
+            q, do = q_ref[at, lanes], do_ref[at, lanes]
+            if half == 0:
+                delta_pair = lax.dot_general(
+                    half_rows,
+                    do.astype(f32) * o_ref[at, lanes].astype(f32),
+                    nt,
+                    precision=lax.Precision.HIGHEST,
+                    preferred_element_type=f32,
+                )
+            delta = delta_pair[half : half + 1]
+            lse = lse_ref[0, h : h + 1, at]
+            for low, high in ((0, masked), (masked, length)):
+                if low == high:
+                    continue
+                s = lax.dot_general(k_ref[i, low:high], q, nt, preferred_element_type=f32)
+                if low == masked:
+                    s = jnp.where(key <= reach, s, -1e30)
+                p = jnp.exp(s - lse)
+                dp_ = lax.dot_general(v_ref[i, low:high], do, nt, preferred_element_type=f32)
+                ds = (p * (dp_ - delta)).astype(bf16)
+                dv_ref[i, low:high] += jnp.dot(
+                    p.astype(bf16), do, preferred_element_type=f32
+                )
+                dk_ref[i, low:high] += jnp.dot(ds, q, preferred_element_type=f32)
+                term = jnp.dot(kt_ref[i, :, low:high], ds, preferred_element_type=f32)
+                back = term if back is None else back + term
+            if half == 1:
+                dq_ref[at, lanes] = turn(
+                    back.T, row_cos_ref[at], -row_sin_ref[at]
+                ).astype(bf16)
+                back = None
+    lane = lax.broadcasted_iota(jnp.int32, (kv_ref.shape[1], 128), 1)
+
+    def joined(acc):
+        get = lambda place: acc[index[place]]
+        return jnp.where(
+            lane < HEAD_DIM,
+            get((0, 0)) + pltpu.roll(get((0, 1)), HEAD_DIM, 1),
+            get((1, 1)) + pltpu.roll(get((1, 0)), HEAD_DIM, 1),
+        )
+
+    dk = joined(dk_ref) * HEAD_DIM**-0.5
+    dkv_ref[0, :, :128] = turn(dk, cos_ref[...], -sin_ref[...]).astype(bf16)
+    dkv_ref[0, :, 128:] = joined(dv_ref).astype(bf16)
+
+
+def attention_back_call(q, kv, do, o, lse, cosine, sine, row_cos, row_sin, dp):
+    count, width = q.shape
+    keys = kv.shape[1]
+    heads = width // HEAD_DIM
+    rows = pl.BlockSpec((TOK_MB, width), lambda m: (m, 0))
+    return pl.pallas_call(
+        functools.partial(attention_back_kernel, heads, dp),
+        grid=(MICRO,),
+        in_specs=[
+            rows,
+            pl.BlockSpec((1, keys, 256), lambda m: (m, 0, 0)),
+            rows,
+            rows,
+            pl.BlockSpec((1, 8, TOK_MB), lambda m: (m, 0, 0)),
+            pl.BlockSpec((keys, 128), lambda m: (0, 0)),
+            pl.BlockSpec((keys, 128), lambda m: (0, 0)),
+            pl.BlockSpec((TOK_MB, 128), lambda m: (0, 0)),
+            pl.BlockSpec((TOK_MB, 128), lambda m: (0, 0)),
+        ],
+        out_specs=[rows, pl.BlockSpec((1, keys, 256), lambda m: (m, 0, 0))],
+        out_shape=[
+            jax.ShapeDtypeStruct((count, width), bf16),
+            jax.ShapeDtypeStruct((MICRO, keys, 256), bf16),
+        ],
+        scratch_shapes=[
+            pltpu.VMEM((4, keys, 128), bf16),
+            pltpu.VMEM((4, keys, 128), bf16),
+            pltpu.VMEM((4, 128, keys), bf16),
+            pltpu.VMEM((4, keys, 128), f32),
+            pltpu.VMEM((4, keys, 128), f32),
+        ],
+        compiler_params=pltpu.CompilerParams(vmem_limit_bytes=56 * 2**20),
+        cost_estimate=pl.CostEstimate(
+            flops=40 * count * keys * width,
+            bytes_accessed=12 * count * width,
+            transcendentals=count * keys * heads,
+        ),
+    )(q, kv, do, o, lse, cosine, sine, row_cos, row_sin)
+
+
 def attend(queries, keys_all, values_all, allowed):
     factor = HEAD_DIM ** (-0.5)
     scores = jnp.einsum("tkgd,skd->kgts", queries, keys_all, preferred_element_type=f32) * factor
@@ -303,11 +586,22 @@
         w = w.reshape(depth, groups, 2, group, hidden)
         return w.transpose(1, 3, 0, 2, 4).reshape(EXPERTS, depth, 2, hidden)
 
+    query_width = GROUP * HEAD_DIM
+
+    def inproj_flat(w):
+        w = w.reshape(depth, kv_local, query_width + 2 * HEAD_DIM)
+        parts = (w[:, :, :query_width], w[:, :, query_width:-HEAD_DIM], w[:, :, -HEAD_DIM:])
+        return jnp.concatenate([p.reshape(depth, -1) for p in parts], axis=1)
+
+    def inproj_back(w):
+        q, k, v = jnp.split(w, [kv_local * query_width, kv_local * (query_width + HEAD_DIM)], axis=1)
+        return jnp.concatenate([p.reshape(depth, kv_local, -1) for p in (q, k, v)], axis=2)
+
     gains_high = gains.astype(bf16)
     gains_low = (gains - gains_high.astype(f32)).astype(bf16)
     attn_local = jnp.concatenate(
         [
-            inproj_weight.reshape(depth, in_width).astype(bf16),
+            inproj_flat(inproj_weight.astype(bf16)),
             outproj_weight.reshape(out_width, depth).T.astype(bf16),
             jnp.concatenate(
                 [
@@ -335,47 +629,71 @@
     gain_second = small_t[1:2] + small_t[3:4]
 
     device_index = lax.axis_index("dp")
-    inner = jnp.arange(TOK_MB, dtype=jnp.int32)
-    positions = jnp.where(
-        inner < PROMPT_DEV, device_index * PROMPT_DEV + inner, prompt_total + inner - PROMPT_DEV
-    )
-    cosine, sine = angles_for(positions, HEAD_DIM)
-    cosine = jnp.tile(cosine, (MICRO, 1))
-    sine = jnp.tile(sine, (MICRO, 1))
-    key_index = jnp.arange(prompt_total + CONT, dtype=jnp.int32)
-    allowed = (key_index[None, :] <= positions[:, None]) & (
-        (key_index[None, :] < prompt_total) | (inner[:, None] >= PROMPT_DEV)
-    )
-    query_width = GROUP * HEAD_DIM
-    cos_query, sin_query = cosine[:, None, None, :], sine[:, None, None, :]
-    cos_key, sin_key = cosine[:, None, :], sine[:, None, :]
-
     inputs = tokens.astype(f32)
     inverse_first = lax.rsqrt(jnp.mean(inputs * inputs, axis=-1, keepdims=True) + eps_norm)
     norm_first = inputs * inverse_first
-    normed_first = (norm_first * gain_first).astype(bf16)
-    mixed = jnp.dot(normed_first, inproj_full, preferred_element_type=f32).reshape(
-        count, kv_local, -1
-    )
-    queries = rotate(
-        mixed[..., :query_width].reshape(count, kv_local, GROUP, HEAD_DIM), cos_query, sin_query
-    ).astype(bf16)
-    keys = rotate(mixed[..., query_width : query_width + HEAD_DIM], cos_key, sin_key)
-    both = jnp.concatenate([keys, mixed[..., query_width + HEAD_DIM :]], axis=-1).astype(bf16)
-    both = both.reshape(MICRO, TOK_MB, kv_local * 2 * HEAD_DIM)
+    cosine, sine = angles_for(jnp.arange(prompt_total + CONT), HEAD_DIM)
+
+    def of_rows(table):
+        own = lax.dynamic_slice_in_dim(table, device_index * PROMPT_DEV, PROMPT_DEV, 0)
+        return jnp.concatenate([own, table[prompt_total:]], axis=0)
+
+    in_kernels = kv_local * HEAD_DIM == 128
+    queries_width = kv_local * query_width
+    both_width = kv_local * 2 * HEAD_DIM
+    if in_kernels:
+        cos_all = jnp.concatenate([cosine] * 4, axis=1)
+        sin_all = jnp.concatenate([-sine, sine] * 2, axis=1)
+        cos_row, sin_row = of_rows(cos_all), of_rows(sin_all)
+        normed_first, queries, both = project_call(
+            tokens,
+            jnp.pad(gain_first, ((0, 7), (0, 0))),
+            inproj_full,
+            jnp.concatenate([cos_row] * MICRO, axis=0),
+            jnp.concatenate([sin_row] * MICRO, axis=0),
+        )
+    else:
+        cosine, sine = (jnp.tile(of_rows(t), (MICRO, 1))[:, None, :] for t in (cosine, sine))
+        normed_first = (norm_first * gain_first).astype(bf16)
+        mixed = jnp.dot(normed_first, inproj_full, preferred_element_type=f32)
+        queries = rotate(
+            mixed[:, :queries_width].reshape(count, -1, HEAD_DIM), cosine, sine
+        ).astype(bf16)
+        keys = rotate(
+            mixed[:, queries_width : queries_width + kv_local * HEAD_DIM].reshape(
+                count, -1, HEAD_DIM
+            ),
+            cosine,
+            sine,
+        )
+        both = jnp.concatenate(
+            [keys.reshape(count, -1), mixed[:, queries_width + kv_local * HEAD_DIM :]], axis=1
+        ).astype(bf16)
+    both = both.reshape(MICRO, TOK_MB, both_width)
     prompt_both = lax.all_gather(both[:, :PROMPT_DEV], "dp", axis=1, tiled=True)
-    both_all = jnp.concatenate([prompt_both, both[:, PROMPT_DEV:]], axis=1).reshape(
-        MICRO, prompt_total + CONT, kv_local, 2 * HEAD_DIM
-    )
-    kept = []
-    attended = []
-    for m in range(MICRO):
-        q = queries[m * TOK_MB : (m + 1) * TOK_MB]
-        k, v = both_all[m, :, :, :HEAD_DIM], both_all[m, :, :, HEAD_DIM:]
-        out, softened, soft_low = attend(q, k, v, allowed)
-        attended.append(out.reshape(TOK_MB, -1))
-        kept.append((q, k, v, softened, soft_low))
-    attended = jnp.concatenate(attended, axis=0)
+    both_all = jnp.concatenate([prompt_both, both[:, PROMPT_DEV:]], axis=1)
+    if in_kernels:
+        attended, lse = attention_call(queries, both_all, "dp")
+    else:
+        inner = jnp.arange(TOK_MB, dtype=jnp.int32)
+        positions = jnp.where(
+            inner < PROMPT_DEV, device_index * PROMPT_DEV + inner, prompt_total + inner - PROMPT_DEV
+        )
+        key_index = jnp.arange(prompt_total + CONT, dtype=jnp.int32)
+        allowed = (key_index[None, :] <= positions[:, None]) & (
+            (key_index[None, :] < prompt_total) | (inner[:, None] >= PROMPT_DEV)
+        )
+        kept = []
+        attended = []
+        for m in range(MICRO):
+            q = queries[m * TOK_MB : (m + 1) * TOK_MB].reshape(TOK_MB, kv_local, GROUP, HEAD_DIM)
+            k, v = (
+                t.reshape(-1, kv_local, HEAD_DIM) for t in jnp.split(both_all[m], 2, axis=1)
+            )
+            out, softened, soft_low = attend(q, k, v, allowed)
+            attended.append(out.reshape(TOK_MB, -1))
+            kept.append((q, k, v, softened, soft_low))
+        attended = jnp.concatenate(attended, axis=0)
     branch = lax.dot_general(
         attended, outproj_full, (((1,), (1,)), ((), ())), preferred_element_type=f32
     ).astype(bf16)
@@ -395,15 +713,6 @@
         normed_second, cotangent, gates_wide, gu_full, down_full, group
     )
     contract_last = (((1,), (1,)), ((), ()))
-    rows_grad = lax.dot_general(
-        hidden_grad, gu_full, contract_last, preferred_element_type=f32
-    ).astype(bf16)
-    summed = line_sum(jnp.concatenate([rows_grad, gate_grad.astype(bf16)], axis=1), n_tensor, 2)
-    mixture = lax.dot_general(active, down_full, contract_last, preferred_element_type=f32).astype(
-        bf16
-    )
-    mixture = line_sum(mixture, n_tensor, 1)
-    block_out = (middle + mixture.astype(f32)).astype(bf16)
     contract_first = (((0,), (0,)), ((), ()))
     down_grad = lax.dot_general(
         cotangent, active, contract_first, preferred_element_type=f32
@@ -411,8 +720,18 @@
     gateup_grad = lax.dot_general(
         normed_second, hidden_grad, contract_first, preferred_element_type=f32
     ).astype(bf16)
+    hidden_grad, down_grad, gateup_grad = lax.optimization_barrier(
+        (hidden_grad, down_grad, gateup_grad)
+    )
     down_grad = lax.psum_scatter(down_grad, "dp", scatter_dimension=0, tiled=True)
     gateup_grad = lax.psum_scatter(gateup_grad, "dp", scatter_dimension=0, tiled=True)
+    rows_grad = lax.dot_general(
+        hidden_grad, gu_full, contract_last, preferred_element_type=f32
+    ).astype(bf16)
+    mixture = lax.dot_general(active, down_full, contract_last, preferred_element_type=f32).astype(
+        bf16
+    )
+    summed = line_sum(jnp.concatenate([rows_grad, gate_grad.astype(bf16)], axis=1), n_tensor, 2)
 
     model = tokens.shape[1]
     gate_grad = summed[:, model : model + EXPERTS].astype(f32)
@@ -436,46 +755,73 @@
     outproj_grad = lax.dot_general(
         branch_own, attended, contract_first, preferred_element_type=f32
     )
-    attended_grad = (
-        jnp.dot(branch_own, outproj_full, preferred_element_type=f32)
-        .astype(bf16)
-        .reshape(count, kv_local, GROUP, HEAD_DIM)
-    )
-    queries_grad, both_grad = [], []
-    for m in range(MICRO):
-        q, k, v, softened, soft_low = kept[m]
-        dq, dk, dv = attend_back(
-            q, k, v, softened, soft_low, attended_grad[m * TOK_MB : (m + 1) * TOK_MB]
+    attended_grad = jnp.dot(branch_own, outproj_full, preferred_element_type=f32).astype(bf16)
+    attended_grad, down_grad, gateup_grad, mixture = lax.optimization_barrier(
+        (attended_grad, down_grad, gateup_grad, mixture)
+    )
+    if in_kernels:
+        lse_rows = lse[:, :8].reshape(MICRO, TOK_MB, 8).transpose(0, 2, 1)
+        queries_grad, both_grad = attention_back_call(
+            queries, both_all, attended_grad, attended, lse_rows,
+            cos_all, sin_all, cos_row, sin_row, "dp",
         )
-        queries_grad.append(dq)
-        both_grad.append(
-            jnp.concatenate([dk, dv], axis=-1).reshape(
-                prompt_total + CONT, kv_local * 2 * HEAD_DIM
-            )
-        )
-    queries_grad = jnp.concatenate(queries_grad, axis=0)
-    both_grad = jnp.stack(both_grad)
+    else:
+        queries_grad, both_grad = [], []
+        for m in range(MICRO):
+            q, k, v, softened, soft_low = kept[m]
+            dout = attended_grad[m * TOK_MB : (m + 1) * TOK_MB].reshape(q.shape)
+            dq, dk, dv = attend_back(q, k, v, softened, soft_low, dout)
+            queries_grad.append(dq.reshape(TOK_MB, -1, HEAD_DIM))
+            both_grad.append(jnp.concatenate([t.reshape(-1, both_width // 2) for t in (dk, dv)], 1))
+        queries_grad = rotate(jnp.concatenate(queries_grad, axis=0), cosine, -sine)
+        queries_grad = queries_grad.reshape(count, -1).astype(bf16)
+        both_grad = jnp.stack(both_grad)
+    both_grad, mixture = lax.optimization_barrier((both_grad, mixture))
+    mixture = lax.psum(mixture, "tensor")
+    block_out = (middle + mixture.astype(f32)).astype(bf16)
     prompt_grad = lax.psum_scatter(
         both_grad[:, :prompt_total].astype(bf16), "dp", scatter_dimension=1, tiled=True
-    ).astype(f32)
-    both_grad = jnp.concatenate([prompt_grad, both_grad[:, prompt_total:]], axis=1).reshape(
-        count, kv_local, 2 * HEAD_DIM
-    )
-    keys_grad, values_grad = both_grad[..., :HEAD_DIM], both_grad[..., HEAD_DIM:]
-    queries_raw_grad = rotate(queries_grad, cos_query, -sin_query).reshape(count, kv_local, -1)
-    keys_raw_grad = rotate(keys_grad, cos_key, -sin_key)
-    mixed_grad = (
-        jnp.concatenate([queries_raw_grad, keys_raw_grad, values_grad], axis=-1)
-        .astype(bf16)
-        .reshape(count, -1)
-    )
+    )
+    both_grad = jnp.concatenate(
+        [prompt_grad.astype(both_grad.dtype), both_grad[:, prompt_total:]], axis=1
+    ).reshape(count, both_width)
+    if not in_kernels:
+        keys_grad = rotate(
+            both_grad[:, : both_width // 2].reshape(count, -1, HEAD_DIM), cosine, -sine
+        )
+        both_grad = jnp.concatenate(
+            [keys_grad.reshape(count, -1), both_grad[:, both_width // 2 :]], axis=1
+        ).astype(bf16)
+    mixed_grad = jnp.concatenate([queries_grad, both_grad], axis=1)
     normed_first_grad = lax.dot_general(
         mixed_grad, inproj_full, contract_last, preferred_element_type=f32
     ).astype(bf16)
-    normed_first_grad = line_sum(normed_first_grad, n_tensor, 1).astype(f32)
     inproj_grad = lax.dot_general(
         normed_first, mixed_grad, contract_first, preferred_element_type=f32
     )
+    attn_grad = jnp.concatenate(
+        [
+            inproj_grad,
+            outproj_grad,
+            router_grad,
+            gain_second_grad[:, None],
+            jnp.zeros((model, 127 - EXPERTS), f32),
+        ],
+        axis=1,
+    ).astype(bf16)
+    down_next = adam_update(
+        down_weight, down_first, down_second,
+        down_grad.T.reshape(down_weight.shape).astype(f32), weight_decay, 0.05,
+    )
+    gateup_next = adam_update(
+        gateup_weight, gateup_first, gateup_second,
+        gateup_back(gateup_grad).astype(f32), weight_decay, 0.05,
+    )
+    normed_first_grad, attn_grad, down_next, gateup_next = lax.optimization_barrier(
+        (normed_first_grad, attn_grad, down_next, gateup_next)
+    )
+    attn_grad = lax.psum_scatter(attn_grad, "dp", scatter_dimension=0, tiled=True).astype(f32)
+    normed_first_grad = line_sum(normed_first_grad, n_tensor, 1).astype(f32)
     norm_first_grad = normed_first_grad * gain_first
     gain_first_grad = jnp.sum(normed_first_grad * norm_first, axis=0)
     tokens_grad = middle_grad + inverse_first * (
@@ -483,40 +829,34 @@
         - norm_first * jnp.mean(norm_first_grad * norm_first, axis=-1, keepdims=True)
     )
 
-    attn_grad = lax.psum_scatter(
-        jnp.concatenate([inproj_grad, outproj_grad], axis=1).astype(bf16),
-        "dp",
-        scatter_dimension=0,
-        tiled=True,
-    ).astype(f32)
-    small_grad = lax.psum_scatter(
-        jnp.concatenate(
-            [router_grad, gain_first_grad[:, None], gain_second_grad[:, None]], axis=1
+    gain_first_parts = lax.all_gather(gain_first_grad, "dp")
+    gain_first_grad = lax.dynamic_slice_in_dim(
+        jnp.sum(gain_first_parts, axis=0), device_index * depth, depth, 0
+    )
+    split = (in_width, in_width + out_width, in_width + out_width + EXPERTS)
+    inproj_grad, outproj_grad, router_grad, gain_second_grad = (
+        attn_grad[:, : split[0]],
+        attn_grad[:, split[0] : split[1]],
+        attn_grad[:, split[1] : split[2]],
+        attn_grad[:, split[2]],
+    )
+    updates = (
+        adam_update(
+            inproj_weight, inproj_first, inproj_second, inproj_back(inproj_grad), weight_decay, 0.05
         ),
-        "dp",
-        scatter_dimension=0,
-        tiled=True,
-    )
-    reduced = (
-        attn_grad[:, :in_width].reshape(inproj_weight.shape),
-        attn_grad[:, in_width:].T.reshape(outproj_weight.shape),
-        gateup_back(gateup_grad).astype(f32),
-        down_grad.T.reshape(down_weight.shape).astype(f32),
-        small_grad[:, :EXPERTS],
-        small_grad[:, EXPERTS:].T,
-    )
-    triples = (
-        (inproj_weight, inproj_first, inproj_second, weight_decay, 0.05),
-        (outproj_weight, outproj_first, outproj_second, weight_decay, 0.3),
-        (gateup_weight, gateup_first, gateup_second, weight_decay, 0.05),
-        (down_weight, down_first, down_second, weight_decay, 0.05),
-        (router_weight, router_first, router_second, weight_decay, 0.05),
-        (gains, gains_first, gains_second, 0.0, 0.4),
-    )
-    results = [block_out, tokens_grad]
-    for (weight, first, second, decay, rate), gradient in zip(triples, reduced):
-        results.extend(adam_update(weight, first, second, gradient, decay, rate))
-    return tuple(results)
+        adam_update(
+            outproj_weight, outproj_first, outproj_second,
+            outproj_grad.T.reshape(outproj_weight.shape), weight_decay, 0.3,
+        ),
+        gateup_next,
+        down_next,
+        adam_update(router_weight, router_first, router_second, router_grad, weight_decay, 0.05),
+        adam_update(
+            gains, gains_first, gains_second,
+            jnp.stack([gain_first_grad, gain_second_grad]), 0.0, 0.4,
+        ),
+    )
+    return (block_out, tokens_grad) + sum(updates, ())
 
 
 def solution(mesh):

time: 2040 us -> 855 us (0.42)
  Pallas kernels: 1370 us -> 515 us
  waiting for transfers between devices: 231 us -> 42 us
  matrix products: 235 us -> 113 us
  other arithmetic: 115 us -> 74.6 us
    pallas_call x4 -> x3, Pallas kernels: 1330 us -> 414 us  [line_sum(): pl.pallas_call(functools.partial(line_sum_kernel, n, chunks), out_shape=j...]
    dot_general x11 -> x0, matrix products: 103 us -> none  [the longest x2 30.4 us: attend_back(): jnp.einsum('tkgd,skd->kgts', attended_grad, values_all, preferred_element...]
    unnamed x13 -> x11, waiting for transfers between devices: 98 us -> 1.74 us
    reduce_scatter x1, waiting for transfers between devices: 86.2 us -> 0.01 us  [shards(): lax.psum_scatter(gateup_grad, 'dp', scatter_dimension=0, tiled=True)]
    pallas_call x0 -> x3, Pallas kernels: none -> 59.2 us  [the longest x1 33.5 us: attention_back_call(): pl.pallas_call(functools.partial(attention_back_kernel, heads, dp), grid=...]
    convert_element_type x4 -> x2, other arithmetic: 33.1 us -> 1.35 us  [the longest x1 1.27 us: shards(): inproj_weight.astype(bf16)]
    sub x2 -> x0, matrix products: 28.6 us -> none  [attend(): exponent = jnp.exp(scores - row_max)]
  transfers between devices with their start and end apart: 9 -> 9, of which waited for: 6 -> 3; matrix products, arithmetic and copies ran while one was open for 9% -> 21% of each run, Pallas kernels for 16% -> 51%
where the time goes in v2:
time: 855 us; the launch traced here: 847 us
  Pallas kernels  515 us (60%)
  matrix products  113 us (13%)
  local copies, waits for them, and re-layouts  76.7 us (9%)
  other arithmetic  74.6 us (9%)
  waiting for transfers between devices  42 us (5%)
  between operations  14.8 us (2%)
  blocking collectives  10 us (1%)
    pallas_call x3, Pallas kernels, line_sum(): pl.pallas_call(functools.partial(line_sum_kernel, n, chunks), out_shape=j...  414 us
    pallas_call x1, Pallas kernels, expert_call(): pl.pallas_call(functools.partial(expert_kernel, group), grid=(steps,), in...  41.5 us
    pallas_call x1, Pallas kernels, attention_back_call(): pl.pallas_call(functools.partial(attention_back_kernel, heads, dp), grid=...  33.5 us
    all_gather x1, waiting for transfers between devices, shards(): attn_full = lax.all_gather(attn_local, 'dp', axis=0, tiled=True)  30.7 us
    unnamed x75, local copies, waits for them, and re-layouts  28.7 us
    sub x6, other arithmetic, adam_update(): weight - learn_rate * (update + decay_rate * weight)  28.2 us
    dot_general x1, matrix products, shards(): lax.dot_general(hidden_grad, gu_full, contract_last, preferred_element_ty...  23.8 us
    dot_general x1, matrix products, shards(): lax.dot_general(normed_second, hidden_grad, contract_first, preferred_ele...  23.2 us
  transfers between devices with their start and end apart: 9, of which 3 were waited for; matrix products, arithmetic and copies ran while one was open for 21% of the time, Pallas kernels for 51%

profile of v2, /device:TPU:0, one launch (start us, length us, event | category | flops | bytes accessed | tf_op | source)
XLA Modules:
  0.0 847.4 jit_solution(4800630238325183503)
XLA Ops:
  13.6 2.8 fusion.30
  19.6 30.7 %all-gather.7.cloned.1.call-done = bf16[1536,1152]{1,0:T(8,128)(2,1)} async-done(((bf16[192,1152]{1,0:T(8,128)(2,1)}), bf16[1536,1152]{1,0:T(8,128)(2,1)}) %all-gather.7.cloned.1.call-update) | async-done | bytes 3538960 | tf_op jit(solution)/shard_map/all_gather | solution.py:618
  53.3 1.9 slice.105.w_ref
  56.0 5.2 shard_map.356
  61.2 1.9 copy-done.14
  63.8 2.4 bitcast_bitcast_fusion
  66.8 3.2 convert_element_type.161
  70.0 3.6 copy.156
  73.5 3.8 reshape.131
  77.9 9.5 %all-gather.9.cloned.1.call-done = bf16[2,1024,256]{2,1,0:T(8,128)(2,1)} async-done(((bf16[2,128,256]{2,1,0:T(8,128)(2,1)}), bf16[2,1024,256]{2,1,0:T(8,128)(2,1)}) %all-gather.9.cloned.1.call-update) | async-done | bytes 1048592 | tf_op jit(solution)/shard_map/all_gather | solution.py:673
  88.8 20.5 %shard_map.357 = (bf16[1280,384]{1,0:T(8,128)(2,1)S(1)}, f32[1280,128]{1,0:T(8,128)S(1)}) custom-call(bf16[1280,384]{1,0:T(8,128)(2,1)S(1)} %get-tuple-element.47.q_ref, bf16[2,1536,256]{2,1,0:T(8,128)(2,1)S(1)} %pad_maximum_fusion.2.kv_ref), custom_call_target="tpu_custom_call" | custom-call | flops 12079595520 | bytes 3932160 | tf_op jit(solution)/shard_map/pallas_call | solution.py:389
  109.3 3.9 convolution_convert_fusion.4.x_ref
  113.2 108.3 %shard_map.358 = bf16[1280,1536]{1,0:T(8,128)(2,1)S(1)} custom-call(bf16[1280,1536]{1,0:T(8,128)(2,1)S(1)} %convolution_convert_fusion.4.x_ref), custom_call_target="tpu_custom_call" | custom-call | flops 1966080 | bytes 196608000 | tf_op jit(solution)/shard_map/pallas_call | solution.py:164
  223.4 1.8 multiply_convert_fusion.rows_ref
  225.3 2.1 select_reduce_fusion
  227.4 1.9 copy-done.6
  230.6 2.1 copy-done.7
  232.7 41.5 %shard_map.359 = (bf16[1280,2048]{1,0:T(8,128)(2,1)}, bf16[1280,4096]{1,0:T(8,128)(2,1)}, f32[1280,128]{1,0:T(8,128)S(1)}) custom-call(bf16[1280,1536]{1,0:T(8,128)(2,1)S(1)} %copy-done.7, bf16[1280,1536]{1,0:T(8,128)(2,1)} %outgrad_ref.1, f32[1280,128]{1,0:T(8,128)S(1)} %pad.9.gates_ref, bf16[1536,4096]{1,0:T(8,128)(2,1)} %all-gather.11.cloned.1.call-done.gu_ref, ...), custom_call_target="tpu_custom_call" | custom-call | flops 24159191040 | bytes 34603008 | tf_op jit(solution)/shard_map/pallas_call | solution.py:225
  274.2 12.6 %fusion.10 = bf16[1536,2048]{0,1:T(8,128)(2,1)} fusion(bf16[1280,2048]{1,0:T(8,128)(2,1)} %get-tuple-element.51, bf16[1280,1536]{1,0:T(8,128)(2,1)S(1)} %copy-done.21), kind=kOutput, calls=%fused_computation.27 | convolution fusion | flops 8056209408 | bytes 15466496 | tf_op jit(solution)/shard_map/dot_general | solution.py:717
  286.8 23.2 %convolution_convert_fusion = bf16[1536,4096]{1,0:T(8,128)(2,1)} fusion(bf16[1280,1536]{1,0:T(8,128)(2,1)S(1)} %copy-done.7, bf16[1280,4096]{1,0:T(8,128)(2,1)} %get-tuple-element.52), kind=kOutput, calls=%fused_computation | convolution fusion | flops 16112418816 | bytes 27000832 | tf_op jit(solution)/shard_map/dot_general | solution.py:720
  310.1 8.7 %copy.148 = bf16[1536,2048]{1,0:T(8,128)(2,1)} copy(bf16[1536,2048]{0,1:T(8,128)(2,1)} %fusion.10) | data formatting | bytes 12582912
  322.0 23.8 %convolution_convert_fusion.2 = bf16[1280,1536]{1,0:T(8,128)(2,1)S(1)} fusion(bf16[1280,4096]{1,0:T(8,128)(2,1)} %get-tuple-element.52, bf16[1536,4096]{1,0:T(8,128)(2,1)} %all-gather.11.cloned.1.call-done.gu_ref), kind=kOutput, calls=%fused_computation.22 | convolution fusion | flops 16108093440 | bytes 27000832 | tf_op jit(solution)/shard_map/dot_general | solution.py:728
  346.1 112.2 %shard_map.360 = bf16[1280,1664]{1,0:T(8,128)(2,1)S(1)} custom-call(bf16[1280,1664]{1,0:T(8,128)(2,1)S(1)} %pad_maximum_fusion.x_ref), custom_call_target="tpu_custom_call" | custom-call | flops 2129920 | bytes 212992000 | tf_op jit(solution)/shard_map/pallas_call | solution.py:164
  458.6 5.3 multiply_reduce_fusion
  464.0 4.5 multiply_add_fusion
  468.5 5.3 convolution_convert_fusion.8.do_ref
  473.9 13.5 %convolution_convert_fusion.5 = bf16[1280,1536]{1,0:T(8,128)(2,1)} fusion(bf16[1280,2048]{1,0:T(8,128)(2,1)} %get-tuple-element.51, bf16[1536,2048]{1,0:T(8,128)(2,1)} %all-gather.13.cloned.1.call-done.down_ref), kind=kOutput, calls=%fused_computation.25 | convolution fusion | flops 8055029760 | bytes 15466496 | tf_op jit(solution)/shard_map/dot_general | solution.py:731
  487.4 2.2 copy.149
  489.6 33.5 %shard_map.361 = (bf16[1280,384]{1,0:T(8,128)(2,1)}, bf16[2,1536,256]{2,1,0:T(8,128)(2,1)}) custom-call(bf16[1280,384]{1,0:T(8,128)(2,1)} %copy-done.15, bf16[2,1536,256]{2,1,0:T(8,128)(2,1)} %copy-done.11, bf16[1280,384]{1,0:T(8,128)(2,1)} %convolution_convert_fusion.8.do_ref, bf16[1280,384]{1,0:T(8,128)(2,1)} %copy-done.12, f32[2,8,640]{2,1,0:T(8,128)} %bitcast.81, ...), custom_call_target="tpu_custom_call" | custom-call | flops 30198988800 | bytes 5898240 | tf_op jit(solution)/shard_map/pallas_call | solution.py:498
  523.1 2.3 slice.94
  525.6 3.5 convolution_convert_fusion.9
  529.1 6.4 convolution_convert_fusion.7
  535.6 1.7 copy.140
  539.2 4.9 multiply_subtract_fusion.1
  544.1 1.9 slice.95
  546.0 4.2 reshape.140
  553.0 13.9 %multiply_subtract_fusion = (f32[16,192,2,128]{3,2,1,0:T(2,128)}, f32[16,192,2,128]{3,2,1,0:T(2,128)}, f32[16,192,2,128]{3,2,1,0:T(2,128)}) fusion(f32[16,192,2,128]{3,2,1,0:T(2,128)S(1)} %copy-done.17, f32[8,2,192,2,128]{4,3,2,1,0:T(2,128)S(1)} %copy.143, f32[16,192,2,128]{3,2,1,0:T(2,128)S(1)} %copy-done.22, f32[16,192,2,128]{3,2,1,0:T(2,128)} %param.32), kind=kLoop, calls=%fused_computation.34 | loop fusion | flops 11796480 | bytes 22020096 | tf_op jit(solution)/shard_map/sub | solution.py:54
  567.9 6.4 convolution_convert_fusion.6
  575.1 15.1 %concatenate.53 = bf16[1536,1152]{0,1:T(8,128)(2,1)S(1)} concatenate(bf16[1536,640]{0,1:T(8,128)(2,1)} %convolution_convert_fusion.6, bf16[1536,384]{0,1:T(8,128)(2,1)} %convolution_convert_fusion.7, bf16[1536,16]{0,1:T(8,128)(2,1)} %convolution_convert_fusion.9, bf16[1536,1]{0,1:T(2,128)(2,1)S(1)} %broadcast_in_dim.40, bf16[1536,111]{0,1:T(8,128)(2,1)} %broadcast_in_dim.41), dimensions={1} | concatenate | bytes 7077888 | tf_op jit(solution)/shard_map/concatenate | solution.py:802
  590.2 7.2 convolution_convert_fusion.1.x_ref
  597.4 4.1 copy.150
  601.5 2.1 copy-done.10
  603.6 193.8 %shard_map.362 = bf16[1280,1536]{1,0:T(8,128)(2,1)S(1)} custom-call(bf16[1280,1536]{1,0:T(8,128)(2,1)S(1)} %copy-done.10), custom_call_target="tpu_custom_call" | custom-call | flops 1966080 | bytes 196608000 | tf_op jit(solution)/shard_map/pallas_call | solution.py:164
  797.5 2.9 fusion.7
  800.4 10.0 %all-gather.1 = f32[8,1,1536]{2,1,0:T(1,128)S(1)} all-gather(f32[1,1,1536]{2,1,0:T(1,128)S(1)} %reshape.142), channel_id=2, replica_groups=mesh['dp'=8,'tensor'=4] {'dp'}, dimensions={0}, use_global_device_ids=true | all-gather | bytes 55296 | tf_op jit(solution)/shard_map/all_gather | solution.py:832
  811.1 13.9 %fusion.5 = (f32[1280,1536]{1,0:T(8,128)}, bf16[1280,1536]{1,0:T(8,128)(2,1)}) fusion(f32[1280,1536]{1,0:T(8,128)} %copy-done.16, bf16[1280,1536]{1,0:T(8,128)(2,1)} %copy-done.8, bf16[1280,1536]{1,0:T(8,128)(2,1)} %x_ref.1, f32[1280]{0:T(1024)S(1)} %broadcast_multiply_fusion, f32[1536]{0:T(1024)S(1)} %copy-done.31, f32[1280]{0:T(1024)S(1)} %add_rsqrt_fusion, ...), kind=kLoop, calls=%fused_computation.11 | loop fusion | flops 25559040 | bytes 35405824 | tf_op jit(solution)/shard_map/add | solution.py:827
  832.6 2.3 multiply_subtract_fusion.3
  836.3 4.4 multiply_subtract_fusion.2
  (159 shorter events, 39.5 us)
Async XLA Ops:
  7.2 43.1 %all-gather.7.cloned.1.call-start = ((), (), s32[]{:S(2)}) async-start(), calls=%async_computation.4 | async-start | bytes 3981312 | tf_op jit(solution)/shard_map/all_gather | solution.py:618
  13.5 73.9 %all-gather.9.cloned.1.call-start = ((), (), s32[]{:S(2)}) async-start(), calls=%async_computation.5 | async-start | bytes 1179648 | tf_op jit(solution)/shard_map/all_gather | solution.py:673
  17.7 0.9 copy-start.25
  17.7 1.1 copy-start.26
  18.8 0.6 copy-start.29
  53.2 2.7 copy-start
  61.1 1.9 copy-start.14
  63.0 25.7 %copy-start.15 = (bf16[1280,384]{1,0:T(8,128)(2,1)}, bf16[1280,384]{1,0:T(8,128)(2,1)S(1)}, u32[]{:S(2)}) copy-start(bf16[1280,384]{1,0:T(8,128)(2,1)S(1)} %get-tuple-element.47.q_ref) | copy-start | bytes 2949124
  63.8 166.8 %all-gather.13.cloned.1.call-start = ((), (), s32[]{:S(2)}) async-start(), calls=%async_computation.7 | async-start | bytes 7077888 | tf_op jit(solution)/shard_map/all_gather | solution.py:620
  66.2 164.3 %all-gather.11.cloned.1.call-start = ((), (), s32[]{:S(2)}) async-start(), calls=%async_computation.6 | async-start | bytes 14155776 | tf_op jit(solution)/shard_map/all_gather | solution.py:619
  70.0 7.5 copy-start.33
  77.4 410.0 %reduce-scatter.13.cloned.1.call-start = ((), (), s32[]{:S(2)}) async-start(), calls=%async_computation.11 | async-start | bytes 7077888
  88.7 20.5 %copy-start.11 = (bf16[2,1536,256]{2,1,0:T(8,128)(2,1)}, bf16[2,1536,256]{2,1,0:T(8,128)(2,1)S(1)}, u32[]{:S(2)}) copy-start(bf16[2,1536,256]{2,1,0:T(8,128)(2,1)S(1)} %pad_maximum_fusion.2.kv_ref) | copy-start | bytes 4718596
  109.3 3.9 copy-start.12
  113.1 108.4 %copy-start.1 = (bf16[1280,1536]{1,0:T(8,128)(2,1)S(1)}, bf16[1280,1536]{1,0:T(8,128)(2,1)}, u32[]{:S(2)}) copy-start(bf16[1280,1536]{1,0:T(8,128)(2,1)} %x_ref.1) | copy-start | bytes 11796484
  221.5 1.9 copy-start.4
  227.4 1.9 copy-start.6
  230.6 2.1 copy-start.7
  232.7 41.5 %copy-start.21 = (bf16[1280,1536]{1,0:T(8,128)(2,1)S(1)}, bf16[1280,1536]{1,0:T(8,128)(2,1)}, u32[]{:S(2)}) copy-start(bf16[1280,1536]{1,0:T(8,128)(2,1)} %outgrad_ref.1) | copy-start | bytes 11796484
  318.8 0.8 copy-start.30
  318.8 170.8 %reduce-scatter.9.cloned.1.call-start = ((), (), s32[]{:S(2)}) async-start(), calls=%async_computation.8 | async-start | bytes 14155776 | tf_op jit(solution)/shard_map/reduce_scatter | solution.py:727
  319.4 247.5 %reduce-scatter.11.cloned.1.call-start = ((), (), s32[]{:S(2)}) async-start(), calls=%async_computation.10 | async-start | bytes 1179648 | tf_op jit(solution)/shard_map/reduce_scatter | solution.py:782
  346.1 112.5 %copy-start.2 = (bf16[1280,1536]{1,0:T(8,128)(2,1)S(1)}, bf16[1280,1536]{1,0:T(8,128)(2,1)}, u32[]{:S(2)}) copy-start(bf16[1280,1536]{1,0:T(8,128)(2,1)} %x_ref.1) | copy-start | bytes 11796484
  346.1 112.5 %copy-start.5 = (bf16[1280,1536]{1,0:T(8,128)(2,1)S(1)}, bf16[1280,1536]{1,0:T(8,128)(2,1)}, u32[]{:S(2)}) copy-start(bf16[1280,1536]{1,0:T(8,128)(2,1)} %copy-done.4) | copy-start | bytes 11796484
  458.3 5.6 copy-start.9
  468.5 5.4 copy-start.16
  523.1 6.0 copy-start.13
  525.5 285.6 %all-reduce.4.cloned.1.call-start = ((), (), s32[]{:S(2)}) async-start(), calls=%async_computation.9 | async-start | bytes 7864320 | tf_op jit(solution)/shard_map/psum | solution.py:780
  529.1 6.4 copy-start.20
  537.3 1.4 copy-start.18
  537.3 1.9 copy-start.19
  537.4 288.7 %reduce-scatter.15.cloned.1.call-start = ((), (), s32[]{:S(2)}) async-start(), calls=%async_computation.12 | async-start | bytes 3981312
  550.2 1.9 copy-start.17
  550.2 2.8 copy-start.22
  553.0 13.9 %copy-start.24 = (bf16[2,512,256]{2,1,0:T(8,128)(2,1)S(1)}, bf16[2,512,256]{2,1,0:T(8,128)(2,1)}, u32[]{:S(2)}) copy-start(bf16[2,512,256]{2,1,0:T(8,128)(2,1)} %slice.95) | copy-start | bytes 1572868
  553.0 14.9 %copy-start.34 = (bf16[1280,384]{1,0:T(8,128)(2,1)S(1)}, bf16[1280,384]{1,0:T(8,128)(2,1)}, u32[]{:S(2)}) copy-start(bf16[1280,384]{1,0:T(8,128)(2,1)} %get-tuple-element.61) | copy-start | bytes 2949124
  567.9 6.4 copy-start.28
  601.5 2.1 copy-start.10
  603.6 193.8 %copy-start.3 = (bf16[1280,1536]{1,0:T(8,128)(2,1)S(1)}, bf16[1280,1536]{1,0:T(8,128)(2,1)}, u32[]{:S(2)}) copy-start(bf16[1280,1536]{1,0:T(8,128)(2,1)} %x_ref.1) | copy-start | bytes 11796484
  603.6 193.8 %copy-start.31 = (f32[1536]{0:T(1024)S(1)}, f32[1536]{0:T(1024)}, u32[]{:S(2)}) copy-start(f32[1536]{0:T(1024)} %get-tuple-element.91) | copy-start | bytes 18436
  797.4 2.9 copy-start.8
  825.0 6.2 copy-start.32
  825.0 7.6 copy-start.27
  828.1 8.2 copy-start.23
Sparse Core Ops, SparseCore 0:
  13.6 36.6 all-gather.6
  63.9 23.4 all-gather.8
  89.9 45.5 all-gather.12
  137.8 72.1 all-gather.10
  318.9 59.6 reduce-scatter.12
  382.4 92.3 reduce-scatter.8
  525.6 33.1 reduce-scatter.10
  561.3 210.1 all-reduce.3
  775.4 50.6 reduce-scatter.14

commit v3 on v2

--- a/solution.py
+++ b/solution.py
@@ -24,7 +24,8 @@
 weight_decay = 0.1
 bf16 = jnp.bfloat16
 f32 = jnp.float32
-line_chunks = 10
+line_chunks = 20
+line_lag = 2
 MESH = pl.DeviceIdType.MESH
 
 
@@ -102,7 +103,7 @@
     def step(t, carry):
         for half in (0, 1):
             at = place(half)
-            c = t - at
+            c = t - line_lag * at
 
             @pl.when((c >= 0) & (c < chunks))
             def _():
@@ -127,7 +128,7 @@
 
         for half in (0, 1):
             at = place(half)
-            c = t - 2 * (n - 1) + at
+            c = t - line_lag * (2 * (n - 1) - at)
 
             @pl.when((at < n - 1) & (c >= 0) & (c < chunks))
             def _():
@@ -139,7 +140,7 @@
 
         return carry
 
-    lax.fori_loop(0, chunks + 2 * (n - 1), step, 0)
+    lax.fori_loop(0, chunks + 2 * (n - 1) * line_lag, step, 0)
 
     def finish(c, carry):
         for half in (0, 1):
@@ -330,79 +331,137 @@
 nt = (((1,), (1,)), ((), ()))
 
 
-def attention_kernel(heads, dp, q_ref, kv_ref, o_ref, lse_ref, k_ref, v_ref):
-    prompt_total = kv_ref.shape[1] - CONT
-    me = lax.axis_index(dp)
-    keys = spread(kv_ref[0, :, :128].astype(f32), HEAD_DIM**-0.5)
-    values = spread(kv_ref[0, :, 128:].astype(f32), 1.0)
-    for i, place in enumerate(keys):
-        k_ref[i] = keys[place]
-        v_ref[i] = values[place]
-    index = {place: i for i, place in enumerate(keys)}
-    lane = lax.broadcasted_iota(jnp.int32, (1, 128), 1)
-    for start, rows, length in row_tiles(prompt_total):
-        row = lax.broadcasted_iota(jnp.int32, (rows, 1), 0)
-        if start == 0:
-            masked = 0
-            reach = row + me * PROMPT_DEV
-        else:
-            masked = length - 256
-            reach = row
-        column = lax.broadcasted_iota(jnp.int32, (rows, length - masked), 1)
-        lse = jnp.zeros((rows, 128), f32)
-        pair_out = None
-        for h, (kv, half, pair) in enumerate(head_places(heads)):
-            q = q_ref[start : start + rows, pair * 128 : (pair + 1) * 128]
-            i = index[kv, half]
-            tail = lax.dot_general(q, k_ref[i, masked:length], nt, preferred_element_type=f32)
-            tail = jnp.where(column <= reach, tail, -1e30)
-            top = jnp.max(tail, axis=1, keepdims=True)
-            if masked:
-                head = lax.dot_general(q, k_ref[i, :masked], nt, preferred_element_type=f32)
-                top = jnp.maximum(top, jnp.max(head, axis=1, keepdims=True))
-                p_head = jnp.exp(head - top)
-            p_tail = jnp.exp(tail - top)
-            total = jnp.sum(p_tail, axis=1, keepdims=True)
-            out = jnp.dot(
-                p_tail.astype(bf16), v_ref[i, masked:length], preferred_element_type=f32
-            )
-            if masked:
-                total = total + jnp.sum(p_head, axis=1, keepdims=True)
-                out = out + jnp.dot(
-                    p_head.astype(bf16), v_ref[i, :masked], preferred_element_type=f32
+def meet(me, n):
+    barrier = pltpu.get_barrier_semaphore()
+
+    def greet(k, carry):
+        pl.semaphore_signal(
+            barrier, inc=1, device_id={"dp": lax.rem(me + k, n)}, device_id_type=MESH
+        )
+        return carry
+
+    lax.fori_loop(1, n, greet, 0)
+    pl.semaphore_wait(barrier, n - 1)
+
+
+def load_spread(m, all_ref, kv_ref, k_ref, v_ref, kt_ref=None):
+    total = all_ref.shape[1]
+    own = pl.ds(pl.multiple_of(m * TOK_MB + PROMPT_DEV, 16), CONT)
+    for low, high, rows in ((0, total, all_ref[m]), (total, total + CONT, kv_ref[own])):
+        keys = spread(rows[:, :128].astype(f32), HEAD_DIM**-0.5)
+        values = spread(rows[:, 128:].astype(f32), 1.0)
+        for i, place in enumerate(keys):
+            k_ref[i, low:high] = keys[place]
+            v_ref[i, low:high] = values[place]
+            if kt_ref is not None:
+                kt_ref[i, :, low:high] = keys[place].astype(f32).T.astype(bf16)
+    return {place: i for i, place in enumerate(keys)}
+
+
+def attention_kernel(heads, n, q_ref, kv_ref, o_ref, lse_ref, all_ref, k_ref, v_ref, send, recv):
+    prompt_total = all_ref.shape[1]
+    me = lax.axis_index("dp")
+
+    def piece(m, k):
+        rows = all_ref.at[m, pl.ds(pl.multiple_of(me * PROMPT_DEV, PROMPT_DEV), PROMPT_DEV)]
+        return pltpu.make_async_remote_copy(
+            src_ref=rows,
+            dst_ref=rows,
+            send_sem=send.at[m, k],
+            recv_sem=recv.at[m, k],
+            device_id={"dp": lax.rem(me + k, n)},
+            device_id_type=MESH,
+        )
+
+    for m in range(MICRO):
+        all_ref[m, pl.ds(pl.multiple_of(me * PROMPT_DEV, PROMPT_DEV), PROMPT_DEV)] = kv_ref[
+            m * TOK_MB : m * TOK_MB + PROMPT_DEV
+        ]
+    meet(me, n)
+
+    def every(m, act):
+        def one(k, carry):
+            act(piece(m, k))
+            return carry
+
+        lax.fori_loop(1, n, one, 0)
+
+    for m in range(MICRO):
+        every(m, lambda copy: copy.start())
+
+    def micro(m, carry):
+        every(m, lambda copy: copy.wait_recv())
+        index = load_spread(m, all_ref, kv_ref, k_ref, v_ref)
+        lane = lax.broadcasted_iota(jnp.int32, (1, 128), 1)
+        for start, rows, length in row_tiles(prompt_total):
+            at = pl.ds(pl.multiple_of(m * TOK_MB + start, 128), rows)
+            row = lax.broadcasted_iota(jnp.int32, (rows, 1), 0)
+            if start == 0:
+                masked = 0
+                reach = row + me * PROMPT_DEV
+            else:
+                masked = length - 256
+                reach = row
+            column = lax.broadcasted_iota(jnp.int32, (rows, length - masked), 1)
+            lse = jnp.zeros((rows, 128), f32)
+            pair_out = None
+            for h, (kv, half, pair) in enumerate(head_places(heads)):
+                q = q_ref[at, pair * 128 : (pair + 1) * 128]
+                i = index[kv, half]
+                tail = lax.dot_general(q, k_ref[i, masked:length], nt, preferred_element_type=f32)
+                tail = jnp.where(column <= reach, tail, -1e30)
+                top = jnp.max(tail, axis=1, keepdims=True)
+                if masked:
+                    head = lax.dot_general(q, k_ref[i, :masked], nt, preferred_element_type=f32)
+                    top = jnp.maximum(top, jnp.max(head, axis=1, keepdims=True))
+                    p_head = jnp.exp(head - top)
+                p_tail = jnp.exp(tail - top)
+                total = jnp.sum(p_tail, axis=1, keepdims=True)
+                out = jnp.dot(
+                    p_tail.astype(bf16), v_ref[i, masked:length], preferred_element_type=f32
                 )
-            out = out / total
-            lse = jnp.where(lane == h, top + jnp.log(total), lse)
-            if half == 0:
-                pair_out = out
-            else:
-                o_ref[start : start + rows, pair * 128 : (pair + 1) * 128] = (
-                    pair_out + out
-                ).astype(bf16)
-        lse_ref[start : start + rows] = lse
-
-
-def attention_call(q, kv, dp):
+                if masked:
+                    total = total + jnp.sum(p_head, axis=1, keepdims=True)
+                    out = out + jnp.dot(
+                        p_head.astype(bf16), v_ref[i, :masked], preferred_element_type=f32
+                    )
+                out = out / total
+                lse = jnp.where(lane == h, top + jnp.log(total), lse)
+                if half == 0:
+                    pair_out = out
+                else:
+                    o_ref[at, pair * 128 : (pair + 1) * 128] = (pair_out + out).astype(bf16)
+            lse_ref[at] = lse
+        return carry
+
+    lax.fori_loop(0, MICRO, micro, 0)
+    for m in range(MICRO):
+        every(m, lambda copy: copy.wait_send())
+
+
+def attention_call(q, kv, n):
     count, width = q.shape
-    keys = kv.shape[1]
+    keys = PROMPT_DEV * n + CONT
     heads = width // HEAD_DIM
+    whole = pl.BlockSpec(memory_space=pltpu.VMEM)
     return pl.pallas_call(
-        functools.partial(attention_kernel, heads, dp),
-        grid=(MICRO,),
-        in_specs=[
-            pl.BlockSpec((TOK_MB, width), lambda m: (m, 0)),
-            pl.BlockSpec((1, keys, 256), lambda m: (m, 0, 0)),
-        ],
-        out_specs=[
-            pl.BlockSpec((TOK_MB, width), lambda m: (m, 0)),
-            pl.BlockSpec((TOK_MB, 128), lambda m: (m, 0)),
-        ],
+        functools.partial(attention_kernel, heads, n),
+        in_specs=[whole] * 2,
+        out_specs=[whole] * 3,
         out_shape=[
             jax.ShapeDtypeStruct((count, width), bf16),
             jax.ShapeDtypeStruct((count, 128), f32),
+            jax.ShapeDtypeStruct((MICRO, PROMPT_DEV * n, 256), bf16),
         ],
-        scratch_shapes=[pltpu.VMEM((4, keys, 128), bf16), pltpu.VMEM((4, keys, 128), bf16)],
-        compiler_params=pltpu.CompilerParams(vmem_limit_bytes=48 * 2**20),
+        scratch_shapes=[
+            pltpu.VMEM((4, keys, 128), bf16),
+            pltpu.VMEM((4, keys, 128), bf16),
+            pltpu.SemaphoreType.DMA((MICRO, n)),
+            pltpu.SemaphoreType.DMA((MICRO, n)),
+        ],
+        compiler_params=pltpu.CompilerParams(
+            collective_id=3, has_side_effects=True, vmem_limit_bytes=48 * 2**20
+        ),
         cost_estimate=pl.CostEstimate(
             flops=16 * count * keys * width,
             bytes_accessed=8 * count * width,
@@ -412,122 +471,154 @@
 
 
 def attention_back_kernel(
-    heads, dp, q_ref, kv_ref, do_ref, o_ref, lse_ref, cos_ref, sin_ref, row_cos_ref, row_sin_ref,
-    dq_ref, dkv_ref, k_ref, v_ref, kt_ref, dk_ref, dv_ref,
+    heads, n, q_ref, kv_ref, all_ref, do_ref, o_ref, lse_ref,
+    cos_ref, sin_ref, row_cos_ref, row_sin_ref,
+    grad_ref, k_ref, v_ref, kt_ref, dk_ref, dv_ref, sent_ref, got_ref, send, recv,
 ):
-    prompt_total = kv_ref.shape[1] - CONT
-    me = lax.axis_index(dp)
-    keys = spread(kv_ref[0, :, :128].astype(f32), HEAD_DIM**-0.5)
-    values = spread(kv_ref[0, :, 128:].astype(f32), 1.0)
-    for i, place in enumerate(keys):
-        k_ref[i] = keys[place]
-        v_ref[i] = values[place]
-        kt_ref[i] = keys[place].astype(f32).T.astype(bf16)
-    index = {place: i for i, place in enumerate(keys)}
-    dk_ref[...] = jnp.zeros_like(dk_ref)
-    dv_ref[...] = jnp.zeros_like(dv_ref)
+    prompt_total = all_ref.shape[1]
+    me = lax.axis_index("dp")
+    width = heads * HEAD_DIM
+
+    def piece(m, k):
+        to = lax.rem(me + k, n)
+        return pltpu.make_async_remote_copy(
+            src_ref=sent_ref.at[m, pl.ds(pl.multiple_of(to * PROMPT_DEV, PROMPT_DEV), PROMPT_DEV)],
+            dst_ref=got_ref.at[m, k],
+            send_sem=send.at[m, k],
+            recv_sem=recv.at[m, k],
+            device_id={"dp": to},
+            device_id_type=MESH,
+        )
+
+    def every(m, act):
+        def one(k, carry):
+            act(piece(m, k))
+            return carry
+
+        lax.fori_loop(1, n, one, 0)
+
+    meet(me, n)
     half_rows = (
         lax.broadcasted_iota(jnp.int32, (8, 128), 1) // HEAD_DIM
         == lax.broadcasted_iota(jnp.int32, (8, 128), 0)
     ).astype(f32)
-    for start, rows, length in row_tiles(prompt_total):
-        at = slice(start, start + rows)
-        column = lax.broadcasted_iota(jnp.int32, (1, rows), 1)
-        if start == 0:
-            masked = 0
-            reach = column + me * PROMPT_DEV
-        else:
-            masked = length - 256
-            reach = column
-        key = lax.broadcasted_iota(jnp.int32, (length - masked, rows), 0)
-        back = None
-        for h, (kv, half, pair) in enumerate(head_places(heads)):
-            lanes = slice(pair * 128, (pair + 1) * 128)
-            i = index[kv, half]
-            q, do = q_ref[at, lanes], do_ref[at, lanes]
-            if half == 0:
-                delta_pair = lax.dot_general(
-                    half_rows,
-                    do.astype(f32) * o_ref[at, lanes].astype(f32),
-                    nt,
-                    precision=lax.Precision.HIGHEST,
-                    preferred_element_type=f32,
-                )
-            delta = delta_pair[half : half + 1]
-            lse = lse_ref[0, h : h + 1, at]
-            for low, high in ((0, masked), (masked, length)):
-                if low == high:
-                    continue
-                s = lax.dot_general(k_ref[i, low:high], q, nt, preferred_element_type=f32)
-                if low == masked:
-                    s = jnp.where(key <= reach, s, -1e30)
-                p = jnp.exp(s - lse)
-                dp_ = lax.dot_general(v_ref[i, low:high], do, nt, preferred_element_type=f32)
-                ds = (p * (dp_ - delta)).astype(bf16)
-                dv_ref[i, low:high] += jnp.dot(
-                    p.astype(bf16), do, preferred_element_type=f32
-                )
-                dk_ref[i, low:high] += jnp.dot(ds, q, preferred_element_type=f32)
-                term = jnp.dot(kt_ref[i, :, low:high], ds, preferred_element_type=f32)
-                back = term if back is None else back + term
-            if half == 1:
-                dq_ref[at, lanes] = turn(
-                    back.T, row_cos_ref[at], -row_sin_ref[at]
-                ).astype(bf16)
-                back = None
-    lane = lax.broadcasted_iota(jnp.int32, (kv_ref.shape[1], 128), 1)
-
-    def joined(acc):
-        get = lambda place: acc[index[place]]
-        return jnp.where(
-            lane < HEAD_DIM,
-            get((0, 0)) + pltpu.roll(get((0, 1)), HEAD_DIM, 1),
-            get((1, 1)) + pltpu.roll(get((1, 0)), HEAD_DIM, 1),
-        )
-
-    dk = joined(dk_ref) * HEAD_DIM**-0.5
-    dkv_ref[0, :, :128] = turn(dk, cos_ref[...], -sin_ref[...]).astype(bf16)
-    dkv_ref[0, :, 128:] = joined(dv_ref).astype(bf16)
-
-
-def attention_back_call(q, kv, do, o, lse, cosine, sine, row_cos, row_sin, dp):
+
+    def micro(m, carry):
+        index = load_spread(m, all_ref, kv_ref, k_ref, v_ref, kt_ref)
+        dk_ref[...] = jnp.zeros_like(dk_ref)
+        dv_ref[...] = jnp.zeros_like(dv_ref)
+        for start, rows, length in row_tiles(prompt_total):
+            at = pl.ds(pl.multiple_of(m * TOK_MB + start, 128), rows)
+            inner = slice(start, start + rows)
+            column = lax.broadcasted_iota(jnp.int32, (1, rows), 1)
+            if start == 0:
+                masked = 0
+                reach = column + me * PROMPT_DEV
+            else:
+                masked = length - 256
+                reach = column
+            key = lax.broadcasted_iota(jnp.int32, (length - masked, rows), 0)
+            back = None
+            for h, (kv, half, pair) in enumerate(head_places(heads)):
+                lanes = slice(pair * 128, (pair + 1) * 128)
+                i = index[kv, half]
+                q, do = q_ref[at, lanes], do_ref[at, lanes]
+                if half == 0:
+                    delta_pair = lax.dot_general(
+                        half_rows,
+                        do.astype(f32) * o_ref[at, lanes].astype(f32),
+                        nt,
+                        precision=lax.Precision.HIGHEST,
+                        preferred_element_type=f32,
+                    )
+                delta = delta_pair[half : half + 1]
+                lse = lse_ref[m, h : h + 1, inner]
+                for low, high in ((0, masked), (masked, length)):
+                    if low == high:
+                        continue
+                    s = lax.dot_general(k_ref[i, low:high], q, nt, preferred_element_type=f32)
+                    if low == masked:
+                        s = jnp.where(key <= reach, s, -1e30)
+                    p = jnp.exp(s - lse)
+                    dp_ = lax.dot_general(v_ref[i, low:high], do, nt, preferred_element_type=f32)
+                    ds = (p * (dp_ - delta)).astype(bf16)
+                    dv_ref[i, low:high] += jnp.dot(
+                        p.astype(bf16), do, preferred_element_type=f32
+                    )
+                    dk_ref[i, low:high] += jnp.dot(ds, q, preferred_element_type=f32)
+                    term = jnp.dot(kt_ref[i, :, low:high], ds, preferred_element_type=f32)
+                    back = term if back is None else back + term
+                if half == 1:
+                    grad_ref[at, lanes] = turn(
+                        back.T, row_cos_ref[inner], -row_sin_ref[inner]
+                    ).astype(bf16)
+                    back = None
+        lane = lax.broadcasted_iota(jnp.int32, (dk_ref.shape[1], 128), 1)
+
+        def joined(acc):
+            get = lambda place: acc[index[place]]
+            return jnp.where(
+                lane < HEAD_DIM,
+                get((0, 0)) + pltpu.roll(get((0, 1)), HEAD_DIM, 1),
+                get((1, 1)) + pltpu.roll(get((1, 0)), HEAD_DIM, 1),
+            )
+
+        dk = turn(joined(dk_ref) * HEAD_DIM**-0.5, cos_ref[...], -sin_ref[...]).astype(bf16)
+        dv = joined(dv_ref).astype(bf16)
+        sent_ref[m, :, :128] = dk[:prompt_total]
+        sent_ref[m, :, 128:] = dv[:prompt_total]
+        every(m, lambda copy: copy.start())
+        own = pl.ds(pl.multiple_of(m * TOK_MB + PROMPT_DEV, 128), CONT)
+        grad_ref[own, width : width + 128] = dk[prompt_total:]
+        grad_ref[own, width + 128 :] = dv[prompt_total:]
+        return carry
+
+    lax.fori_loop(0, MICRO, micro, 0)
+
+    def collect(m, carry):
+        every(m, lambda copy: copy.wait_recv())
+        own = sent_ref[m, pl.ds(pl.multiple_of(me * PROMPT_DEV, PROMPT_DEV), PROMPT_DEV)]
+        total = lax.fori_loop(
+            1, n, lambda k, t: t + got_ref[m, k].astype(f32), own.astype(f32)
+        )
+        at = pl.ds(pl.multiple_of(m * TOK_MB, 128), PROMPT_DEV)
+        grad_ref[at, width:] = total.astype(bf16)
+        every(m, lambda copy: copy.wait_send())
+        return carry
+
+    lax.fori_loop(0, MICRO, collect, 0)
+
+
+def attention_back_call(q, kv, prompts, do, o, lse, cosine, sine, row_cos, row_sin, n):
     count, width = q.shape
-    keys = kv.shape[1]
+    keys = prompts.shape[1] + CONT
     heads = width // HEAD_DIM
-    rows = pl.BlockSpec((TOK_MB, width), lambda m: (m, 0))
+    whole = pl.BlockSpec(memory_space=pltpu.VMEM)
     return pl.pallas_call(
-        functools.partial(attention_back_kernel, heads, dp),
-        grid=(MICRO,),
-        in_specs=[
-            rows,
-            pl.BlockSpec((1, keys, 256), lambda m: (m, 0, 0)),
-            rows,
-            rows,
-            pl.BlockSpec((1, 8, TOK_MB), lambda m: (m, 0, 0)),
-            pl.BlockSpec((keys, 128), lambda m: (0, 0)),
-            pl.BlockSpec((keys, 128), lambda m: (0, 0)),
-            pl.BlockSpec((TOK_MB, 128), lambda m: (0, 0)),
-            pl.BlockSpec((TOK_MB, 128), lambda m: (0, 0)),
-        ],
-        out_specs=[rows, pl.BlockSpec((1, keys, 256), lambda m: (m, 0, 0))],
-        out_shape=[
-            jax.ShapeDtypeStruct((count, width), bf16),
-            jax.ShapeDtypeStruct((MICRO, keys, 256), bf16),
-        ],
+        functools.partial(attention_back_kernel, heads, n),
+        in_specs=[whole] * 10,
+        out_specs=whole,
+        out_shape=jax.ShapeDtypeStruct((count, width + 256), bf16),
         scratch_shapes=[
             pltpu.VMEM((4, keys, 128), bf16),
             pltpu.VMEM((4, keys, 128), bf16),
             pltpu.VMEM((4, 128, keys), bf16),
             pltpu.VMEM((4, keys, 128), f32),
             pltpu.VMEM((4, keys, 128), f32),
+            pltpu.VMEM((MICRO, prompts.shape[1], 256), bf16),
+            pltpu.VMEM((MICRO, n, PROMPT_DEV, 256), bf16),
+            pltpu.SemaphoreType.DMA((MICRO, n)),
+            pltpu.SemaphoreType.DMA((MICRO, n)),
         ],
-        compiler_params=pltpu.CompilerParams(vmem_limit_bytes=56 * 2**20),
+        compiler_params=pltpu.CompilerParams(
+            collective_id=4, has_side_effects=True, vmem_limit_bytes=56 * 2**20
+        ),
         cost_estimate=pl.CostEstimate(
             flops=40 * count * keys * width,
             bytes_accessed=12 * count * width,
             transcendentals=count * keys * heads,
         ),
-    )(q, kv, do, o, lse, cosine, sine, row_cos, row_sin)
+    )(q, kv, prompts, do, o, lse, cosine, sine, row_cos, row_sin)
 
 
 def attend(queries, keys_all, values_all, allowed):
@@ -669,12 +760,12 @@
         both = jnp.concatenate(
             [keys.reshape(count, -1), mixed[:, queries_width + kv_local * HEAD_DIM :]], axis=1
         ).astype(bf16)
-    both = both.reshape(MICRO, TOK_MB, both_width)
-    prompt_both = lax.all_gather(both[:, :PROMPT_DEV], "dp", axis=1, tiled=True)
-    both_all = jnp.concatenate([prompt_both, both[:, PROMPT_DEV:]], axis=1)
     if in_kernels:
-        attended, lse = attention_call(queries, both_all, "dp")
+        attended, lse, prompt_both = attention_call(queries, both, n_dp)
     else:
+        both = both.reshape(MICRO, TOK_MB, both_width)
+        prompt_both = lax.all_gather(both[:, :PROMPT_DEV], "dp", axis=1, tiled=True)
+        both_all = jnp.concatenate([prompt_both, both[:, PROMPT_DEV:]], axis=1)
         inner = jnp.arange(TOK_MB, dtype=jnp.int32)
         positions = jnp.where(
             inner < PROMPT_DEV, device_index * PROMPT_DEV + inner, prompt_total + inner - PROMPT_DEV
@@ -732,7 +823,6 @@
         bf16
     )
     summed = line_sum(jnp.concatenate([rows_grad, gate_grad.astype(bf16)], axis=1), n_tensor, 2)
-
     model = tokens.shape[1]
     gate_grad = summed[:, model : model + EXPERTS].astype(f32)
     outgrad = cotangent.astype(f32)
@@ -740,7 +830,7 @@
     logits_grad = chosen_grad.astype(bf16)
     router_grad = lax.dot_general(
         normed_second, logits_grad, contract_first, preferred_element_type=f32
-    )
+    ).astype(bf16)
     normed_second_grad = summed[:, :model].astype(f32) + lax.dot_general(
         logits_grad, router_full, contract_last, preferred_element_type=f32
     )
@@ -754,16 +844,18 @@
     branch_own = middle_grad.astype(bf16)
     outproj_grad = lax.dot_general(
         branch_own, attended, contract_first, preferred_element_type=f32
-    )
+    ).astype(bf16)
     attended_grad = jnp.dot(branch_own, outproj_full, preferred_element_type=f32).astype(bf16)
     attended_grad, down_grad, gateup_grad, mixture = lax.optimization_barrier(
         (attended_grad, down_grad, gateup_grad, mixture)
     )
+    mixture = lax.psum(mixture, "tensor")
+    block_out = (middle + mixture.astype(f32)).astype(bf16)
     if in_kernels:
         lse_rows = lse[:, :8].reshape(MICRO, TOK_MB, 8).transpose(0, 2, 1)
-        queries_grad, both_grad = attention_back_call(
-            queries, both_all, attended_grad, attended, lse_rows,
-            cos_all, sin_all, cos_row, sin_row, "dp",
+        mixed_grad = attention_back_call(
+            queries, both, prompt_both, attended_grad, attended, lse_rows,
+            cos_all, sin_all, cos_row, sin_row, n_dp,
         )
     else:
         queries_grad, both_grad = [], []
@@ -774,41 +866,40 @@
             queries_grad.append(dq.reshape(TOK_MB, -1, HEAD_DIM))
             both_grad.append(jnp.concatenate([t.reshape(-1, both_width // 2) for t in (dk, dv)], 1))
         queries_grad = rotate(jnp.concatenate(queries_grad, axis=0), cosine, -sine)
-        queries_grad = queries_grad.reshape(count, -1).astype(bf16)
         both_grad = jnp.stack(both_grad)
-    both_grad, mixture = lax.optimization_barrier((both_grad, mixture))
-    mixture = lax.psum(mixture, "tensor")
-    block_out = (middle + mixture.astype(f32)).astype(bf16)
-    prompt_grad = lax.psum_scatter(
-        both_grad[:, :prompt_total].astype(bf16), "dp", scatter_dimension=1, tiled=True
-    )
-    both_grad = jnp.concatenate(
-        [prompt_grad.astype(both_grad.dtype), both_grad[:, prompt_total:]], axis=1
-    ).reshape(count, both_width)
-    if not in_kernels:
+        prompt_grad = lax.psum_scatter(
+            both_grad[:, :prompt_total].astype(bf16), "dp", scatter_dimension=1, tiled=True
+        )
+        both_grad = jnp.concatenate(
+            [prompt_grad.astype(f32), both_grad[:, prompt_total:]], axis=1
+        ).reshape(count, both_width)
         keys_grad = rotate(
             both_grad[:, : both_width // 2].reshape(count, -1, HEAD_DIM), cosine, -sine
         )
-        both_grad = jnp.concatenate(
-            [keys_grad.reshape(count, -1), both_grad[:, both_width // 2 :]], axis=1
+        mixed_grad = jnp.concatenate(
+            [
+                queries_grad.reshape(count, -1),
+                keys_grad.reshape(count, -1),
+                both_grad[:, both_width // 2 :],
+            ],
+            axis=1,
         ).astype(bf16)
-    mixed_grad = jnp.concatenate([queries_grad, both_grad], axis=1)
     normed_first_grad = lax.dot_general(
         mixed_grad, inproj_full, contract_last, preferred_element_type=f32
     ).astype(bf16)
     inproj_grad = lax.dot_general(
         normed_first, mixed_grad, contract_first, preferred_element_type=f32
-    )
+    ).astype(bf16)
     attn_grad = jnp.concatenate(
         [
             inproj_grad,
             outproj_grad,
             router_grad,
-            gain_second_grad[:, None],
-            jnp.zeros((model, 127 - EXPERTS), f32),
+            gain_second_grad[:, None].astype(bf16),
+            jnp.zeros((model, 127 - EXPERTS), bf16),
         ],
         axis=1,
-    ).astype(bf16)
+    )
     down_next = adam_update(
         down_weight, down_first, down_second,
         down_grad.T.reshape(down_weight.shape).astype(f32), weight_decay, 0.05,

time: 855 us -> 778 us (0.910)
  Pallas kernels: 515 us -> 472 us
  waiting for transfers between devices: 42 us -> 22.9 us
  matrix products: 113 us -> 101 us
    pallas_call x3, Pallas kernels: 414 us -> 347 us  [line_sum(): pl.pallas_call(functools.partial(line_sum_kernel, n, chunks), out_shape=j...]
    pallas_call x2, Pallas kernels: 54 us -> 77.5 us  [the longest x1 43.6 us: attention_back_call(): pl.pallas_call(functools.partial(attention_back_kernel, heads, n), in_spe...]
    all_gather x1 -> x0, waiting for transfers between devices: 9.51 us -> none  [shards(): prompt_both = lax.all_gather(both[:, :PROMPT_DEV], 'dp', axis=1, tiled=True)]
    unnamed x75 -> x93, local copies, waits for them, and re-layouts: 28.7 us -> 29.2 us
  transfers between devices with their start and end apart: 9 -> 7, of which waited for: 3 -> 1; matrix products, arithmetic and copies ran while one was open for 21% -> 21% of each run, Pallas kernels for 51% -> 56%
where the time goes in v3:
time: 778 us; the launch traced here: 768 us
  Pallas kernels  472 us (61%)
  matrix products  101 us (13%)
  local copies, waits for them, and re-layouts  76.3 us (10%)
  other arithmetic  70.5 us (9%)
  waiting for transfers between devices  22.9 us (3%)
  between operations  15.5 us (2%)
  blocking collectives  9.25 us (1%)
    pallas_call x3, Pallas kernels, line_sum(): pl.pallas_call(functools.partial(line_sum_kernel, n, chunks), out_shape=j...  347 us
    pallas_call x1, Pallas kernels, attention_back_call(): pl.pallas_call(functools.partial(attention_back_kernel, heads, n), in_spe...  43.6 us
    pallas_call x1, Pallas kernels, expert_call(): pl.pallas_call(functools.partial(expert_kernel, group), grid=(steps,), in...  41.4 us
    pallas_call x1, Pallas kernels, attention_call(): pl.pallas_call(functools.partial(attention_kernel, heads, n), in_specs=[w...  33.9 us
    unnamed x93, local copies, waits for them, and re-layouts  29.2 us
    sub x6, other arithmetic, adam_update(): weight - learn_rate * (update + decay_rate * weight)  27.5 us
    dot_general x1, matrix products, shards(): lax.dot_general(hidden_grad, gu_full, contract_last, preferred_element_ty...  23.6 us
    dot_general x1, matrix products, shards(): lax.dot_general(normed_second, hidden_grad, contract_first, preferred_ele...  23.2 us
  transfers between devices with their start and end apart: 7, of which 1 were waited for; matrix products, arithmetic and copies ran while one was open for 21% of the time, Pallas kernels for 56%

profile of v3, /device:TPU:0, one launch (start us, length us, event | category | flops | bytes accessed | tf_op | source)
XLA Modules:
  0.0 767.9 jit_solution(6850102093735957581)
XLA Ops:
  17.4 1.8 concatenate.32
  19.3 2.4 bitcast_bitcast_fusion
  23.1 2.4 copy.156
  25.6 2.4 reshape.133
  28.5 2.8 fusion.30
  33.9 22.2 %all-gather.6.cloned.1.call-done = bf16[1536,1152]{1,0:T(8,128)(2,1)} async-done(((bf16[192,1152]{1,0:T(8,128)(2,1)}), bf16[1536,1152]{1,0:T(8,128)(2,1)}) %all-gather.6.cloned.1.call-update) | async-done | bytes 3538960 | tf_op jit(solution)/shard_map/all_gather | solution.py:709
  57.3 1.5 fusion.38
  59.1 1.9 slice.89.w_ref
  61.7 5.4 shard_map.356
  67.2 1.9 copy-done.11
  69.0 33.9 %shard_map.357 = (bf16[1280,384]{1,0:T(8,128)(2,1)S(1)}, f32[1280,128]{1,0:T(8,128)S(1)}, bf16[2,1024,256]{2,1,0:T(8,128)(2,1)S(1)}) custom-call(bf16[1280,384]{1,0:T(8,128)(2,1)S(1)} %get-tuple-element.44.q_ref, bf16[1280,256]{1,0:T(8,128)(2,1)S(1)} %get-tuple-element.45.kv_ref), custom_call_target="tpu_custom_call" | custom-call | flops 12079595520 | bytes 3932160 | tf_op jit(solution)/shard_map/pallas_call | solution.py:447
  103.0 4.2 convolution_convert_fusion.4.x_ref
  107.3 102.1 %shard_map.358 = bf16[1280,1536]{1,0:T(8,128)(2,1)S(1)} custom-call(bf16[1280,1536]{1,0:T(8,128)(2,1)S(1)} %convolution_convert_fusion.4.x_ref), custom_call_target="tpu_custom_call" | custom-call | flops 1966080 | bytes 196608000 | tf_op jit(solution)/shard_map/pallas_call | solution.py:165
  211.4 1.8 multiply_convert_fusion.rows_ref
  213.2 2.1 select_reduce_fusion
  215.3 1.9 copy-done.5
  220.1 2.1 copy-done.6
  222.3 41.4 %shard_map.359 = (bf16[1280,2048]{1,0:T(8,128)(2,1)}, bf16[1280,4096]{1,0:T(8,128)(2,1)}, f32[1280,128]{1,0:T(8,128)S(1)}) custom-call(bf16[1280,1536]{1,0:T(8,128)(2,1)S(1)} %copy-done.6, bf16[1280,1536]{1,0:T(8,128)(2,1)} %outgrad_ref.1, f32[1280,128]{1,0:T(8,128)S(1)} %pad.9.gates_ref, bf16[1536,4096]{1,0:T(8,128)(2,1)} %all-gather.8.cloned.1.call-done.gu_ref, ...), custom_call_target="tpu_custom_call" | custom-call | flops 24159191040 | bytes 34603008 | tf_op jit(solution)/shard_map/pallas_call | solution.py:226
  263.7 12.6 %fusion.10 = bf16[1536,2048]{0,1:T(8,128)(2,1)} fusion(bf16[1280,2048]{1,0:T(8,128)(2,1)} %get-tuple-element.48, bf16[1280,1536]{1,0:T(8,128)(2,1)S(1)} %copy-done.22), kind=kOutput, calls=%fused_computation.27 | convolution fusion | flops 8056209408 | bytes 15466496 | tf_op jit(solution)/shard_map/dot_general | solution.py:808
  276.3 23.2 %convolution_convert_fusion = bf16[1536,4096]{1,0:T(8,128)(2,1)} fusion(bf16[1280,1536]{1,0:T(8,128)(2,1)S(1)} %copy-done.6, bf16[1280,4096]{1,0:T(8,128)(2,1)} %get-tuple-element.49), kind=kOutput, calls=%fused_computation | convolution fusion | flops 16112418816 | bytes 27000832 | tf_op jit(solution)/shard_map/dot_general | solution.py:811
  299.5 8.7 %copy.148 = bf16[1536,2048]{1,0:T(8,128)(2,1)} copy(bf16[1536,2048]{0,1:T(8,128)(2,1)} %fusion.10) | data formatting | bytes 12582912
  311.4 23.6 %convolution_convert_fusion.2 = bf16[1280,1536]{1,0:T(8,128)(2,1)S(1)} fusion(bf16[1280,4096]{1,0:T(8,128)(2,1)} %get-tuple-element.49, bf16[1536,4096]{1,0:T(8,128)(2,1)} %all-gather.8.cloned.1.call-done.gu_ref), kind=kOutput, calls=%fused_computation.22 | convolution fusion | flops 16108093440 | bytes 27000832 | tf_op jit(solution)/shard_map/dot_general | solution.py:819
  335.4 106.3 %shard_map.360 = bf16[1280,1664]{1,0:T(8,128)(2,1)S(1)} custom-call(bf16[1280,1664]{1,0:T(8,128)(2,1)S(1)} %pad_maximum_fusion.x_ref), custom_call_target="tpu_custom_call" | custom-call | flops 2129920 | bytes 212992000 | tf_op jit(solution)/shard_map/pallas_call | solution.py:165
  442.0 5.8 multiply_reduce_fusion
  449.2 4.5 multiply_add_fusion
  453.8 2.8 convolution_convert_fusion.7
  456.6 1.7 copy-done.16
  458.3 5.2 convolution_convert_fusion.8.do_ref
  463.6 10.1 %convolution_convert_fusion.5 = bf16[1280,1536]{1,0:T(8,128)(2,1)} fusion(bf16[1280,2048]{1,0:T(8,128)(2,1)S(1)} %bitcast.82, bf16[1536,2048]{1,0:T(8,128)(2,1)S(1)} %bitcast.80), kind=kOutput, calls=%fused_computation.25 | convolution fusion | flops 8055029760 | bytes 15466496 | tf_op jit(solution)/shard_map/dot_general | solution.py:822
  473.7 1.4 copy.149
  475.2 43.6 %shard_map.361 = bf16[1280,640]{1,0:T(8,128)(2,1)} custom-call(bf16[1280,384]{1,0:T(8,128)(2,1)} %copy-done.13, bf16[1280,256]{1,0:T(8,128)(2,1)} %copy-done.14, bf16[2,1024,256]{2,1,0:T(8,128)(2,1)} %copy-done.15, bf16[1280,384]{1,0:T(8,128)(2,1)} %convolution_convert_fusion.8.do_ref, bf16[1280,384]{1,0:T(8,128)(2,1)} %copy-done.10, f32[2,8,640]{2,1,0:T(8,128)} %bitcast.77, ...), custom_call_target="tpu_custom_call" | custom-call | flops 30198988800 | bytes 5898240 | tf_op jit(solution)/shard_map/pallas_call | solution.py:597
  518.8 5.5 convolution_convert_fusion.6
  524.5 1.7 copy.140
  526.2 4.2 reshape.141
  530.4 3.3 copy.143
  534.4 15.1 %concatenate.40 = bf16[1536,1152]{0,1:T(8,128)(2,1)S(1)} concatenate(bf16[1536,640]{0,1:T(8,128)(2,1)} %convolution_convert_fusion.6, bf16[1536,384]{0,1:T(8,128)(2,1)} %convolution_convert_fusion.7, bf16[1536,16]{0,1:T(8,128)(2,1)} %convolution_convert_fusion.9, bf16[1536,1]{0,1:T(2,128)(2,1)S(1)} %convert_element_type.205, bf16[1536,111]{0,1:T(8,128)(2,1)} %broadcast_in_dim.37), dimensions={1} | concatenate | bytes 7077888 | tf_op jit(solution)/shard_map/concatenate | solution.py:893
  549.5 6.1 multiply_subtract_fusion.1
  555.6 4.8 convolution_convert_fusion.1.x_ref
  562.1 12.1 %multiply_subtract_fusion = (f32[16,192,2,128]{3,2,1,0:T(2,128)}, f32[16,192,2,128]{3,2,1,0:T(2,128)}, f32[16,192,2,128]{3,2,1,0:T(2,128)}) fusion(f32[16,192,2,128]{3,2,1,0:T(2,128)S(1)} %copy-done.18, f32[8,2,192,2,128]{4,3,2,1,0:T(2,128)S(1)} %copy-done.19, f32[16,192,2,128]{3,2,1,0:T(2,128)S(1)} %copy-done.23, f32[16,192,2,128]{3,2,1,0:T(2,128)S(1)} %copy-done.24), kind=kLoop, calls=%fused_computation.34 | loop fusion | flops 11796480 | bytes 22020096 | tf_op jit(solution)/shard_map/sub | solution.py:55
  574.2 3.9 copy.150
  578.2 2.1 copy-done.9
  580.3 139.0 %shard_map.362 = bf16[1280,1536]{1,0:T(8,128)(2,1)S(1)} custom-call(bf16[1280,1536]{1,0:T(8,128)(2,1)S(1)} %copy-done.9), custom_call_target="tpu_custom_call" | custom-call | flops 1966080 | bytes 196608000 | tf_op jit(solution)/shard_map/pallas_call | solution.py:165
  719.3 2.9 fusion.7
  722.3 9.2 %all-gather.1 = f32[8,1,1536]{2,1,0:T(1,128)S(1)} all-gather(f32[1,1,1536]{2,1,0:T(1,128)S(1)} %reshape.143), channel_id=2, replica_groups=mesh['dp'=8,'tensor'=4] {'dp'}, dimensions={0}, use_global_device_ids=true | all-gather | bytes 55296 | tf_op jit(solution)/shard_map/all_gather | solution.py:923
  732.2 13.7 %fusion.5 = (f32[1280,1536]{1,0:T(8,128)}, bf16[1280,1536]{1,0:T(8,128)(2,1)}) fusion(f32[1280,1536]{1,0:T(8,128)} %copy-done.16, bf16[1280,1536]{1,0:T(8,128)(2,1)} %copy-done.8, bf16[1280,1536]{1,0:T(8,128)(2,1)} %x_ref.1, f32[1280]{0:T(1024)S(1)} %broadcast_multiply_fusion, f32[1536]{0:T(1024)S(1)} %copy-done.33, f32[1280]{0:T(1024)S(1)} %add_rsqrt_fusion, ...), kind=kLoop, calls=%fused_computation.11 | loop fusion | flops 25559040 | bytes 35405824 | tf_op jit(solution)/shard_map/add | solution.py:918
  749.2 1.7 copy.145
  752.5 2.3 multiply_subtract_fusion.3
  756.1 4.4 multiply_subtract_fusion.2
  (167 shorter events, 36.4 us)
Async XLA Ops:
  7.2 48.9 %all-gather.6.cloned.1.call-start = ((), (), s32[]{:S(2)}) async-start(), calls=%async_computation.3 | async-start | bytes 3981312 | tf_op jit(solution)/shard_map/all_gather | solution.py:709
  8.5 13.3 %copy-start.17 = (f32[16,192,2,128]{3,2,1,0:T(2,128)S(1)}, f32[16,192,2,128]{3,2,1,0:T(2,128)}, u32[]{:S(2)}) copy-start(f32[16,192,2,128]{3,2,1,0:T(2,128)} %param.30) | copy-start | bytes 9437188
  19.3 200.1 %all-gather.10.cloned.1.call-start = ((), (), s32[]{:S(2)}) async-start(), calls=%async_computation.5 | async-start | bytes 7077888 | tf_op jit(solution)/shard_map/all_gather | solution.py:711
  21.8 198.4 %all-gather.8.cloned.1.call-start = ((), (), s32[]{:S(2)}) async-start(), calls=%async_computation.4 | async-start | bytes 14155776 | tf_op jit(solution)/shard_map/all_gather | solution.py:710
  23.1 4.9 copy-start.37
  28.0 445.7 %reduce-scatter.10.cloned.1.call-start = ((), (), s32[]{:S(2)}) async-start(), calls=%async_computation.8 | async-start | bytes 7077888
  28.5 189.0 %copy-start.30 = (pred[1280,16]{1,0:T(8,128)(4,1)}, pred[1280,16]{1,0:T(8,128)(4,1)S(1)}, u32[]{:S(2)}) copy-start(pred[1280,16]{1,0:T(8,128)(4,1)S(1)} %copy.136) | copy-start | bytes 61444
  32.6 0.9 copy-start.27
  32.6 1.1 copy-start.28
  33.8 22.3 %copy-start.31 = (f32[128,128]{1,0:T(8,128)}, f32[128,128]{1,0:T(8,128)S(1)}, u32[]{:S(2)}) copy-start(f32[128,128]{1,0:T(8,128)S(1)} %constant_dynamic-slice_fusion) | copy-start | bytes 196612
  59.0 2.7 copy-start
  67.1 1.9 copy-start.11
  69.0 33.9 %copy-start.13 = (bf16[1280,384]{1,0:T(8,128)(2,1)}, bf16[1280,384]{1,0:T(8,128)(2,1)S(1)}, u32[]{:S(2)}) copy-start(bf16[1280,384]{1,0:T(8,128)(2,1)S(1)} %get-tuple-element.44.q_ref) | copy-start | bytes 2949124
  69.0 33.9 %copy-start.14 = (bf16[1280,256]{1,0:T(8,128)(2,1)}, bf16[1280,256]{1,0:T(8,128)(2,1)S(1)}, u32[]{:S(2)}) copy-start(bf16[1280,256]{1,0:T(8,128)(2,1)S(1)} %get-tuple-element.45.kv_ref) | copy-start | bytes 1966084
  103.0 4.3 copy-start.15
  103.0 350.7 %copy-start.10 = (bf16[1280,384]{1,0:T(8,128)(2,1)}, bf16[1280,384]{1,0:T(8,128)(2,1)S(1)}, u32[]{:S(2)}) copy-start(bf16[1280,384]{1,0:T(8,128)(2,1)S(1)} %get-tuple-element.46.o_ref) | copy-start | bytes 2949124
  209.4 1.9 copy-start.3
  215.3 1.9 copy-start.5
  220.1 2.1 copy-start.6
  222.3 41.4 %copy-start.22 = (bf16[1280,1536]{1,0:T(8,128)(2,1)S(1)}, bf16[1280,1536]{1,0:T(8,128)(2,1)}, u32[]{:S(2)}) copy-start(bf16[1280,1536]{1,0:T(8,128)(2,1)} %outgrad_ref.1) | copy-start | bytes 11796484
  308.2 166.9 %reduce-scatter.8.cloned.1.call-start = ((), (), s32[]{:S(2)}) async-start(), calls=%async_computation.6 | async-start | bytes 14155776 | tf_op jit(solution)/shard_map/reduce_scatter | solution.py:818
  308.8 423.4 %all-reduce.4.cloned.1.call-start = ((), (), s32[]{:S(2)}) async-start(), calls=%async_computation.7 | async-start | bytes 7864320 | tf_op jit(solution)/shard_map/psum | solution.py:852
  335.3 106.4 %copy-start.21 = (f32[1280,16]{1,0:T(8,128)S(1)}, f32[1280,16]{1,0:T(8,128)}, u32[]{:S(2)}) copy-start(f32[1280,16]{1,0:T(8,128)} %copy-done.20) | copy-start | bytes 245764
  335.3 106.7 %copy-start.1 = (bf16[1280,1536]{1,0:T(8,128)(2,1)S(1)}, bf16[1280,1536]{1,0:T(8,128)(2,1)}, u32[]{:S(2)}) copy-start(bf16[1280,1536]{1,0:T(8,128)(2,1)} %x_ref.1) | copy-start | bytes 11796484
  335.3 106.7 %copy-start.4 = (bf16[1280,1536]{1,0:T(8,128)(2,1)S(1)}, bf16[1280,1536]{1,0:T(8,128)(2,1)}, u32[]{:S(2)}) copy-start(bf16[1280,1536]{1,0:T(8,128)(2,1)} %copy-done.3) | copy-start | bytes 11796484
  335.3 106.7 %copy-start.35 = (f32[1280]{0:T(1024)S(1)}, f32[1280]{0:T(1024)}, u32[]{:S(2)}) copy-start(f32[1280]{0:T(1024)} %copy-done.34) | copy-start | bytes 15364
  442.0 5.8 copy-start.7
  453.7 4.6 copy-start.16
  453.7 9.8 %slice-start = ((s8[6291456]{0:T(1024)(128)(4,1)}), s8[4194304]{0:T(1024)(128)(4,1)S(1)}, s32[]{:S(2)}) async-start(s8[6291456]{0:T(1024)(128)(4,1)} %bitcast.79), calls=%async_computation.10 | async-start | bytes 8388608
  453.7 9.8 %slice-start.2 = ((s8[5242880]{0:T(1024)(128)(4,1)}), s8[4194304]{0:T(1024)(128)(4,1)S(1)}, s32[]{:S(2)}) async-start(s8[5242880]{0:T(1024)(128)(4,1)} %bitcast.81), calls=%async_computation.12 | async-start | bytes 8388608
  458.3 5.3 slice-start.1
  458.3 5.3 slice-start.3
  475.1 270.8 %reduce-scatter.12.cloned.1.call-start = ((), (), s32[]{:S(2)}) async-start(), calls=%async_computation.9 | async-start | bytes 3981312
  475.2 43.6 %copy-start.12 = (bf16[1280,1536]{1,0:T(8,128)(2,1)S(1)}, bf16[1280,1536]{1,0:T(8,128)(2,1)}, u32[]{:S(2)}) copy-start(bf16[1280,1536]{1,0:T(8,128)(2,1)} %copy-done.11) | copy-start | bytes 11796484
  549.5 6.1 copy-start.26
  549.5 6.1 copy-start.39
  555.6 4.9 copy-start.18
  555.6 4.9 copy-start.19
  555.6 5.7 copy-start.23
  555.6 6.5 copy-start.24
  574.2 3.9 copy-start.38
  578.2 2.1 copy-start.9
  580.3 139.0 %copy-start.2 = (bf16[1280,1536]{1,0:T(8,128)(2,1)S(1)}, bf16[1280,1536]{1,0:T(8,128)(2,1)}, u32[]{:S(2)}) copy-start(bf16[1280,1536]{1,0:T(8,128)(2,1)} %x_ref.1) | copy-start | bytes 11796484
  580.3 139.0 %copy-start.33 = (f32[1536]{0:T(1024)S(1)}, f32[1536]{0:T(1024)}, u32[]{:S(2)}) copy-start(f32[1536]{0:T(1024)} %get-tuple-element.85) | copy-start | bytes 18436
  719.3 2.9 copy-start.8
  745.9 5.2 copy-start.36
  745.9 6.6 copy-start.29
  748.0 8.2 %copy-start.25 = (f32[192,2,320]{2,1,0:T(2,128)S(1)}, f32[192,2,320]{2,1,0:T(2,128)}, u32[]{:S(2)}) copy-start(f32[192,2,320]{2,1,0:T(2,128)} %param.24) | copy-start | bytes 1474564
  (3 other events, 2.3 us)
Sparse Core Ops, SparseCore 0:
  19.4 36.6 all-gather.5
  58.5 56.6 all-gather.9
  117.7 72.1 all-gather.7
  308.3 61.3 reduce-scatter.9
  373.5 92.4 reduce-scatter.7
  475.3 181.2 all-reduce.3
  660.5 51.3 reduce-scatter.11

commit v4 on v3

--- a/solution.py
+++ b/solution.py
@@ -24,9 +24,10 @@
 weight_decay = 0.1
 bf16 = jnp.bfloat16
 f32 = jnp.float32
-line_chunks = 20
+line_parts = 20
 line_lag = 2
 MESH = pl.DeviceIdType.MESH
+nt = (((1,), (1,)), ((), ()))
 
 
 def angles_for(positions, head_size):
@@ -55,25 +56,36 @@
     return (weight - learn_rate * (update + decay_rate * weight), first_next, second_next)
 
 
-def line_sum_kernel(n, chunks, x_ref, o_ref, held, send_red, recv_red, send_out, recv_out):
+def line_steps(n):
+    return line_parts + 2 * (n - 1) * line_lag
+
+
+def line_engine(
+    n, x_ref, o_ref, held, send_red, recv_red, send_out, recv_out, complete=lambda at: None
+):
     me = lax.axis_index("tensor")
-    rows = x_ref.shape[0] // (2 * chunks)
+    parts = line_parts
+    rows = x_ref.shape[0] // (2 * parts)
     low, high = me - 1, me + 1
 
-    barrier = pltpu.get_barrier_semaphore()
-
-    @pl.when(me > 0)
-    def _():
-        pl.semaphore_signal(barrier, inc=1, device_id={"tensor": low}, device_id_type=MESH)
-
-    @pl.when(me < n - 1)
-    def _():
-        pl.semaphore_signal(barrier, inc=1, device_id={"tensor": high}, device_id_type=MESH)
-
-    pl.semaphore_wait(barrier, jnp.where((me > 0) & (me < n - 1), 2, 1))
+    def greet():
+        barrier = pltpu.get_barrier_semaphore()
+
+        @pl.when(me > 0)
+        def _():
+            pl.semaphore_signal(barrier, inc=1, device_id={"tensor": low}, device_id_type=MESH)
+
+        @pl.when(me < n - 1)
+        def _():
+            pl.semaphore_signal(barrier, inc=1, device_id={"tensor": high}, device_id_type=MESH)
+
+        return jnp.where((me > 0) & (me < n - 1), 2, 1)
+
+    def begin():
+        pl.semaphore_wait(pltpu.get_barrier_semaphore(), greet())
 
     def part(half, c):
-        return pl.ds(pl.multiple_of((half * chunks + c) * rows, 16), rows)
+        return pl.ds(pl.multiple_of((half * parts + c) * rows, 16), rows)
 
     def reduce_copy(half, c, src):
         to = low if half == 0 else high
@@ -100,12 +112,12 @@
     def place(half):
         return n - 1 - me if half == 0 else me
 
-    def step(t, carry):
+    def slot(t):
         for half in (0, 1):
             at = place(half)
             c = t - line_lag * at
 
-            @pl.when((c >= 0) & (c < chunks))
+            @pl.when((c >= 0) & (c < parts))
             def _():
                 @pl.when(at == 0)
                 def _():
@@ -125,12 +137,13 @@
                     def _():
                         o_ref[part(half, c)] = total.astype(o_ref.dtype)
                         out_copy(half, c).start()
+                        complete(part(half, c))
 
         for half in (0, 1):
             at = place(half)
             c = t - line_lag * (2 * (n - 1) - at)
 
-            @pl.when((at < n - 1) & (c >= 0) & (c < chunks))
+            @pl.when((at < n - 1) & (c >= 0) & (c < parts))
             def _():
                 out_copy(half, c).wait_recv()
 
@@ -138,37 +151,54 @@
                 def _():
                     out_copy(half, c).start()
 
+                complete(part(half, c))
+
+    def finish():
+        def one(c, carry):
+            for half in (0, 1):
+                at = place(half)
+
+                @pl.when(at < n - 1)
+                def _():
+                    reduce_copy(half, c, held).wait_send()
+
+                @pl.when(at > 0)
+                def _():
+                    out_copy(half, c).wait_send()
+
+            return carry
+
+        lax.fori_loop(0, parts, one, 0)
+
+    return greet, begin, slot, finish
+
+
+def line_scratch(shape, dtype):
+    return [pltpu.VMEM(shape, dtype)] + [
+        pltpu.SemaphoreType.DMA((2, line_parts)) for _ in range(4)
+    ]
+
+
+def line_sum_kernel(n, x_ref, o_ref, *scratch):
+    _, begin, slot, finish = line_engine(n, x_ref, o_ref, *scratch)
+    begin()
+
+    def step(t, carry):
+        slot(t)
         return carry
 
-    lax.fori_loop(0, chunks + 2 * (n - 1) * line_lag, step, 0)
-
-    def finish(c, carry):
-        for half in (0, 1):
-            at = place(half)
-
-            @pl.when(at < n - 1)
-            def _():
-                reduce_copy(half, c, held).wait_send()
-
-            @pl.when(at > 0)
-            def _():
-                out_copy(half, c).wait_send()
-
-        return carry
-
-    lax.fori_loop(0, chunks, finish, 0)
+    lax.fori_loop(0, line_steps(n), step, 0)
+    finish()
 
 
 def line_sum(x, n, barrier_id):
     rows, width = x.shape
-    chunks = line_chunks
     return pl.pallas_call(
-        functools.partial(line_sum_kernel, n, chunks),
+        functools.partial(line_sum_kernel, n),
         out_shape=jax.ShapeDtypeStruct(x.shape, x.dtype),
         in_specs=[pl.BlockSpec(memory_space=pltpu.VMEM)],
         out_specs=pl.BlockSpec(memory_space=pltpu.VMEM),
-        scratch_shapes=[pltpu.VMEM(x.shape, x.dtype)]
-        + [pltpu.SemaphoreType.DMA((2, chunks)) for _ in range(4)],
+        scratch_shapes=line_scratch(x.shape, x.dtype),
         compiler_params=pltpu.CompilerParams(
             collective_id=barrier_id, has_side_effects=True, vmem_limit_bytes=24 * 2**20
         ),
@@ -176,6 +206,445 @@
             flops=rows * width, bytes_accessed=100 * rows * width, transcendentals=0
         ),
     )(x)
+
+
+gather_parts = 3
+
+
+def gather_engine(n, pairs, own_sem, far_send, far_recv, near_send, near_recv):
+    me = lax.axis_index("dp")
+    core, chip, chips = lax.rem(me, 2), me // 2, n // 2
+
+    def rows(a, p):
+        size = pairs[a][0].shape[0] // gather_parts
+        return pl.ds(p * size, size)
+
+    def far(a, p, k):
+        x_ref, out_ref = pairs[a]
+        return pltpu.make_async_remote_copy(
+            src_ref=x_ref.at[rows(a, p)],
+            dst_ref=out_ref.at[me, rows(a, p)],
+            send_sem=far_send.at[a, p, k],
+            recv_sem=far_recv.at[a, p, k],
+            device_id={"dp": lax.rem(chip + k, chips) * 2 + core},
+            device_id_type=MESH,
+        )
+
+    def near(a, p, k):
+        x_ref, out_ref = pairs[a]
+        owner = lax.rem(chip + chips - k, chips) * 2 + core
+        target = out_ref.at[owner, rows(a, p)]
+        return pltpu.make_async_remote_copy(
+            src_ref=x_ref.at[rows(a, p)] if k == 0 else target,
+            dst_ref=target,
+            send_sem=near_send.at[a, p, k],
+            recv_sem=near_recv.at[a, p, k],
+            device_id={"dp": me + 1 - 2 * core},
+            device_id_type=MESH,
+        )
+
+    def own(a):
+        x_ref, out_ref = pairs[a]
+        return pltpu.make_async_copy(x_ref, out_ref.at[me], own_sem.at[a])
+
+    arrays = range(len(pairs))
+
+    def greet():
+        barrier = pltpu.get_barrier_semaphore()
+        for k in range(1, chips):
+            pl.semaphore_signal(
+                barrier,
+                inc=1,
+                device_id={"dp": lax.rem(chip + k, chips) * 2 + core},
+                device_id_type=MESH,
+            )
+        pl.semaphore_signal(
+            barrier, inc=1, device_id={"dp": me + 1 - 2 * core}, device_id_type=MESH
+        )
+        return chips
+
+    def start():
+        for p in range(gather_parts):
+            for a in arrays:
+                for k in range(1, chips):
+                    far(a, p, k).start()
+        for p in range(gather_parts):
+            for a in arrays:
+                near(a, p, 0).start()
+        for a in arrays:
+            own(a).start()
+
+    def forward(p):
+        for a in arrays:
+            for k in range(1, chips):
+                far(a, p, k).wait_recv()
+                near(a, p, k).start()
+
+    def finish():
+        for a in arrays:
+            own(a).wait()
+            for p in range(gather_parts):
+                for k in range(chips):
+                    near(a, p, k).wait_recv()
+                    near(a, p, k).wait_send()
+                    if k:
+                        far(a, p, k).wait_send()
+
+    return greet, start, forward, finish
+
+
+def gather_scratch(arrays, n):
+    return [pltpu.SemaphoreType.DMA((arrays,))] + [
+        pltpu.SemaphoreType.DMA((arrays, gather_parts, n // 2)) for _ in range(4)
+    ]
+
+
+def gather_kernel(n, x_ref, out_ref, *scratch):
+    greet, start, forward, finish = gather_engine(n, [(x_ref, out_ref)], *scratch)
+    pl.semaphore_wait(pltpu.get_barrier_semaphore(), greet())
+    start()
+    for p in range(gather_parts):
+        forward(p)
+    finish()
+
+
+def gather(x, n, barrier_id):
+    depth, width = x.shape
+    out = pl.pallas_call(
+        functools.partial(gather_kernel, n),
+        out_shape=jax.ShapeDtypeStruct((n, depth, width), x.dtype),
+        in_specs=[pl.BlockSpec(memory_space=pltpu.VMEM)],
+        out_specs=pl.BlockSpec(memory_space=pltpu.VMEM),
+        scratch_shapes=gather_scratch(1, n),
+        compiler_params=pltpu.CompilerParams(
+            collective_id=barrier_id, has_side_effects=True, vmem_limit_bytes=16 * 2**20
+        ),
+    )(x)
+    return out.reshape(n * depth, width)
+
+
+def line_gather_kernel(n, n_dp, x_ref, a_ref, b_ref, o_ref, a_out, b_out, *scratch):
+    line, spread_out = scratch[:5], scratch[5:]
+    greet, _, slot, finish = line_engine(n, x_ref, o_ref, *line)
+    greet_dp, start, forward, finish_dp = gather_engine(
+        n_dp, [(a_ref, a_out), (b_ref, b_out)], *spread_out
+    )
+    peers = greet() + greet_dp()
+    pl.semaphore_wait(pltpu.get_barrier_semaphore(), peers)
+    start()
+
+    def step(t, carry):
+        slot(t)
+        return carry
+
+    total = line_steps(n)
+    done = 0
+    for p in range(gather_parts):
+        until = total * (p + 1) // gather_parts
+        lax.fori_loop(done, until, step, 0)
+        done = until
+        forward(p)
+    finish()
+    finish_dp()
+
+
+def line_gather(x, a, b, n, n_dp, barrier_id):
+    rows, width = x.shape
+    whole, anywhere = pl.BlockSpec(memory_space=pltpu.VMEM), pl.BlockSpec(memory_space=pl.ANY)
+    o, a_all, b_all = pl.pallas_call(
+        functools.partial(line_gather_kernel, n, n_dp),
+        out_shape=[jax.ShapeDtypeStruct(x.shape, x.dtype)]
+        + [jax.ShapeDtypeStruct((n_dp,) + t.shape, t.dtype) for t in (a, b)],
+        in_specs=[whole, anywhere, anywhere],
+        out_specs=[whole, anywhere, anywhere],
+        scratch_shapes=line_scratch(x.shape, x.dtype) + gather_scratch(2, n_dp),
+        compiler_params=pltpu.CompilerParams(
+            collective_id=barrier_id, has_side_effects=True, vmem_limit_bytes=24 * 2**20
+        ),
+        cost_estimate=pl.CostEstimate(
+            flops=rows * width, bytes_accessed=100 * rows * width, transcendentals=0
+        ),
+    )(x, a, b)
+    return o, a_all.reshape(-1, a.shape[1]), b_all.reshape(-1, b.shape[1])
+
+
+def last_kernel(
+    n, n_dp, x_ref, tokens_ref, middle_ref, gain_ref, weights_ref, gain_second_ref,
+    grad_ref, weights_out, gains_out, o_ref, held, send_red, recv_red, send_out, recv_out,
+    tokens_v, middle_v, grad_v, in_sem, out_sem, got, w_send, w_recv,
+    g_from, g_got, g_send, g_recv, z_from, z_got, z_send, z_recv, acc,
+):
+    me, line = lax.axis_index("dp"), lax.axis_index("tensor")
+    model = x_ref.shape[1]
+    rows = x_ref.shape[0] // (2 * line_parts)
+    depth = weights_out.shape[0]
+
+    def norm_of(at):
+        x = tokens_v[at].astype(f32)
+        inverse = lax.rsqrt(jnp.mean(x * x, axis=-1, keepdims=True) + eps_norm)
+        return x * inverse, inverse
+
+    def complete(at):
+        norm, inverse = norm_of(at)
+        grad = o_ref[at].astype(f32) * gain_ref[0:1]
+        mean = jnp.mean(grad * norm, axis=-1, keepdims=True)
+        grad_v[at] = middle_v[at] + inverse * (grad - norm * mean)
+
+    _, _, slot, finish = line_engine(
+        n, x_ref, o_ref, held, send_red, recv_red, send_out, recv_out, complete
+    )
+
+    def weights_copy(k):
+        to = lax.rem(me + k, n_dp)
+        return pltpu.make_async_remote_copy(
+            src_ref=weights_ref.at[to], dst_ref=got.at[k],
+            send_sem=w_send.at[k], recv_sem=w_recv.at[k],
+            device_id={"dp": to}, device_id_type=MESH,
+        )
+
+    def gains_copy(k):
+        to = lax.rem(me + k, n_dp)
+        return pltpu.make_async_remote_copy(
+            src_ref=g_from.at[to], dst_ref=g_got.at[k],
+            send_sem=g_send.at[k], recv_sem=g_recv.at[k],
+            device_id={"dp": to}, device_id_type=MESH,
+        )
+
+    def line_copy(k):
+        to = lax.rem(line + k, n)
+        return pltpu.make_async_remote_copy(
+            src_ref=z_from, dst_ref=z_got.at[k],
+            send_sem=z_send.at[k], recv_sem=z_recv.at[k],
+            device_id={"tensor": to}, device_id_type=MESH,
+        )
+
+    def loop(count, act):
+        def one(k, carry):
+            act(k)
+            return carry
+
+        lax.fori_loop(1, count, one, 0)
+
+    load_tokens = pltpu.make_async_copy(tokens_ref, tokens_v, in_sem.at[0])
+    load_middle = pltpu.make_async_copy(middle_ref, middle_v, in_sem.at[1])
+    load_tokens.start()
+    load_middle.start()
+    barrier = pltpu.get_barrier_semaphore()
+
+    def greet(axis, place, count):
+        loop(
+            count,
+            lambda k: pl.semaphore_signal(
+                barrier, inc=1, device_id={axis: lax.rem(place + k, count)}, device_id_type=MESH
+            ),
+        )
+
+    greet("dp", me, n_dp)
+    greet("tensor", line, n)
+    pl.semaphore_wait(barrier, n_dp + n - 2)
+    loop(n_dp, lambda k: weights_copy(k).start())
+    acc[...] = jnp.zeros_like(acc)
+    load_tokens.wait()
+    load_middle.wait()
+
+    def step(t, carry):
+        slot(t)
+
+        @pl.when(t < line_parts)
+        def _():
+            for half in (0, 1):
+                at = pl.ds(pl.multiple_of((half * line_parts + t) * rows, 16), rows)
+                norm, _ = norm_of(at)
+                term = x_ref[at].astype(f32) * norm
+                acc[...] += jnp.sum(term.reshape(rows // 8, 8, model), axis=0)
+
+        return carry
+
+    total = line_steps(n)
+    lax.fori_loop(0, line_parts, step, 0)
+    width = g_from.shape[2]
+    for p in range(n_dp):
+        moved = acc[...] if p == 0 else pltpu.roll(acc[...], model - p * depth, 1)
+        g_from[p, :8] = moved[:, :width]
+        g_from[p, 8:] = gain_second_ref[p]
+    loop(n_dp, lambda k: gains_copy(k).start())
+    late = min(line_parts + 4, total)
+    lax.fori_loop(line_parts, late, step, 0)
+    loop(n_dp, lambda k: gains_copy(k).wait_recv())
+    z_from[...] = lax.fori_loop(1, n_dp, lambda k, t: t + g_got[k], g_from[me])
+    loop(n, lambda k: line_copy(k).start())
+    loop(n_dp, lambda k: weights_copy(k).wait_recv())
+    lax.fori_loop(late, total, step, 0)
+    size = 32
+
+    def add(b, carry):
+        at = pl.ds(pl.multiple_of(b * size, 16), size)
+        weights_out[at] = lax.fori_loop(
+            1, n_dp, lambda k, t: t + got[k, at].astype(f32), weights_ref[me, at].astype(f32)
+        )
+        return carry
+
+    every = pltpu.make_async_copy(grad_v, grad_ref, out_sem)
+    every.start()
+    lax.fori_loop(0, depth // size, add, 0)
+    loop(n, lambda k: line_copy(k).wait_recv())
+    gains_out[...] = lax.fori_loop(1, n, lambda k, t: t + z_got[k], z_from[...])
+    finish()
+    loop(n_dp, lambda k: weights_copy(k).wait_send())
+    loop(n_dp, lambda k: gains_copy(k).wait_send())
+    loop(n, lambda k: line_copy(k).wait_send())
+    every.wait()
+
+
+def last_call(x, tokens, middle, gain, weights, gain_second, n, n_dp, barrier_id):
+    count, model = x.shape
+    depth, width = model // n_dp, weights.shape[1]
+    lanes = -(-depth // 128) * 128
+    gain_second = jnp.where(lax.axis_index("tensor") == 0, gain_second, 0.0)
+    gain_second = jnp.pad(
+        gain_second.reshape(n_dp, 1, depth), ((0, 0), (0, 7), (0, lanes - depth))
+    )
+    whole, anywhere = pl.BlockSpec(memory_space=pltpu.VMEM), pl.BlockSpec(memory_space=pl.ANY)
+    dma = pltpu.SemaphoreType.DMA
+    grad, weights, gains = pl.pallas_call(
+        functools.partial(last_kernel, n, n_dp),
+        out_shape=[
+            jax.ShapeDtypeStruct((count, model), f32),
+            jax.ShapeDtypeStruct((depth, width), f32),
+            jax.ShapeDtypeStruct((16, lanes), f32),
+        ],
+        in_specs=[whole, anywhere, anywhere, whole, whole, whole],
+        out_specs=[anywhere, whole, whole],
+        scratch_shapes=[pltpu.VMEM(x.shape, bf16)]
+        + line_scratch(x.shape, x.dtype)
+        + [
+            pltpu.VMEM((count, model), bf16),
+            pltpu.VMEM((count, model), f32),
+            pltpu.VMEM((count, model), f32),
+            dma((2,)),
+            dma,
+            pltpu.VMEM((n_dp, depth, width), bf16),
+            dma((n_dp,)),
+            dma((n_dp,)),
+            pltpu.VMEM((n_dp, 16, lanes), f32),
+            pltpu.VMEM((n_dp, 16, lanes), f32),
+            dma((n_dp,)),
+            dma((n_dp,)),
+            pltpu.VMEM((16, lanes), f32),
+            pltpu.VMEM((n, 16, lanes), f32),
+            dma((n,)),
+            dma((n,)),
+            pltpu.VMEM((8, model), f32),
+        ],
+        compiler_params=pltpu.CompilerParams(
+            collective_id=barrier_id, has_side_effects=True, vmem_limit_bytes=56 * 2**20
+        ),
+        cost_estimate=pl.CostEstimate(
+            flops=count * model, bytes_accessed=2**20, transcendentals=0
+        ),
+    )(x, tokens, middle, gain, weights.reshape(n_dp, depth, width), gain_second)
+    gains = jnp.stack([jnp.sum(gains[:8, :depth], axis=0), gains[8, :depth]])
+    return grad, weights, gains
+
+
+def expert_grads_kernel(
+    n, shape, x_ref, rows_ref, outgrad_ref, down_ref, hidden_ref, active_ref, active_rows_ref,
+    o_ref, gateup_grad_ref, down_grad_ref, mixture_ref, rows_t, outgrad_t, o_sem, sum_ref, *scratch,
+):
+    mixture_steps, gateup_steps, down_steps = shape
+    i = pl.program_id(0)
+    steps = sum(shape)
+    _, begin, slot, finish = line_engine(n, x_ref, sum_ref, *scratch)
+    total = line_steps(n)
+    each = -(-total // steps)
+    pl.when(i == 0)(begin)
+
+    def slots(low, high):
+        def one(j, carry):
+            t = i * each + j
+            pl.when(t < total)(lambda: slot(t))
+            return carry
+
+        lax.fori_loop(low, high, one, 0)
+
+    slots(0, 1)
+
+    @pl.when(i < mixture_steps)
+    def _():
+        mixture_ref[...] = lax.dot_general(
+            active_rows_ref[...], down_ref[...], nt, preferred_element_type=f32
+        ).astype(bf16)
+        size = active_rows_ref.shape[0]
+        columns = pl.ds(pl.multiple_of(i * size, size), size)
+        rows_t[:, columns] = rows_ref[...].T
+        outgrad_t[:, columns] = outgrad_ref[...].T
+
+    @pl.when((i >= mixture_steps) & (i < mixture_steps + gateup_steps))
+    def _():
+        gateup_grad_ref[...] = jnp.dot(
+            rows_t[...], hidden_ref[...], preferred_element_type=f32
+        ).astype(bf16)
+
+    @pl.when(i >= mixture_steps + gateup_steps)
+    def _():
+        down_grad_ref[...] = jnp.dot(
+            outgrad_t[...], active_ref[...], preferred_element_type=f32
+        ).astype(bf16)
+
+    slots(1, each)
+
+    @pl.when(i == steps - 1)
+    def _():
+        copy = pltpu.make_async_copy(sum_ref, o_ref, o_sem)
+        copy.start()
+        finish()
+        copy.wait()
+
+
+def expert_grads_call(x, rows, outgrad, down, hidden, active, n, barrier_id):
+    tokens, model = rows.shape
+    block, tile = min(512, active.shape[1]), 256
+    c, a, b = shape = (tokens // tile, hidden.shape[1] // block, active.shape[1] // block)
+    whole = pl.BlockSpec(memory_space=pltpu.VMEM)
+    first = lambda i: (jnp.minimum(i, c - 1), 0)
+    second = lambda i: (0, jnp.clip(i - c, 0, a - 1))
+    third = lambda i: (0, jnp.clip(i - c - a, 0, b - 1))
+    return pl.pallas_call(
+        functools.partial(expert_grads_kernel, n, shape),
+        grid=(a + b + c,),
+        in_specs=[
+            whole,
+            pl.BlockSpec((tile, model), first),
+            pl.BlockSpec((tile, model), first),
+            whole,
+            pl.BlockSpec((tokens, block), second),
+            pl.BlockSpec((tokens, block), third),
+            pl.BlockSpec((tile, active.shape[1]), first),
+        ],
+        out_specs=[
+            pl.BlockSpec(memory_space=pl.ANY),
+            pl.BlockSpec((model, block), second),
+            pl.BlockSpec((model, block), third),
+            pl.BlockSpec((tile, model), first),
+        ],
+        out_shape=[
+            jax.ShapeDtypeStruct(x.shape, x.dtype),
+            jax.ShapeDtypeStruct((model, hidden.shape[1]), bf16),
+            jax.ShapeDtypeStruct((model, active.shape[1]), bf16),
+            jax.ShapeDtypeStruct((tokens, model), bf16),
+        ],
+        scratch_shapes=[pltpu.VMEM((model, tokens), bf16)] * 2
+        + [pltpu.SemaphoreType.DMA, pltpu.VMEM(x.shape, x.dtype)]
+        + line_scratch(x.shape, x.dtype),
+        compiler_params=pltpu.CompilerParams(
+            collective_id=barrier_id, has_side_effects=True, vmem_limit_bytes=58 * 2**20
+        ),
+        cost_estimate=pl.CostEstimate(
+            flops=2 * tokens * model * (hidden.shape[1] + 2 * active.shape[1]),
+            bytes_accessed=10 * tokens * model,
+            transcendentals=0,
+        ),
+    )(x, rows, outgrad, down, hidden, active, active)
 
 
 def expert_kernel(group, rows_ref, outgrad_ref, gates_ref, gu_ref, down_ref,
@@ -326,9 +795,6 @@
     for start in range(0, CONT, 256):
         tiles.append((PROMPT_DEV + start, 256, prompt_total + start + 256))
     return tiles
-
-
-nt = (((1,), (1,)), ((), ()))
 
 
 def meet(me, n):
@@ -706,11 +1172,9 @@
         ],
         axis=1,
     )
-    attn_full = lax.all_gather(attn_local, "dp", axis=0, tiled=True)
-    gu_full = lax.all_gather(gateup_flat(gateup_weight.astype(bf16)), "dp", axis=0, tiled=True)
-    down_full = lax.all_gather(
-        down_weight.reshape(EXPERTS * hidden, depth).T.astype(bf16), "dp", axis=0, tiled=True
-    )
+    attn_full = gather(attn_local, n_dp, 5)
+    gu_local = gateup_flat(gateup_weight.astype(bf16))
+    down_local = down_weight.reshape(EXPERTS * hidden, depth).T.astype(bf16)
     inproj_full = attn_full[:, :in_width]
     outproj_full = attn_full[:, in_width : in_width + out_width]
     small_full = attn_full[:, in_width + out_width :]
@@ -788,7 +1252,7 @@
     branch = lax.dot_general(
         attended, outproj_full, (((1,), (1,)), ((), ())), preferred_element_type=f32
     ).astype(bf16)
-    branch = line_sum(branch, n_tensor, 1)
+    branch, gu_full, down_full = line_gather(branch, gu_local, down_local, n_tensor, n_dp, 6)
 
     middle = inputs + branch.astype(f32)
     inverse_second = lax.rsqrt(jnp.mean(middle * middle, axis=-1, keepdims=True) + eps_norm)
@@ -805,31 +1269,23 @@
     )
     contract_last = (((1,), (1,)), ((), ()))
     contract_first = (((0,), (0,)), ((), ()))
-    down_grad = lax.dot_general(
-        cotangent, active, contract_first, preferred_element_type=f32
-    ).astype(bf16)
-    gateup_grad = lax.dot_general(
-        normed_second, hidden_grad, contract_first, preferred_element_type=f32
-    ).astype(bf16)
-    hidden_grad, down_grad, gateup_grad = lax.optimization_barrier(
-        (hidden_grad, down_grad, gateup_grad)
-    )
-    down_grad = lax.psum_scatter(down_grad, "dp", scatter_dimension=0, tiled=True)
-    gateup_grad = lax.psum_scatter(gateup_grad, "dp", scatter_dimension=0, tiled=True)
     rows_grad = lax.dot_general(
         hidden_grad, gu_full, contract_last, preferred_element_type=f32
     ).astype(bf16)
-    mixture = lax.dot_general(active, down_full, contract_last, preferred_element_type=f32).astype(
-        bf16
-    )
-    summed = line_sum(jnp.concatenate([rows_grad, gate_grad.astype(bf16)], axis=1), n_tensor, 2)
+    summed, gateup_grad, down_grad, mixture = expert_grads_call(
+        jnp.concatenate([rows_grad, gate_grad.astype(bf16)], axis=1),
+        normed_second, cotangent, down_full, hidden_grad, active, n_tensor, 2,
+    )
+    mixture = lax.psum(mixture, "tensor")
     model = tokens.shape[1]
     gate_grad = summed[:, model : model + EXPERTS].astype(f32)
     outgrad = cotangent.astype(f32)
     chosen_grad = gates * (gate_grad - jnp.sum(gates * gate_grad, axis=-1, keepdims=True))
     logits_grad = chosen_grad.astype(bf16)
     router_grad = lax.dot_general(
-        normed_second, logits_grad, contract_first, preferred_element_type=f32
+        normed_second,
+        jnp.pad(logits_grad, ((0, 0), (0, 128 - EXPERTS))),
+        contract_first, preferred_element_type=f32
     ).astype(bf16)
     normed_second_grad = summed[:, :model].astype(f32) + lax.dot_general(
         logits_grad, router_full, contract_last, preferred_element_type=f32
@@ -841,16 +1297,14 @@
         - norm_second * jnp.mean(norm_second_grad * norm_second, axis=-1, keepdims=True)
     )
 
+    middle_grad, down_grad, gateup_grad = lax.optimization_barrier((middle_grad, down_grad, gateup_grad))
+    down_grad = lax.psum_scatter(down_grad, "dp", scatter_dimension=0, tiled=True)
+    gateup_grad = lax.psum_scatter(gateup_grad, "dp", scatter_dimension=0, tiled=True)
     branch_own = middle_grad.astype(bf16)
     outproj_grad = lax.dot_general(
         branch_own, attended, contract_first, preferred_element_type=f32
     ).astype(bf16)
     attended_grad = jnp.dot(branch_own, outproj_full, preferred_element_type=f32).astype(bf16)
-    attended_grad, down_grad, gateup_grad, mixture = lax.optimization_barrier(
-        (attended_grad, down_grad, gateup_grad, mixture)
-    )
-    mixture = lax.psum(mixture, "tensor")
-    block_out = (middle + mixture.astype(f32)).astype(bf16)
     if in_kernels:
         lse_rows = lse[:, :8].reshape(MICRO, TOK_MB, 8).transpose(0, 2, 1)
         mixed_grad = attention_back_call(
@@ -895,8 +1349,6 @@
             inproj_grad,
             outproj_grad,
             router_grad,
-            gain_second_grad[:, None].astype(bf16),
-            jnp.zeros((model, 127 - EXPERTS), bf16),
         ],
         axis=1,
     )
@@ -908,28 +1360,17 @@
         gateup_weight, gateup_first, gateup_second,
         gateup_back(gateup_grad).astype(f32), weight_decay, 0.05,
     )
-    normed_first_grad, attn_grad, down_next, gateup_next = lax.optimization_barrier(
-        (normed_first_grad, attn_grad, down_next, gateup_next)
-    )
-    attn_grad = lax.psum_scatter(attn_grad, "dp", scatter_dimension=0, tiled=True).astype(f32)
-    normed_first_grad = line_sum(normed_first_grad, n_tensor, 1).astype(f32)
-    norm_first_grad = normed_first_grad * gain_first
-    gain_first_grad = jnp.sum(normed_first_grad * norm_first, axis=0)
-    tokens_grad = middle_grad + inverse_first * (
-        norm_first_grad
-        - norm_first * jnp.mean(norm_first_grad * norm_first, axis=-1, keepdims=True)
-    )
-
-    gain_first_parts = lax.all_gather(gain_first_grad, "dp")
-    gain_first_grad = lax.dynamic_slice_in_dim(
-        jnp.sum(gain_first_parts, axis=0), device_index * depth, depth, 0
-    )
+    tokens_grad, attn_grad, gains_grad = last_call(
+        normed_first_grad, tokens, middle_grad, jnp.pad(gain_first, ((0, 7), (0, 0))),
+        attn_grad, gain_second_grad, n_tensor, n_dp, 7,
+    )
+    mixture, tokens_grad = lax.optimization_barrier((mixture, tokens_grad))
+    block_out = (middle + mixture.astype(f32)).astype(bf16)
     split = (in_width, in_width + out_width, in_width + out_width + EXPERTS)
-    inproj_grad, outproj_grad, router_grad, gain_second_grad = (
+    inproj_grad, outproj_grad, router_grad = (
         attn_grad[:, : split[0]],
         attn_grad[:, split[0] : split[1]],
         attn_grad[:, split[1] : split[2]],
-        attn_grad[:, split[2]],
     )
     updates = (
         adam_update(
@@ -942,10 +1383,7 @@
         gateup_next,
         down_next,
         adam_update(router_weight, router_first, router_second, router_grad, weight_decay, 0.05),
-        adam_update(
-            gains, gains_first, gains_second,
-            jnp.stack([gain_first_grad, gain_second_grad]), 0.0, 0.4,
-        ),
+        adam_update(gains, gains_first, gains_second, gains_grad, 0.0, 0.4),
     )
     return (block_out, tokens_grad) + sum(updates, ())
 

time: 778 us -> 761 us (0.978)
  Pallas kernels: 472 us -> 530 us
  matrix products: 101 us -> 57.5 us
  waiting for transfers between devices: 22.9 us -> 0.59 us
  blocking collectives: 9.25 us -> 0 us
    pallas_call x3 -> x4, Pallas kernels: 347 us -> 410 us  [the longest x1 144 us: last_call(): pl.pallas_call(functools.partial(last_kernel, n, n_dp), out_shape=[jax.Sh...]
    dot_general x4 -> x1, matrix products: 47.3 us -> 3.47 us  [shards(): lax.dot_general(normed_second, jnp.pad(logits_grad, ((0, 0), (0, 128 - EX...]
    all_gather x3 -> x0, waiting for transfers between devices: 22.3 us -> none  [the longest x1 22.2 us: shards(): attn_full = lax.all_gather(attn_local, 'dp', axis=0, tiled=True)]
    add x2 -> x1, other arithmetic: 15.2 us -> 0.92 us  [shards(): gain_second = small_t[1:2] + small_t[3:4]]
    convert_element_type x5 -> x4, other arithmetic: 4.68 us -> 15.1 us  [the longest x1 8.06 us: shards(): block_out = (middle + mixture.astype(f32)).astype(bf16)]
    all_gather x1 -> x0, blocking collectives: 9.25 us -> none  [shards(): gain_first_parts = lax.all_gather(gain_first_grad, 'dp')]
    concatenate x1, local copies, waits for them, and re-layouts: 15.1 us -> 6.04 us  [shards(): jnp.concatenate([inproj_grad, outproj_grad, router_grad], axis=1)]
    unnamed x93 -> x118, local copies, waits for them, and re-layouts: 29.2 us -> 32.7 us
  transfers between devices with their start and end apart: 7 -> 3, of which waited for: 1 -> 0; matrix products, arithmetic and copies ran while one was open for 21% -> 11% of each run, Pallas kernels for 56% -> 25%
where the time goes in v4:
time: 761 us; the launch traced here: 751 us
  Pallas kernels  530 us (70%)
  other arithmetic  75.5 us (10%)
  local copies, waits for them, and re-layouts  71.3 us (9%)
  matrix products  57.5 us (8%)
  between operations  16.6 us (2%)
    pallas_call x1, Pallas kernels, last_call(): pl.pallas_call(functools.partial(last_kernel, n, n_dp), out_shape=[jax.Sh...  144 us
    pallas_call x1, Pallas kernels, expert_grads_call(): pl.pallas_call(functools.partial(expert_grads_kernel, n, shape), grid=(a...  122 us
    pallas_call x1, Pallas kernels, line_gather(): pl.pallas_call(functools.partial(line_gather_kernel, n, n_dp), out_shape=...  119 us
    pallas_call x1, Pallas kernels, attention_back_call(): pl.pallas_call(functools.partial(attention_back_kernel, heads, n), in_spe...  43.5 us
    pallas_call x1, Pallas kernels, expert_call(): pl.pallas_call(functools.partial(expert_kernel, group), grid=(steps,), in...  41.3 us
    unnamed x118, local copies, waits for them, and re-layouts  32.7 us
    pallas_call x1, Pallas kernels, attention_call(): pl.pallas_call(functools.partial(attention_kernel, heads, n), in_specs=[w...  29.7 us
    sub x6, other arithmetic, adam_update(): weight - learn_rate * (update + decay_rate * weight)  27 us
  transfers between devices with their start and end apart: 3, of which 0 were waited for; matrix products, arithmetic and copies ran while one was open for 11% of the time, Pallas kernels for 25%

profile of v4, /device:TPU:0, one launch (start us, length us, event | category | flops | bytes accessed | tf_op | source)
XLA Modules:
  0.0 751.3 jit_solution(15819863770463084137)
XLA Ops:
  9.8 2.8 fusion.21
  20.4 25.5 %shard_map.356 = bf16[8,192,1152]{2,1,0:T(8,128)(2,1)S(1)} custom-call(bf16[192,1152]{1,0:T(8,128)(2,1)S(1)} %copy-done.10), custom_call_target="tpu_custom_call" | custom-call | tf_op jit(solution)/shard_map/pallas_call | solution.py:313
  49.1 1.6 copy.158
  50.7 2.4 bitcast_bitcast_fusion.b_ref
  53.1 3.2 convert_element_type.151
  56.3 3.6 copy.192
  59.9 3.8 reshape.139.a_ref
  63.7 2.0 copy.185
  68.9 2.1 copy-done
  72.5 5.2 shard_map.357
  77.7 1.9 copy-done.17
  79.7 29.7 %shard_map.358 = (bf16[1280,384]{1,0:T(8,128)(2,1)S(1)}, f32[1280,128]{1,0:T(8,128)S(1)}, bf16[2,1024,256]{2,1,0:T(8,128)(2,1)S(1)}) custom-call(bf16[1280,384]{1,0:T(8,128)(2,1)S(1)} %get-tuple-element.44.q_ref, bf16[1280,256]{1,0:T(8,128)(2,1)S(1)} %get-tuple-element.45.kv_ref), custom_call_target="tpu_custom_call" | custom-call | flops 12079595520 | bytes 3932160 | tf_op jit(solution)/shard_map/pallas_call | solution.py:913
  112.1 2.2 convolution_convert_fusion.2.x_ref
  114.4 118.8 %shard_map.359 = (bf16[1280,1536]{1,0:T(8,128)(2,1)S(1)}, bf16[8,192,4096]{2,1,0:T(8,128)(2,1)S(1)}, bf16[8,192,2048]{2,1,0:T(8,128)(2,1)S(1)}) custom-call(bf16[1280,1536]{1,0:T(8,128)(2,1)S(1)} %convolution_convert_fusion.2.x_ref, bf16[192,4096]{1,0:T(8,128)(2,1)S(1)} %copy-done.7, bf16[192,2048]{1,0:T(8,128)(2,1)S(1)} %copy-done.8), custom_call_target="tpu_custom_call" | custom-call | flops 1966080 | bytes 196608000 | tf_op jit(solution)/shard_map/pallas_call | solution.py:354
  233.2 4.6 copy-done.13
  237.7 2.7 copy-done.14
  242.5 1.8 multiply_convert_fusion.rows_ref
  244.3 1.8 select_reduce_fusion
  246.1 1.9 copy-done.5
  248.0 2.0 copy.157
  249.9 1.6 fusion.15
  254.0 2.1 copy-done.6
  256.1 41.3 %shard_map.360 = (bf16[1280,2048]{1,0:T(8,128)(2,1)}, bf16[1280,4096]{1,0:T(8,128)(2,1)}, f32[1280,128]{1,0:T(8,128)S(1)}) custom-call(bf16[1280,1536]{1,0:T(8,128)(2,1)S(1)} %copy-done.6, bf16[1280,1536]{1,0:T(8,128)(2,1)} %outgrad_ref.3, f32[1280,128]{1,0:T(8,128)S(1)} %pad.18.gates_ref, bf16[1536,4096]{1,0:T(8,128)(2,1)} %bitcast.69, ...), custom_call_target="tpu_custom_call" | custom-call | flops 24159191040 | bytes 34603008 | tf_op jit(solution)/shard_map/pallas_call | solution.py:695
  297.4 22.2 %convolution_convert_fusion.1 = bf16[1280,1536]{1,0:T(8,128)(2,1)S(1)} fusion(bf16[1280,4096]{1,0:T(8,128)(2,1)} %get-tuple-element.50.hidden_ref, bf16[1536,4096]{1,0:T(8,128)(2,1)} %bitcast.70), kind=kOutput, calls=%fused_computation.9 | convolution fusion | flops 16108093440 | bytes 27000832 | tf_op jit(solution)/shard_map/dot_general | solution.py:1272
  319.7 2.3 pad_maximum_fusion.x_ref
  322.0 121.6 %shard_map.361 = (bf16[1280,1664]{1,0:T(8,128)(2,1)}, bf16[1536,4096]{1,0:T(8,128)(2,1)}, bf16[1536,2048]{1,0:T(8,128)(2,1)}, bf16[1280,1536]{1,0:T(8,128)(2,1)}) custom-call(bf16[1280,1664]{1,0:T(8,128)(2,1)} %pad_maximum_fusion.x_ref, bf16[1280,1536]{1,0:T(8,128)(2,1)} %copy-done.5, bf16[1280,1536]{1,0:T(8,128)(2,1)} %outgrad_ref.3, ...), custom_call_target="tpu_custom_call" | custom-call | flops 32212254720 | bytes 19660800 | tf_op jit(solution)/shard_map/pallas_call | solution.py:612
  446.7 7.6 %multiply_reduce_fusion = (f32[1536]{0:T(1024)}, f32[1280]{0:T(1024)S(1)}, f32[1280,1536]{1,0:T(8,128)S(1)}) fusion(bf16[1280,1536]{1,0:T(8,128)(2,1)} %copy-done.3, bf16[1280,1536]{1,0:T(8,128)(2,1)} %tokens_ref.1, f32[1280]{0:T(1024)S(1)} %copy-done.43, f32[1536]{0:T(1024)S(1)} %get-tuple-element.176, bf16[1280,16]{1,0:T(8,128)(2,1)S(1)} %fusion.11, ...), kind=kOutput, calls=%fused_computation.2 | convolution fusion | flops 84538624 | bytes 20409344 | tf_op jit(solution)/shard_map/dot_general | solution.py:1290
  455.3 4.8 multiply_add_fusion.middle_ref
  466.0 1.9 copy.159
  469.3 1.8 pad_maximum_fusion.8.row_sin_ref
  471.1 1.7 pad_maximum_fusion.7.row_cos_ref
  472.8 3.5 convolution_convert_fusion.6
  476.3 6.1 convolution_convert_fusion.4
  482.4 3.1 convolution_convert_fusion.5.do_ref
  485.6 43.5 %shard_map.362 = bf16[1280,640]{1,0:T(8,128)(2,1)} custom-call(bf16[1280,384]{1,0:T(8,128)(2,1)} %copy-done.19, bf16[1280,256]{1,0:T(8,128)(2,1)} %copy-done.20, bf16[2,1024,256]{2,1,0:T(8,128)(2,1)} %copy-done.21, bf16[1280,384]{1,0:T(8,128)(2,1)} %convolution_convert_fusion.5.do_ref, bf16[1280,384]{1,0:T(8,128)(2,1)} %copy-done.15, f32[2,8,640]{2,1,0:T(8,128)} %bitcast.91, ...), custom_call_target="tpu_custom_call" | custom-call | flops 30198988800 | bytes 5898240 | tf_op jit(solution)/shard_map/pallas_call | solution.py:1063
  529.2 4.3 convolution_convert_fusion.3
  533.5 1.9 pad_maximum_fusion.1
  535.4 6.0 copy.160
  541.4 6.6 convolution_convert_fusion.x_ref
  548.1 144.1 %shard_map.363 = (f32[1280,1536]{1,0:T(8,128)}, f32[192,1152]{1,0:T(8,128)}, f32[16,256]{1,0:T(8,128)}) custom-call(bf16[1280,1536]{1,0:T(8,128)(2,1)} %convolution_convert_fusion.x_ref, bf16[1280,1536]{1,0:T(8,128)(2,1)} %tokens_ref.1, f32[1280,1536]{1,0:T(8,128)} %multiply_add_fusion.middle_ref, f32[8,1536]{1,0:T(8,128)} %copy-done.12, ...), custom_call_target="tpu_custom_call" | custom-call | flops 1966080 | bytes 1048576 | tf_op jit(solution)/shard_map/pallas_call | solution.py:509
  699.8 2.2 multiply_subtract_fusion.3
  702.0 4.5 multiply_subtract_fusion.2
  706.6 8.1 %add_convert_fusion = bf16[1280,1536]{1,0:T(8,128)(2,1)} fusion(bf16[1280,1536]{1,0:T(8,128)(2,1)} %all-reduce.6.cloned.1.call-done, bf16[1280,1536]{1,0:T(8,128)(2,1)} %copy-done.3, bf16[1280,1536]{1,0:T(8,128)(2,1)} %tokens_ref.1), kind=kLoop, calls=%fused_computation.1 | loop fusion | flops 11796480 | bytes 15728640 | tf_op jit(solution)/shard_map/convert_element_type | solution.py:1368
  714.6 4.6 multiply_subtract_fusion.1
  719.3 4.2 reshape.150
  723.5 1.6 copy.168
  726.3 14.1 %multiply_subtract_fusion = (f32[16,192,2,128]{3,2,1,0:T(2,128)}, f32[16,192,2,128]{3,2,1,0:T(2,128)}, f32[16,192,2,128]{3,2,1,0:T(2,128)}) fusion(f32[16,192,2,128]{3,2,1,0:T(2,128)S(1)} %copy-done.22, f32[8,2,192,2,128]{4,3,2,1,0:T(2,128)S(1)} %copy.168, f32[16,192,2,128]{3,2,1,0:T(2,128)S(1)} %copy-done.26, f32[16,192,2,128]{3,2,1,0:T(2,128)} %param.32), kind=kLoop, calls=%fused_computation.19 | loop fusion | flops 11796480 | bytes 22020096 | tf_op jit(solution)/shard_map/sub | solution.py:56
  740.4 3.2 copy.195
  (180 shorter events, 44.4 us)
Async XLA Ops:
  8.0 698.5 %all-reduce.6.cloned.1.call-start = ((), (), s32[]{:S(2)}) async-start(), calls=%async_computation.2 | async-start | bytes 7864320 | tf_op jit(solution)/shard_map/psum | solution.py:1279
  9.5 7.1 copy-start.47
  9.5 7.1 copy-start.44
  9.7 7.9 %copy-start.31 = (f32[2,192,192]{2,1,0:T(8,128)S(1)}, f32[2,192,192]{2,1,0:T(8,128)}, u32[]{:S(2)}) copy-start(f32[2,192,192]{2,1,0:T(8,128)} %param.27) | copy-start | bytes 884740
  13.9 4.6 copy-start.28
  13.9 4.6 copy-start.29
  20.4 28.0 %copy-start.46 = (s32[1280,8]{0,1:T(8,128)S(1)}, s32[1280,8]{0,1:T(8,128)}, u32[]{:S(2)}) copy-start(s32[1280,8]{0,1:T(8,128)} %param.23) | copy-start | bytes 122884
  68.8 2.1 copy-start
  72.5 5.2 copy-start.12
  77.7 1.9 copy-start.17
  79.7 29.7 %copy-start.19 = (bf16[1280,384]{1,0:T(8,128)(2,1)}, bf16[1280,384]{1,0:T(8,128)(2,1)S(1)}, u32[]{:S(2)}) copy-start(bf16[1280,384]{1,0:T(8,128)(2,1)S(1)} %get-tuple-element.44.q_ref) | copy-start | bytes 2949124
  79.7 29.7 %copy-start.20 = (bf16[1280,256]{1,0:T(8,128)(2,1)}, bf16[1280,256]{1,0:T(8,128)(2,1)S(1)}, u32[]{:S(2)}) copy-start(bf16[1280,256]{1,0:T(8,128)(2,1)S(1)} %get-tuple-element.45.kv_ref) | copy-start | bytes 1966084
  112.1 2.2 copy-start.7
  112.1 2.3 copy-start.8
  114.4 126.1 %copy-start.1 = (bf16[1280,1536]{1,0:T(8,128)(2,1)S(1)}, bf16[1280,1536]{1,0:T(8,128)(2,1)}, u32[]{:S(2)}) copy-start(bf16[1280,1536]{1,0:T(8,128)(2,1)} %tokens_ref.1) | copy-start | bytes 11796484
  233.2 4.6 copy-start.13
  237.7 2.7 copy-start.14
  240.4 2.0 copy-start.3
  254.0 2.1 copy-start.6
  443.7 2.9 copy-start.43
  443.7 270.9 %reduce-scatter.5.cloned.1.call-start = ((), (), s32[]{:S(2)}) async-start(), calls=%async_computation.4 | async-start | bytes 7077888 | tf_op jit(solution)/shard_map/reduce_scatter | solution.py:1301
  446.6 7.7 %copy-start.40 = (bf16[1280,16]{1,0:T(8,128)(2,1)}, bf16[1280,16]{1,0:T(8,128)(2,1)S(1)}, u32[]{:S(2)}) copy-start(bf16[1280,16]{1,0:T(8,128)(2,1)S(1)} %fusion.11) | copy-start | bytes 122884
  446.6 7.6 %copy-start.2 = (bf16[1280,1536]{1,0:T(8,128)(2,1)S(1)}, bf16[1280,1536]{1,0:T(8,128)(2,1)}, u32[]{:S(2)}) copy-start(bf16[1280,1536]{1,0:T(8,128)(2,1)} %tokens_ref.1) | copy-start | bytes 11796484
  446.6 7.6 %copy-start.4 = (bf16[1280,1536]{1,0:T(8,128)(2,1)S(1)}, bf16[1280,1536]{1,0:T(8,128)(2,1)}, u32[]{:S(2)}) copy-start(bf16[1280,1536]{1,0:T(8,128)(2,1)} %copy-done.3) | copy-start | bytes 11796484
  446.6 8.7 %copy-start.25 = (bf16[1280,1536]{1,0:T(8,128)(2,1)S(1)}, bf16[1280,1536]{1,0:T(8,128)(2,1)}, u32[]{:S(2)}) copy-start(bf16[1280,1536]{1,0:T(8,128)(2,1)} %outgrad_ref.3) | copy-start | bytes 11796484
  460.2 259.1 %reduce-scatter.3.cloned.1.call-start = ((), (), s32[]{:S(2)}) async-start(), calls=%async_computation.3 | async-start | bytes 14155776 | tf_op jit(solution)/shard_map/reduce_scatter | solution.py:1302
  468.7 7.6 %copy-start.16 = (bf16[1280,384]{1,0:T(8,128)(2,1)S(1)}, bf16[1280,384]{1,0:T(8,128)(2,1)}, u32[]{:S(2)}) copy-start(bf16[1280,384]{1,0:T(8,128)(2,1)} %copy-done.15) | copy-start | bytes 2949124
  472.8 9.6 %slice-start = ((s8[7864320]{0:T(1024)(128)(4,1)}), s8[4194304]{0:T(1024)(128)(4,1)S(1)}, s32[]{:S(2)}) async-start(s8[7864320]{0:T(1024)(128)(4,1)} %bitcast.73), calls=%async_computation.5 | async-start | bytes 8388608
  476.3 6.1 slice-start.1
  485.6 43.6 %copy-start.18 = (bf16[1280,1536]{1,0:T(8,128)(2,1)S(1)}, bf16[1280,1536]{1,0:T(8,128)(2,1)}, u32[]{:S(2)}) copy-start(bf16[1280,1536]{1,0:T(8,128)(2,1)} %copy-done.17) | copy-start | bytes 11796484
  529.2 4.3 copy-start.33
  548.0 144.2 %copy-start.35 = (f32[192,16]{1,0:T(8,128)S(1)}, f32[192,16]{1,0:T(8,128)}, u32[]{:S(2)}) copy-start(f32[192,16]{1,0:T(8,128)} %copy.176) | copy-start | bytes 36868
  548.0 144.2 %copy-start.36 = (f32[192,16]{1,0:T(8,128)S(1)}, f32[192,16]{1,0:T(8,128)}, u32[]{:S(2)}) copy-start(f32[192,16]{1,0:T(8,128)} %copy.175) | copy-start | bytes 36868
  548.0 144.2 %copy-start.37 = (f32[192,16]{1,0:T(8,128)S(1)}, f32[192,16]{1,0:T(8,128)}, u32[]{:S(2)}) copy-start(f32[192,16]{1,0:T(8,128)} %copy.174) | copy-start | bytes 36868
  548.0 144.2 %copy-start.38 = (f32[192,16]{1,0:T(8,128)S(1)}, f32[192,16]{1,0:T(8,128)}, u32[]{:S(2)}) copy-start(f32[192,16]{1,0:T(8,128)} %copy.173) | copy-start | bytes 36868
  692.2 7.0 copy-start.49
  692.2 7.0 copy-start.48
  692.2 7.0 copy-start.50
  692.2 7.0 copy-start.51
  692.2 7.6 %copy-start.32 = (f32[2,192,192]{2,1,0:T(8,128)S(1)}, f32[2,192,192]{2,1,0:T(8,128)}, u32[]{:S(2)}) copy-start(f32[2,192,192]{2,1,0:T(8,128)} %param.27) | copy-start | bytes 884740
  692.3 7.6 %copy-start.39 = (f32[2,192,192]{2,1,0:T(8,128)S(1)}, f32[2,192,192]{2,1,0:T(8,128)}, u32[]{:S(2)}) copy-start(f32[2,192,192]{2,1,0:T(8,128)} %param.28) | copy-start | bytes 884740
  692.3 9.7 %copy-start.27 = (f32[192,2,320]{2,1,0:T(2,128)S(1)}, f32[192,2,320]{2,1,0:T(2,128)}, u32[]{:S(2)}) copy-start(f32[192,2,320]{2,1,0:T(2,128)} %param.24) | copy-start | bytes 1474564
  692.3 9.7 %copy-start.34 = (f32[192,2,320]{2,1,0:T(2,128)S(1)}, f32[192,2,320]{2,1,0:T(2,128)}, u32[]{:S(2)}) copy-start(f32[192,2,320]{2,1,0:T(2,128)} %param.25) | copy-start | bytes 1474564
  706.5 8.1 %copy-start.24 = (f32[16,128,192]{1,2,0:T(8,128)S(1)}, f32[16,128,192]{1,2,0:T(8,128)}, u32[]{:S(2)}) copy-start(f32[16,128,192]{1,2,0:T(8,128)} %param.33) | copy-start | bytes 4718596
  706.5 8.1 %copy-start.30 = (f32[16,128,192]{1,2,0:T(8,128)S(1)}, f32[16,128,192]{1,2,0:T(8,128)}, u32[]{:S(2)}) copy-start(f32[16,128,192]{1,2,0:T(8,128)} %param.34) | copy-start | bytes 4718596
  723.5 2.8 copy-start.26
  723.5 16.9 %slice-start.2 = ((s8[7864320]{0:T(1024)(128)(4,1)}), s8[4194304]{0:T(1024)(128)(4,1)S(1)}, s32[]{:S(2)}) async-start(s8[7864320]{0:T(1024)(128)(4,1)} %bitcast.77), calls=%async_computation.7 | async-start | bytes 8388608
  726.3 14.1 %slice-start.3 = ((s8[7864320]{0:T(1024)(128)(4,1)}), s8[3670016]{0:T(1024)(128)(4,1)S(1)}, s32[]{:S(2)}) async-start(s8[7864320]{0:T(1024)(128)(4,1)} %bitcast.77), calls=%async_computation.8 | async-start | bytes 7340032
  (11 other events, 13.2 us)
Sparse Core Ops, SparseCore 0:
  443.8 171.4 all-reduce.5
Sparse Core Ops, SparseCore 1:
  460.2 63.1 reduce-scatter.4
  527.2 129.0 reduce-scatter.2

commit v5 on v4

--- a/solution.py
+++ b/solution.py
@@ -2,6 +2,7 @@
 
 import jax
 import jax.numpy as jnp
+import numpy as np
 from jax import lax
 from jax.experimental import pallas as pl
 from jax.experimental.pallas import tpu as pltpu
@@ -30,13 +31,6 @@
 nt = (((1,), (1,)), ((), ()))
 
 
-def angles_for(positions, head_size):
-    half_dim = head_size // 2
-    freqs = 10000.0 ** (-2.0 * jnp.arange(half_dim, dtype=f32) / head_size)
-    angles = positions.astype(f32)[..., None] * freqs
-    return (jnp.cos(angles), jnp.sin(angles))
-
-
 def rotate(values, cosine, sine):
     half_dim = values.shape[-1] // 2
     first_half = values[..., :half_dim]
@@ -299,28 +293,81 @@
     ]
 
 
-def gather_kernel(n, x_ref, out_ref, *scratch):
-    greet, start, forward, finish = gather_engine(n, [(x_ref, out_ref)], *scratch)
+def gateup_column(e, part, group, hidden):
+    return (e // group * 2 * group + part * group + e % group) * hidden
+
+
+def gather_kernel(n, group, count, *refs):
+    x_refs, refs = refs[:count], refs[count:]
+    w_ref, refs = (None, refs) if group is None else (refs[0], refs[1:])
+    out_refs, refs = refs[:count], refs[count:]
+    low_ref, scratch = (None, refs) if group is None else (refs[0], refs[1:])
+    greet, start, forward, finish = gather_engine(n, list(zip(x_refs, out_refs)), *scratch)
     pl.semaphore_wait(pltpu.get_barrier_semaphore(), greet())
     start()
+    if group is not None:
+        depth, hidden = low_ref.shape[0], w_ref.shape[1]
+        for e in range(EXPERTS):
+            for part in (0, 1):
+                at = gateup_column(e, part, group, hidden)
+                low_ref[:, at : at + hidden] = w_ref[
+                    pl.ds(e * 2 * depth + part, depth, stride=2)
+                ].astype(bf16)
     for p in range(gather_parts):
         forward(p)
     finish()
 
 
-def gather(x, n, barrier_id):
-    depth, width = x.shape
+def gather(arrays, w, n, group, barrier_id):
+    depth = arrays[0].shape[0]
+    whole = pl.BlockSpec(memory_space=pltpu.VMEM)
+    shapes = [jax.ShapeDtypeStruct((n,) + x.shape, x.dtype) for x in arrays]
+    operands = list(arrays)
+    if group is not None:
+        operands.append(w)
+        shapes.append(jax.ShapeDtypeStruct((depth, w.size // depth), bf16))
     out = pl.pallas_call(
-        functools.partial(gather_kernel, n),
-        out_shape=jax.ShapeDtypeStruct((n, depth, width), x.dtype),
-        in_specs=[pl.BlockSpec(memory_space=pltpu.VMEM)],
-        out_specs=pl.BlockSpec(memory_space=pltpu.VMEM),
-        scratch_shapes=gather_scratch(1, n),
+        functools.partial(gather_kernel, n, group, len(arrays)),
+        out_shape=shapes,
+        in_specs=[whole] * len(operands),
+        out_specs=[whole] * len(shapes),
+        scratch_shapes=gather_scratch(len(arrays), n),
         compiler_params=pltpu.CompilerParams(
-            collective_id=barrier_id, has_side_effects=True, vmem_limit_bytes=16 * 2**20
-        ),
-    )(x)
-    return out.reshape(n * depth, width)
+            collective_id=barrier_id, has_side_effects=True, vmem_limit_bytes=24 * 2**20
+        ),
+    )(*operands)
+    count = len(arrays)
+    return [t.reshape(n * depth, -1) for t in out[:count]] + list(out[count:])
+
+
+def gateup_adam_kernel(group, w_ref, m_ref, v_ref, grad_ref, w_out, m_out, v_out, g_ref):
+    depth, hidden = grad_ref.shape[0], w_ref.shape[1]
+    for e in range(w_ref.shape[0] // (2 * depth)):
+        for part in (0, 1):
+            at = gateup_column(e, part, group, hidden)
+            g_ref[pl.ds(part, depth, stride=2)] = grad_ref[:, at : at + hidden].astype(f32)
+        rows = slice(e * 2 * depth, (e + 1) * 2 * depth)
+        w_out[rows], m_out[rows], v_out[rows] = adam_update(
+            w_ref[rows], m_ref[rows], v_ref[rows], g_ref[...], weight_decay, 0.05
+        )
+
+
+def gateup_adam(w, m, v, grad, group):
+    experts, depth, parts, hidden = w.shape
+    flat = lambda t: t.reshape(experts * depth * parts, hidden)
+    each = 2 * group
+    block = pl.BlockSpec((each * depth * parts, hidden), lambda e: (e, 0))
+    out = pl.pallas_call(
+        functools.partial(gateup_adam_kernel, group),
+        grid=(experts // each,),
+        in_specs=[block] * 3
+        + [pl.BlockSpec((depth, each * parts * hidden), lambda e: (0, e))],
+        out_specs=[block] * 3,
+        out_shape=[jax.ShapeDtypeStruct((experts * depth * parts, hidden), f32)] * 3,
+        scratch_shapes=[pltpu.VMEM((depth * parts, hidden), f32)],
+        compiler_params=pltpu.CompilerParams(vmem_limit_bytes=32 * 2**20),
+    )(flat(w), flat(m), flat(v), grad)
+    return tuple(t.reshape(w.shape) for t in out)
 
 
 def line_gather_kernel(n, n_dp, x_ref, a_ref, b_ref, o_ref, a_out, b_out, *scratch):
@@ -369,7 +416,16 @@
 
 
 def last_kernel(
-    n, n_dp, x_ref, tokens_ref, middle_ref, gain_ref, weights_ref, gain_second_ref,
+    n, n_dp, pieces, x_ref, tokens_ref, middle_ref, gain_ref, gain_second_ref, *refs,
+):
+    weights_refs, refs = refs[:pieces], refs[pieces:]
+    last_body(
+        n, n_dp, x_ref, tokens_ref, middle_ref, gain_ref, weights_refs, gain_second_ref, *refs
+    )
+
+
+def last_body(
+    n, n_dp, x_ref, tokens_ref, middle_ref, gain_ref, weights_refs, gain_second_ref,
     grad_ref, weights_out, gains_out, o_ref, held, send_red, recv_red, send_out, recv_out,
     tokens_v, middle_v, grad_v, in_sem, out_sem, got, w_send, w_recv,
     g_from, g_got, g_send, g_recv, z_from, z_got, z_send, z_recv, acc,
@@ -386,7 +442,7 @@
 
     def complete(at):
         norm, inverse = norm_of(at)
-        grad = o_ref[at].astype(f32) * gain_ref[0:1]
+        grad = o_ref[at].astype(f32) * (gain_ref[0:1] + gain_ref[2:3])
         mean = jnp.mean(grad * norm, axis=-1, keepdims=True)
         grad_v[at] = middle_v[at] + inverse * (grad - norm * mean)
 
@@ -394,11 +450,17 @@
         n, x_ref, o_ref, held, send_red, recv_red, send_out, recv_out, complete
     )
 
-    def weights_copy(k):
+    columns, low = [], 0
+    for ref in weights_refs:
+        columns.append(slice(low, low + ref.shape[2]))
+        low += ref.shape[2]
+    pieces = range(len(columns))
+
+    def weights_copy(k, j):
         to = lax.rem(me + k, n_dp)
         return pltpu.make_async_remote_copy(
-            src_ref=weights_ref.at[to], dst_ref=got.at[k],
-            send_sem=w_send.at[k], recv_sem=w_recv.at[k],
+            src_ref=weights_refs[j].at[to], dst_ref=got.at[k, :, columns[j]],
+            send_sem=w_send.at[j, k], recv_sem=w_recv.at[j, k],
             device_id={"dp": to}, device_id_type=MESH,
         )
 
@@ -442,7 +504,8 @@
     greet("dp", me, n_dp)
     greet("tensor", line, n)
     pl.semaphore_wait(barrier, n_dp + n - 2)
-    loop(n_dp, lambda k: weights_copy(k).start())
+    for j in pieces:
+        loop(n_dp, lambda k: weights_copy(k, j).start())
     acc[...] = jnp.zeros_like(acc)
     load_tokens.wait()
     load_middle.wait()
@@ -466,22 +529,30 @@
     for p in range(n_dp):
         moved = acc[...] if p == 0 else pltpu.roll(acc[...], model - p * depth, 1)
         g_from[p, :8] = moved[:, :width]
-        g_from[p, 8:] = gain_second_ref[p]
+        moved = gain_second_ref[...] if p == 0 else pltpu.roll(
+            gain_second_ref[...], model - p * depth, 1
+        )
+        g_from[p, 8:] = jnp.where(line == 0, moved[:, :width], 0.0)
     loop(n_dp, lambda k: gains_copy(k).start())
     late = min(line_parts + 4, total)
     lax.fori_loop(line_parts, late, step, 0)
     loop(n_dp, lambda k: gains_copy(k).wait_recv())
     z_from[...] = lax.fori_loop(1, n_dp, lambda k, t: t + g_got[k], g_from[me])
     loop(n, lambda k: line_copy(k).start())
-    loop(n_dp, lambda k: weights_copy(k).wait_recv())
+    for j in pieces:
+        loop(n_dp, lambda k: weights_copy(k, j).wait_recv())
     lax.fori_loop(late, total, step, 0)
     size = 32
 
     def add(b, carry):
         at = pl.ds(pl.multiple_of(b * size, 16), size)
-        weights_out[at] = lax.fori_loop(
-            1, n_dp, lambda k, t: t + got[k, at].astype(f32), weights_ref[me, at].astype(f32)
-        )
+        for j, ref in enumerate(weights_refs):
+            weights_out[at, columns[j]] = lax.fori_loop(
+                1,
+                n_dp,
+                lambda k, t: t + got[k, at, columns[j]].astype(f32),
+                ref[me, at].astype(f32),
+            )
         return carry
 
     every = pltpu.make_async_copy(grad_v, grad_ref, out_sem)
@@ -490,7 +561,8 @@
     loop(n, lambda k: line_copy(k).wait_recv())
     gains_out[...] = lax.fori_loop(1, n, lambda k, t: t + z_got[k], z_from[...])
     finish()
-    loop(n_dp, lambda k: weights_copy(k).wait_send())
+    for j in pieces:
+        loop(n_dp, lambda k: weights_copy(k, j).wait_send())
     loop(n_dp, lambda k: gains_copy(k).wait_send())
     loop(n, lambda k: line_copy(k).wait_send())
     every.wait()
@@ -498,22 +570,18 @@
 
 def last_call(x, tokens, middle, gain, weights, gain_second, n, n_dp, barrier_id):
     count, model = x.shape
-    depth, width = model // n_dp, weights.shape[1]
+    depth, width = model // n_dp, sum(w.shape[1] for w in weights)
     lanes = -(-depth // 128) * 128
-    gain_second = jnp.where(lax.axis_index("tensor") == 0, gain_second, 0.0)
-    gain_second = jnp.pad(
-        gain_second.reshape(n_dp, 1, depth), ((0, 0), (0, 7), (0, lanes - depth))
-    )
     whole, anywhere = pl.BlockSpec(memory_space=pltpu.VMEM), pl.BlockSpec(memory_space=pl.ANY)
     dma = pltpu.SemaphoreType.DMA
     grad, weights, gains = pl.pallas_call(
-        functools.partial(last_kernel, n, n_dp),
+        functools.partial(last_kernel, n, n_dp, len(weights)),
         out_shape=[
             jax.ShapeDtypeStruct((count, model), f32),
             jax.ShapeDtypeStruct((depth, width), f32),
             jax.ShapeDtypeStruct((16, lanes), f32),
         ],
-        in_specs=[whole, anywhere, anywhere, whole, whole, whole],
+        in_specs=[whole, anywhere, anywhere, whole, whole] + [whole] * len(weights),
         out_specs=[anywhere, whole, whole],
         scratch_shapes=[pltpu.VMEM(x.shape, bf16)]
         + line_scratch(x.shape, x.dtype)
@@ -524,8 +592,8 @@
             dma((2,)),
             dma,
             pltpu.VMEM((n_dp, depth, width), bf16),
-            dma((n_dp,)),
-            dma((n_dp,)),
+            dma((len(weights), n_dp)),
+            dma((len(weights), n_dp)),
             pltpu.VMEM((n_dp, 16, lanes), f32),
             pltpu.VMEM((n_dp, 16, lanes), f32),
             dma((n_dp,)),
@@ -542,13 +610,14 @@
         cost_estimate=pl.CostEstimate(
             flops=count * model, bytes_accessed=2**20, transcendentals=0
         ),
-    )(x, tokens, middle, gain, weights.reshape(n_dp, depth, width), gain_second)
-    gains = jnp.stack([jnp.sum(gains[:8, :depth], axis=0), gains[8, :depth]])
+    )(x, tokens, middle, gain, gain_second, *(w.reshape(n_dp, depth, -1) for w in weights))
+    gains = jnp.sum(gains.reshape(2, 8, lanes), axis=1)[:, :depth]
     return grad, weights, gains
 
 
 def expert_grads_kernel(
-    n, shape, x_ref, rows_ref, outgrad_ref, down_ref, hidden_ref, active_ref, active_rows_ref,
+    n, shape, x_ref, rows_ref, outgrad_ref, start_ref, rest_ref,
+    hidden_ref, active_ref, active_rows_ref,
     o_ref, gateup_grad_ref, down_grad_ref, mixture_ref, rows_t, outgrad_t, o_sem, sum_ref, *scratch,
 ):
     mixture_steps, gateup_steps, down_steps = shape
@@ -571,8 +640,14 @@
 
     @pl.when(i < mixture_steps)
     def _():
-        mixture_ref[...] = lax.dot_general(
-            active_rows_ref[...], down_ref[...], nt, preferred_element_type=f32
+        half = start_ref.shape[1]
+        mixture_ref[...] = (
+            lax.dot_general(
+                active_rows_ref[:, :half], start_ref[...], nt, preferred_element_type=f32
+            )
+            + lax.dot_general(
+                active_rows_ref[:, half:], rest_ref[...], nt, preferred_element_type=f32
+            )
         ).astype(bf16)
         size = active_rows_ref.shape[0]
         columns = pl.ds(pl.multiple_of(i * size, size), size)
@@ -601,7 +676,9 @@
         copy.wait()
 
 
-def expert_grads_call(x, rows, outgrad, down, hidden, active, n, barrier_id):
+def expert_grads_call(
+    x, rows, outgrad, down_start, down_rest, hidden, active, n, barrier_id
+):
     tokens, model = rows.shape
     block, tile = min(512, active.shape[1]), 256
     c, a, b = shape = (tokens // tile, hidden.shape[1] // block, active.shape[1] // block)
@@ -616,6 +693,7 @@
             whole,
             pl.BlockSpec((tile, model), first),
             pl.BlockSpec((tile, model), first),
+            whole,
             whole,
             pl.BlockSpec((tokens, block), second),
             pl.BlockSpec((tokens, block), third),
@@ -644,11 +722,11 @@
             bytes_accessed=10 * tokens * model,
             transcendentals=0,
         ),
-    )(x, rows, outgrad, down, hidden, active, active)
-
-
-def expert_kernel(group, rows_ref, outgrad_ref, gates_ref, gu_ref, down_ref,
-                  active_ref, hidden_ref, gate_grad_ref):
+    )(x, rows, outgrad, down_start, down_rest, hidden, active, active)
+
+
+def expert_kernel(group, steps, rows_ref, outgrad_ref, gates_ref, gu_ref, start_ref, rest_ref,
+                  active_ref, hidden_ref, gate_grad_ref, down_ref):
     step = pl.program_id(0)
     tile = 256
     width = gu_ref.shape[1] // 2
@@ -659,6 +737,14 @@
     @pl.when(step == 0)
     def _():
         gate_grad_ref[...] = jnp.zeros_like(gate_grad_ref)
+
+    @pl.when(step < steps // 2)
+    def _():
+        down_ref[...] = start_ref[...]
+
+    @pl.when(step >= steps // 2)
+    def _():
+        down_ref[...] = rest_ref[...]
 
     def one(t, carry):
         at = pl.ds(pl.multiple_of(t * tile, tile), tile)
@@ -688,19 +774,20 @@
     lax.fori_loop(0, rows_ref.shape[0] // tile, one, 0)
 
 
-def expert_call(rows, outgrad, gates, gu, down, group):
+def expert_call(rows, outgrad, gates, gu, down_start, down_rest, group):
     tokens, model = rows.shape
     width = gu.shape[1] // (EXPERTS // group)
     steps = EXPERTS // group
     return pl.pallas_call(
-        functools.partial(expert_kernel, group),
+        functools.partial(expert_kernel, group, steps),
         grid=(steps,),
         in_specs=[
             pl.BlockSpec((tokens, model), lambda p: (0, 0)),
             pl.BlockSpec((tokens, model), lambda p: (0, 0)),
             pl.BlockSpec((tokens, 128), lambda p: (0, 0)),
             pl.BlockSpec((model, width), lambda p: (0, p)),
-            pl.BlockSpec((model, width // 2), lambda p: (0, p)),
+            pl.BlockSpec((model, width // 2), lambda p: (0, jnp.minimum(p, steps // 2 - 1))),
+            pl.BlockSpec((model, width // 2), lambda p: (0, jnp.maximum(p - steps // 2, 0))),
         ],
         out_specs=[
             pl.BlockSpec((tokens, width // 2), lambda p: (0, p)),
@@ -712,13 +799,14 @@
             jax.ShapeDtypeStruct((tokens, steps * width), bf16),
             jax.ShapeDtypeStruct((tokens, 128), f32),
         ],
+        scratch_shapes=[pltpu.VMEM((model, width // 2), bf16)],
         compiler_params=pltpu.CompilerParams(vmem_limit_bytes=48 * 2**20),
         cost_estimate=pl.CostEstimate(
             flops=2 * tokens * model * steps * width * 3 // 2,
             bytes_accessed=2 * (model * steps * width * 3 // 2 + tokens * steps * width * 3 // 2),
             transcendentals=tokens * steps * width // 2,
         ),
-    )(rows, outgrad, gates, gu, down)
+    )(rows, outgrad, gates, gu, down_start, down_rest)
 
 
 def turn(u, cosine, sine):
@@ -727,49 +815,164 @@
     return u * cosine + other * sine
 
 
+def table_parts(me, prompt_total):
+    return (
+        (0, PROMPT_DEV, pl.multiple_of(me * PROMPT_DEV, PROMPT_DEV)),
+        (PROMPT_DEV, CONT, prompt_total),
+    )
+
+
 def project_kernel(x_ref, gain_ref, w_ref, cos_ref, sin_ref, normed_ref, q_ref, kv_ref):
     x = x_ref[...].astype(f32)
     inverse = lax.rsqrt(jnp.mean(x * x, axis=-1, keepdims=True) + eps_norm)
-    normed = (x * inverse * gain_ref[0:1]).astype(bf16)
+    normed = (x * inverse * (gain_ref[0:1] + gain_ref[2:3])).astype(bf16)
     normed_ref[...] = normed
     mixed = jnp.dot(normed, w_ref[...], preferred_element_type=f32)
-    cosine, sine = cos_ref[...], sin_ref[...]
-    turned = q_ref.shape[1] // 128
-    for c in range(turned):
-        q_ref[:, c * 128 : (c + 1) * 128] = turn(
-            mixed[:, c * 128 : (c + 1) * 128], cosine, sine
-        ).astype(bf16)
-    start = turned * 128
-    kv_ref[:, :128] = turn(mixed[:, start : start + 128], cosine, sine).astype(bf16)
-    kv_ref[:, 128:] = mixed[:, start + 128 :].astype(bf16)
+    block = [mixed[:, c * 128 : (c + 1) * 128] for c in range(5)]
+    low = lax.broadcasted_iota(jnp.int32, block[0].shape, 1) < HEAD_DIM
+    turned = [
+        block[0],
+        jnp.where(low, block[1], block[2]),
+        block[3],
+        jnp.where(low, pltpu.roll(block[1], HEAD_DIM, 1), pltpu.roll(block[4], HEAD_DIM, 1)),
+    ]
+    kv_ref[:, 128:] = jnp.where(low, block[2], block[4]).astype(bf16)
+    prompt_total = cos_ref.shape[0] - CONT
+    for start, rows, at in table_parts(lax.axis_index("dp"), prompt_total):
+        cosine, sine = cos_ref[pl.ds(at, rows)], sin_ref[pl.ds(at, rows)]
+        for c, u in enumerate(turned):
+            u = turn(u[start : start + rows], cosine, sine).astype(bf16)
+            if c < 3:
+                q_ref[start : start + rows, c * 128 : (c + 1) * 128] = u
+            else:
+                kv_ref[start : start + rows, :128] = u
 
 
 def project_call(tokens, gain, w, cosine, sine):
     count, model = tokens.shape
-    tile = 256
     width = w.shape[1]
-    row = lambda n: pl.BlockSpec((tile, n), lambda i: (i, 0))
+    row = lambda n: pl.BlockSpec((TOK_MB, n), lambda i: (i, 0))
+    fixed = lambda t: pl.BlockSpec(t.shape, lambda i: (0, 0))
     return pl.pallas_call(
         project_kernel,
-        grid=(count // tile,),
-        in_specs=[
-            row(model),
-            pl.BlockSpec((8, model), lambda i: (0, 0)),
-            pl.BlockSpec((model, width), lambda i: (0, 0)),
-            row(128),
-            row(128),
-        ],
+        grid=(MICRO,),
+        in_specs=[row(model), fixed(gain), fixed(w), fixed(cosine), fixed(sine)],
         out_specs=[row(model), row(width - 256), row(256)],
         out_shape=[
             jax.ShapeDtypeStruct((count, model), bf16),
             jax.ShapeDtypeStruct((count, width - 256), bf16),
             jax.ShapeDtypeStruct((count, 256), bf16),
         ],
-        compiler_params=pltpu.CompilerParams(vmem_limit_bytes=32 * 2**20),
+        compiler_params=pltpu.CompilerParams(vmem_limit_bytes=48 * 2**20),
         cost_estimate=pl.CostEstimate(
             flops=2 * count * model * width, bytes_accessed=6 * count * model, transcendentals=count
         ),
     )(tokens, gain, w, cosine, sine)
+
+
+def norm_rows(x_ref, b_ref):
+    middle = x_ref[...].astype(f32) + b_ref[...].astype(f32)
+    inverse = lax.rsqrt(jnp.mean(middle * middle, axis=-1, keepdims=True) + eps_norm)
+    return middle * inverse, inverse
+
+
+def route_kernel(x_ref, b_ref, gain_ref, router_ref, routes_ref, normed_ref, gates_ref):
+    norm, _ = norm_rows(x_ref, b_ref)
+    normed = (norm * (gain_ref[1:2] + gain_ref[3:4])).astype(bf16)
+    normed_ref[...] = normed
+    logits = jnp.dot(normed, router_ref[...], preferred_element_type=f32)
+    lane = lax.broadcasted_iota(jnp.int32, logits.shape, 1)
+    routes = routes_ref[...]
+    named = lane == routes[:, 0:1]
+    for k in range(1, TOPK):
+        named = named | (lane == routes[:, k : k + 1])
+    top = jnp.max(jnp.where(named, logits, -1e30), axis=-1, keepdims=True)
+    weights = jnp.where(named, jnp.exp(jnp.where(named, logits, top) - top), 0.0)
+    gates_ref[...] = weights / jnp.sum(weights, axis=-1, keepdims=True)
+
+
+def route_call(tokens, branch, gain, router, routes):
+    count, model = tokens.shape
+    tile = 256
+    row = lambda n: pl.BlockSpec((tile, n), lambda i: (i, 0))
+    fixed = lambda t: pl.BlockSpec(t.shape, lambda i: (0, 0))
+    return pl.pallas_call(
+        route_kernel,
+        grid=(count // tile,),
+        in_specs=[row(model), row(model), fixed(gain), fixed(router), row(TOPK)],
+        out_specs=[row(model), row(128)],
+        out_shape=[
+            jax.ShapeDtypeStruct((count, model), bf16),
+            jax.ShapeDtypeStruct((count, 128), f32),
+        ],
+        compiler_params=pltpu.CompilerParams(vmem_limit_bytes=32 * 2**20),
+    )(tokens, branch, gain, router, routes)
+
+
+def middle_back_kernel(
+    x_ref, b_ref, summed_ref, gates_ref, outgrad_ref, gain_ref, router_ref, outproj_ref,
+    middle_ref, own_ref, attended_ref, logits_ref, gain_out,
+):
+    norm, inverse = norm_rows(x_ref, b_ref)
+    model = x_ref.shape[1]
+    gates = gates_ref[...]
+    gate_grad = summed_ref[:, model:].astype(f32)
+    chosen = gates * (gate_grad - jnp.sum(gates * gate_grad, axis=-1, keepdims=True))
+    logits = chosen.astype(bf16)
+    logits_ref[...] = logits
+    grad = summed_ref[:, :model].astype(f32) + lax.dot_general(
+        logits, router_ref[...], nt, preferred_element_type=f32
+    )
+    term = (grad * norm).reshape(-1, 8, model).sum(axis=0)
+
+    @pl.when(pl.program_id(0) == 0)
+    def _():
+        gain_out[...] = jnp.zeros_like(gain_out)
+
+    gain_out[...] += term
+    grad = grad * (gain_ref[1:2] + gain_ref[3:4])
+    mean = jnp.mean(grad * norm, axis=-1, keepdims=True)
+    middle = outgrad_ref[...].astype(f32) + inverse * (grad - norm * mean)
+    middle_ref[...] = middle
+    own = middle.astype(bf16)
+    own_ref[...] = own
+    attended_ref[...] = jnp.dot(own, outproj_ref[...], preferred_element_type=f32).astype(bf16)
+
+
+def middle_back_call(tokens, branch, summed, gates, outgrad, gain, router, outproj):
+    count, model = tokens.shape
+    tile = 256
+    row = lambda n: pl.BlockSpec((tile, n), lambda i: (i, 0))
+    fixed = lambda t: pl.BlockSpec(t.shape, lambda i: (0, 0))
+    return pl.pallas_call(
+        middle_back_kernel,
+        grid=(count // tile,),
+        in_specs=[
+            row(model),
+            row(model),
+            row(model + 128),
+            row(128),
+            row(model),
+            fixed(gain),
+            fixed(router),
+            fixed(outproj),
+        ],
+        out_specs=[
+            row(model),
+            row(model),
+            row(outproj.shape[1]),
+            row(128),
+            pl.BlockSpec((8, model), lambda i: (0, 0)),
+        ],
+        out_shape=[
+            jax.ShapeDtypeStruct((count, model), f32),
+            jax.ShapeDtypeStruct((count, model), bf16),
+            jax.ShapeDtypeStruct((count, outproj.shape[1]), bf16),
+            jax.ShapeDtypeStruct((count, 128), bf16),
+            jax.ShapeDtypeStruct((8, model), f32),
+        ],
+        compiler_params=pltpu.CompilerParams(vmem_limit_bytes=48 * 2**20),
+    )(tokens, branch, summed, gates, outgrad, gain, router, outproj)
 
 
 def head_places(heads):
@@ -824,7 +1027,11 @@
     return {place: i for i, place in enumerate(keys)}
 
 
-def attention_kernel(heads, n, q_ref, kv_ref, o_ref, lse_ref, all_ref, k_ref, v_ref, send, recv):
+def attention_kernel(
+    heads, n, q_ref, kv_ref, w_ref, o_ref, lse_ref, all_ref, w_out, k_ref, v_ref, send, recv,
+    *spread_out,
+):
+    _, start_w, forward_w, finish_w = gather_engine(n, [(w_ref, w_out)], *spread_out)
     prompt_total = all_ref.shape[1]
     me = lax.axis_index("dp")
 
@@ -854,6 +1061,7 @@
 
     for m in range(MICRO):
         every(m, lambda copy: copy.start())
+    start_w()
 
     def micro(m, carry):
         every(m, lambda copy: copy.wait_recv())
@@ -897,34 +1105,39 @@
                     pair_out = out
                 else:
                     o_ref[at, pair * 128 : (pair + 1) * 128] = (pair_out + out).astype(bf16)
-            lse_ref[at] = lse
+            lse_ref[m, :, start : start + rows] = lse.T[:8]
         return carry
 
     lax.fori_loop(0, MICRO, micro, 0)
+    for p in range(gather_parts):
+        forward_w(p)
     for m in range(MICRO):
         every(m, lambda copy: copy.wait_send())
-
-
-def attention_call(q, kv, n):
+    finish_w()
+
+
+def attention_call(q, kv, w, n):
     count, width = q.shape
     keys = PROMPT_DEV * n + CONT
     heads = width // HEAD_DIM
     whole = pl.BlockSpec(memory_space=pltpu.VMEM)
     return pl.pallas_call(
         functools.partial(attention_kernel, heads, n),
-        in_specs=[whole] * 2,
-        out_specs=[whole] * 3,
+        in_specs=[whole] * 2 + [pl.BlockSpec(memory_space=pl.ANY)],
+        out_specs=[whole] * 3 + [pl.BlockSpec(memory_space=pl.ANY)],
         out_shape=[
             jax.ShapeDtypeStruct((count, width), bf16),
-            jax.ShapeDtypeStruct((count, 128), f32),
+            jax.ShapeDtypeStruct((MICRO, 8, TOK_MB), f32),
             jax.ShapeDtypeStruct((MICRO, PROMPT_DEV * n, 256), bf16),
+            jax.ShapeDtypeStruct((n,) + w.shape, w.dtype),
         ],
         scratch_shapes=[
             pltpu.VMEM((4, keys, 128), bf16),
             pltpu.VMEM((4, keys, 128), bf16),
             pltpu.SemaphoreType.DMA((MICRO, n)),
             pltpu.SemaphoreType.DMA((MICRO, n)),
-        ],
+        ]
+        + gather_scratch(1, n),
         compiler_params=pltpu.CompilerParams(
             collective_id=3, has_side_effects=True, vmem_limit_bytes=48 * 2**20
         ),
@@ -933,17 +1146,24 @@
             bytes_accessed=8 * count * width,
             transcendentals=count * keys * heads,
         ),
-    )(q, kv)
+    )(q, kv, w)
 
 
 def attention_back_kernel(
     heads, n, q_ref, kv_ref, all_ref, do_ref, o_ref, lse_ref,
-    cos_ref, sin_ref, row_cos_ref, row_sin_ref,
+    cos_ref, sin_ref,
     grad_ref, k_ref, v_ref, kt_ref, dk_ref, dv_ref, sent_ref, got_ref, send, recv,
 ):
     prompt_total = all_ref.shape[1]
     me = lax.axis_index("dp")
-    width = heads * HEAD_DIM
+
+    def put_both(at, dk, dv):
+        low = lax.broadcasted_iota(jnp.int32, dk.shape, 1) < HEAD_DIM
+        dk = pltpu.roll(dk, HEAD_DIM, 1)
+        second = grad_ref[at, 128:256].astype(f32)
+        grad_ref[at, 128:256] = jnp.where(low, second, dk).astype(bf16)
+        grad_ref[at, 256:384] = jnp.where(low, dv, second).astype(bf16)
+        grad_ref[at, 512:640] = jnp.where(low, dk, dv).astype(bf16)
 
     def piece(m, k):
         to = lax.rem(me + k, n)
@@ -1015,8 +1235,13 @@
                     term = jnp.dot(kt_ref[i, :, low:high], ds, preferred_element_type=f32)
                     back = term if back is None else back + term
                 if half == 1:
-                    grad_ref[at, lanes] = turn(
-                        back.T, row_cos_ref[inner], -row_sin_ref[inner]
+                    if start == 0:
+                        table = pl.ds(pl.multiple_of(me * PROMPT_DEV, PROMPT_DEV), rows)
+                    else:
+                        table = pl.ds(prompt_total + start - PROMPT_DEV, rows)
+                    to = (0, 1, 3)[pair] * 128
+                    grad_ref[at, to : to + 128] = turn(
+                        back.T, cos_ref[table], -sin_ref[table]
                     ).astype(bf16)
                     back = None
         lane = lax.broadcasted_iota(jnp.int32, (dk_ref.shape[1], 128), 1)
@@ -1029,14 +1254,13 @@
                 get((1, 1)) + pltpu.roll(get((1, 0)), HEAD_DIM, 1),
             )
 
-        dk = turn(joined(dk_ref) * HEAD_DIM**-0.5, cos_ref[...], -sin_ref[...]).astype(bf16)
-        dv = joined(dv_ref).astype(bf16)
-        sent_ref[m, :, :128] = dk[:prompt_total]
-        sent_ref[m, :, 128:] = dv[:prompt_total]
+        dk = turn(joined(dk_ref) * HEAD_DIM**-0.5, cos_ref[...], -sin_ref[...])
+        dv = joined(dv_ref)
+        sent_ref[m, :, :128] = dk[:prompt_total].astype(bf16)
+        sent_ref[m, :, 128:] = dv[:prompt_total].astype(bf16)
         every(m, lambda copy: copy.start())
         own = pl.ds(pl.multiple_of(m * TOK_MB + PROMPT_DEV, 128), CONT)
-        grad_ref[own, width : width + 128] = dk[prompt_total:]
-        grad_ref[own, width + 128 :] = dv[prompt_total:]
+        put_both(own, dk[prompt_total:], dv[prompt_total:])
         return carry
 
     lax.fori_loop(0, MICRO, micro, 0)
@@ -1048,21 +1272,21 @@
             1, n, lambda k, t: t + got_ref[m, k].astype(f32), own.astype(f32)
         )
         at = pl.ds(pl.multiple_of(m * TOK_MB, 128), PROMPT_DEV)
-        grad_ref[at, width:] = total.astype(bf16)
+        put_both(at, total[:, :128], total[:, 128:])
         every(m, lambda copy: copy.wait_send())
         return carry
 
     lax.fori_loop(0, MICRO, collect, 0)
 
 
-def attention_back_call(q, kv, prompts, do, o, lse, cosine, sine, row_cos, row_sin, n):
+def attention_back_call(q, kv, prompts, do, o, lse, cosine, sine, n):
     count, width = q.shape
     keys = prompts.shape[1] + CONT
     heads = width // HEAD_DIM
     whole = pl.BlockSpec(memory_space=pltpu.VMEM)
     return pl.pallas_call(
         functools.partial(attention_back_kernel, heads, n),
-        in_specs=[whole] * 10,
+        in_specs=[whole] * 8,
         out_specs=whole,
         out_shape=jax.ShapeDtypeStruct((count, width + 256), bf16),
         scratch_shapes=[
@@ -1084,7 +1308,7 @@
             bytes_accessed=12 * count * width,
             transcendentals=count * keys * heads,
         ),
-    )(q, kv, prompts, do, o, lse, cosine, sine, row_cos, row_sin)
+    )(q, kv, prompts, do, o, lse, cosine, sine)
 
 
 def attend(queries, keys_all, values_all, allowed):
@@ -1144,88 +1368,72 @@
         return w.transpose(1, 3, 0, 2, 4).reshape(EXPERTS, depth, 2, hidden)
 
     query_width = GROUP * HEAD_DIM
-
-    def inproj_flat(w):
-        w = w.reshape(depth, kv_local, query_width + 2 * HEAD_DIM)
-        parts = (w[:, :, :query_width], w[:, :, query_width:-HEAD_DIM], w[:, :, -HEAD_DIM:])
-        return jnp.concatenate([p.reshape(depth, -1) for p in parts], axis=1)
-
-    def inproj_back(w):
-        q, k, v = jnp.split(w, [kv_local * query_width, kv_local * (query_width + HEAD_DIM)], axis=1)
-        return jnp.concatenate([p.reshape(depth, kv_local, -1) for p in (q, k, v)], axis=2)
-
     gains_high = gains.astype(bf16)
     gains_low = (gains - gains_high.astype(f32)).astype(bf16)
-    attn_local = jnp.concatenate(
-        [
-            inproj_flat(inproj_weight.astype(bf16)),
-            outproj_weight.reshape(out_width, depth).T.astype(bf16),
-            jnp.concatenate(
-                [
-                    router_weight.astype(bf16),
-                    gains_high.T,
-                    gains_low.T,
-                    jnp.zeros((depth, 128 - EXPERTS - 4), bf16),
-                ],
-                axis=1,
-            ),
-        ],
-        axis=1,
-    )
-    attn_full = gather(attn_local, n_dp, 5)
-    gu_local = gateup_flat(gateup_weight.astype(bf16))
+    attn_local = (
+        inproj_weight.reshape(depth, in_width).astype(bf16),
+        outproj_weight.reshape(out_width, depth).T.astype(bf16),
+        jnp.concatenate(
+            [
+                router_weight.astype(bf16),
+                gains_high.T,
+                gains_low.T,
+                jnp.zeros((depth, 128 - EXPERTS - 4), bf16),
+            ],
+            axis=1,
+        ),
+    )
+    if hidden == 128:
+        inproj_full, outproj_full, small_full, gu_local = gather(
+            attn_local, gateup_weight.reshape(-1, hidden), n_dp, group, 5
+        )
+    else:
+        inproj_full, outproj_full, small_full = gather(attn_local, None, n_dp, None, 5)
+        gu_local = gateup_flat(gateup_weight.astype(bf16))
     down_local = down_weight.reshape(EXPERTS * hidden, depth).T.astype(bf16)
-    inproj_full = attn_full[:, :in_width]
-    outproj_full = attn_full[:, in_width : in_width + out_width]
-    small_full = attn_full[:, in_width + out_width :]
-    router_full = small_full[:, :EXPERTS]
-    small_t = small_full[:, EXPERTS : EXPERTS + 4].astype(f32).T
-    gain_first = small_t[0:1] + small_t[2:3]
-    gain_second = small_t[1:2] + small_t[3:4]
+    gain_rows = small_full[:, EXPERTS : EXPERTS + 8].astype(f32).T
 
     device_index = lax.axis_index("dp")
-    inputs = tokens.astype(f32)
-    inverse_first = lax.rsqrt(jnp.mean(inputs * inputs, axis=-1, keepdims=True) + eps_norm)
-    norm_first = inputs * inverse_first
-    cosine, sine = angles_for(jnp.arange(prompt_total + CONT), HEAD_DIM)
+    half_dim = HEAD_DIM // 2
+    freqs = np.float32(10000.0) ** (-2.0 * np.arange(half_dim, dtype=np.float32) / HEAD_DIM)
+    angles = np.arange(prompt_total + CONT, dtype=np.float32)[:, None] * freqs.astype(np.float32)
+    cosine, sine = np.cos(angles), np.sin(angles)
 
     def of_rows(table):
-        own = lax.dynamic_slice_in_dim(table, device_index * PROMPT_DEV, PROMPT_DEV, 0)
+        own = lax.dynamic_slice_in_dim(
+            jnp.asarray(table), device_index * PROMPT_DEV, PROMPT_DEV, 0
+        )
         return jnp.concatenate([own, table[prompt_total:]], axis=0)
 
     in_kernels = kv_local * HEAD_DIM == 128
-    queries_width = kv_local * query_width
     both_width = kv_local * 2 * HEAD_DIM
     if in_kernels:
-        cos_all = jnp.concatenate([cosine] * 4, axis=1)
-        sin_all = jnp.concatenate([-sine, sine] * 2, axis=1)
-        cos_row, sin_row = of_rows(cos_all), of_rows(sin_all)
+        cos_all = np.concatenate([cosine] * 4, axis=1)
+        sin_all = np.concatenate([-sine, sine] * 2, axis=1)
         normed_first, queries, both = project_call(
-            tokens,
-            jnp.pad(gain_first, ((0, 7), (0, 0))),
-            inproj_full,
-            jnp.concatenate([cos_row] * MICRO, axis=0),
-            jnp.concatenate([sin_row] * MICRO, axis=0),
+            tokens, gain_rows, inproj_full, cos_all, sin_all
         )
     else:
         cosine, sine = (jnp.tile(of_rows(t), (MICRO, 1))[:, None, :] for t in (cosine, sine))
-        normed_first = (norm_first * gain_first).astype(bf16)
+        inputs = tokens.astype(f32)
+        inverse_first = lax.rsqrt(jnp.mean(inputs * inputs, axis=-1, keepdims=True) + eps_norm)
+        normed_first = (inputs * inverse_first * (gain_rows[0:1] + gain_rows[2:3])).astype(bf16)
         mixed = jnp.dot(normed_first, inproj_full, preferred_element_type=f32)
+        mixed = mixed.reshape(count, kv_local, -1)
         queries = rotate(
-            mixed[:, :queries_width].reshape(count, -1, HEAD_DIM), cosine, sine
+            mixed[..., :query_width].reshape(count, -1, HEAD_DIM), cosine, sine
         ).astype(bf16)
-        keys = rotate(
-            mixed[:, queries_width : queries_width + kv_local * HEAD_DIM].reshape(
-                count, -1, HEAD_DIM
-            ),
-            cosine,
-            sine,
-        )
+        keys = rotate(mixed[..., query_width : query_width + HEAD_DIM], cosine, sine)
         both = jnp.concatenate(
-            [keys.reshape(count, -1), mixed[:, queries_width + kv_local * HEAD_DIM :]], axis=1
+            [keys.reshape(count, -1), mixed[..., query_width + HEAD_DIM :].reshape(count, -1)],
+            axis=1,
         ).astype(bf16)
     if in_kernels:
-        attended, lse, prompt_both = attention_call(queries, both, n_dp)
+        attended, lse, prompt_both, down_start = attention_call(
+            queries, both, down_local[:, : down_local.shape[1] // 2], n_dp
+        )
+        down_start = down_start.reshape(n_dp * depth, -1)
+        down_rest = down_local[:, down_local.shape[1] // 2 :]
     else:
         both = both.reshape(MICRO, TOK_MB, both_width)
         prompt_both = lax.all_gather(both[:, :PROMPT_DEV], "dp", axis=1, tiled=True)
@@ -1252,20 +1460,15 @@
     branch = lax.dot_general(
         attended, outproj_full, (((1,), (1,)), ((), ())), preferred_element_type=f32
     ).astype(bf16)
-    branch, gu_full, down_full = line_gather(branch, gu_local, down_local, n_tensor, n_dp, 6)
-
-    middle = inputs + branch.astype(f32)
-    inverse_second = lax.rsqrt(jnp.mean(middle * middle, axis=-1, keepdims=True) + eps_norm)
-    norm_second = middle * inverse_second
-    normed_second = (norm_second * gain_second).astype(bf16)
-    logits = jnp.dot(normed_second, router_full, preferred_element_type=f32)
-    named = jnp.any(routes[:, :, None] == jnp.arange(EXPERTS, dtype=jnp.int32), axis=1)
-    top = jnp.max(jnp.where(named, logits, -jnp.inf), axis=-1, keepdims=True)
-    weights = jnp.where(named, jnp.exp(jnp.where(named, logits, top) - top), 0.0)
-    gates = weights / jnp.sum(weights, axis=-1, keepdims=True)
-    gates_wide = jnp.pad(gates, ((0, 0), (0, 128 - EXPERTS)))
+    branch, gu_full, down_rest = line_gather(
+        branch, gu_local, down_rest if in_kernels else down_local, n_tensor, n_dp, 6
+    )
+    if not in_kernels:
+        down_start, down_rest = jnp.split(down_rest, 2, axis=1)
+
+    normed_second, gates_wide = route_call(tokens, branch, gain_rows, small_full, routes)
     active, hidden_grad, gate_grad = expert_call(
-        normed_second, cotangent, gates_wide, gu_full, down_full, group
+        normed_second, cotangent, gates_wide, gu_full, down_start, down_rest, group
     )
     contract_last = (((1,), (1,)), ((), ()))
     contract_first = (((0,), (0,)), ((), ()))
@@ -1274,42 +1477,27 @@
     ).astype(bf16)
     summed, gateup_grad, down_grad, mixture = expert_grads_call(
         jnp.concatenate([rows_grad, gate_grad.astype(bf16)], axis=1),
-        normed_second, cotangent, down_full, hidden_grad, active, n_tensor, 2,
+        normed_second, cotangent, down_start, down_rest, hidden_grad, active, n_tensor, 2,
     )
     mixture = lax.psum(mixture, "tensor")
     model = tokens.shape[1]
-    gate_grad = summed[:, model : model + EXPERTS].astype(f32)
-    outgrad = cotangent.astype(f32)
-    chosen_grad = gates * (gate_grad - jnp.sum(gates * gate_grad, axis=-1, keepdims=True))
-    logits_grad = chosen_grad.astype(bf16)
-    router_grad = lax.dot_general(
-        normed_second,
-        jnp.pad(logits_grad, ((0, 0), (0, 128 - EXPERTS))),
-        contract_first, preferred_element_type=f32
-    ).astype(bf16)
-    normed_second_grad = summed[:, :model].astype(f32) + lax.dot_general(
-        logits_grad, router_full, contract_last, preferred_element_type=f32
-    )
-    norm_second_grad = normed_second_grad * gain_second
-    gain_second_grad = jnp.sum(normed_second_grad * norm_second, axis=0)
-    middle_grad = outgrad + inverse_second * (
-        norm_second_grad
-        - norm_second * jnp.mean(norm_second_grad * norm_second, axis=-1, keepdims=True)
-    )
-
-    middle_grad, down_grad, gateup_grad = lax.optimization_barrier((middle_grad, down_grad, gateup_grad))
+    middle_grad, branch_own, attended_grad, logits_grad, gain_second_grad = middle_back_call(
+        tokens, branch, summed, gates_wide, cotangent, gain_rows, small_full, outproj_full
+    )
+    middle_grad, attended_grad, down_grad, gateup_grad = lax.optimization_barrier(
+        (middle_grad, attended_grad, down_grad, gateup_grad)
+    )
     down_grad = lax.psum_scatter(down_grad, "dp", scatter_dimension=0, tiled=True)
     gateup_grad = lax.psum_scatter(gateup_grad, "dp", scatter_dimension=0, tiled=True)
-    branch_own = middle_grad.astype(bf16)
+    router_grad = lax.dot_general(
+        normed_second, logits_grad, contract_first, preferred_element_type=f32
+    ).astype(bf16)
     outproj_grad = lax.dot_general(
         branch_own, attended, contract_first, preferred_element_type=f32
     ).astype(bf16)
-    attended_grad = jnp.dot(branch_own, outproj_full, preferred_element_type=f32).astype(bf16)
     if in_kernels:
-        lse_rows = lse[:, :8].reshape(MICRO, TOK_MB, 8).transpose(0, 2, 1)
         mixed_grad = attention_back_call(
-            queries, both, prompt_both, attended_grad, attended, lse_rows,
-            cos_all, sin_all, cos_row, sin_row, n_dp,
+            queries, both, prompt_both, attended_grad, attended, lse, cos_all, sin_all, n_dp
         )
     else:
         queries_grad, both_grad = [], []
@@ -1332,39 +1520,38 @@
         )
         mixed_grad = jnp.concatenate(
             [
-                queries_grad.reshape(count, -1),
-                keys_grad.reshape(count, -1),
-                both_grad[:, both_width // 2 :],
+                t.reshape(count, kv_local, -1)
+                for t in (queries_grad, keys_grad, both_grad[:, both_width // 2 :])
             ],
-            axis=1,
-        ).astype(bf16)
+            axis=2,
+        )
+        mixed_grad = mixed_grad.reshape(count, -1).astype(bf16)
     normed_first_grad = lax.dot_general(
         mixed_grad, inproj_full, contract_last, preferred_element_type=f32
     ).astype(bf16)
     inproj_grad = lax.dot_general(
         normed_first, mixed_grad, contract_first, preferred_element_type=f32
     ).astype(bf16)
-    attn_grad = jnp.concatenate(
-        [
-            inproj_grad,
-            outproj_grad,
-            router_grad,
-        ],
-        axis=1,
-    )
+    attn_grad = [inproj_grad, outproj_grad, router_grad]
+    if in_width % 128 or out_width % 128:
+        attn_grad = [jnp.concatenate(attn_grad, axis=1)]
     down_next = adam_update(
         down_weight, down_first, down_second,
         down_grad.T.reshape(down_weight.shape).astype(f32), weight_decay, 0.05,
     )
-    gateup_next = adam_update(
-        gateup_weight, gateup_first, gateup_second,
-        gateup_back(gateup_grad).astype(f32), weight_decay, 0.05,
-    )
+    if hidden == 128:
+        gateup_next = gateup_adam(gateup_weight, gateup_first, gateup_second, gateup_grad, group)
+    else:
+        gateup_next = adam_update(
+            gateup_weight, gateup_first, gateup_second,
+            gateup_back(gateup_grad).astype(f32), weight_decay, 0.05,
+        )
     tokens_grad, attn_grad, gains_grad = last_call(
-        normed_first_grad, tokens, middle_grad, jnp.pad(gain_first, ((0, 7), (0, 0))),
+        normed_first_grad, tokens, middle_grad, gain_rows,
         attn_grad, gain_second_grad, n_tensor, n_dp, 7,
     )
     mixture, tokens_grad = lax.optimization_barrier((mixture, tokens_grad))
+    middle = tokens.astype(f32) + branch.astype(f32)
     block_out = (middle + mixture.astype(f32)).astype(bf16)
     split = (in_width, in_width + out_width, in_width + out_width + EXPERTS)
     inproj_grad, outproj_grad, router_grad = (
@@ -1374,7 +1561,8 @@
     )
     updates = (
         adam_update(
-            inproj_weight, inproj_first, inproj_second, inproj_back(inproj_grad), weight_decay, 0.05
+            inproj_weight, inproj_first, inproj_second,
+            inproj_grad.reshape(inproj_weight.shape), weight_decay, 0.05,
         ),
         adam_update(
             outproj_weight, outproj_first, outproj_second,

time: 761 us -> 717 us (0.942)
  Pallas kernels: 530 us -> 581 us
  other arithmetic: 75.5 us -> 32.8 us
  local copies, waits for them, and re-layouts: 71.3 us -> 38.4 us
  matrix products: 57.5 us -> 42.9 us
    pallas_call x4 -> x7, Pallas kernels: 216 us -> 268 us  [the longest x1 166 us: last_call(): pl.pallas_call(functools.partial(last_kernel, n, n_dp, len(weights)), out...]
    sub x6 -> x5, other arithmetic: 27 us -> 14.1 us  [adam_update(): weight - learn_rate * (update + decay_rate * weight)]
    dot_general x4 -> x1, matrix products: 16 us -> 4.27 us  [shards(): lax.dot_general(normed_second, logits_grad, contract_first, preferred_ele...]
    concatenate x6 -> x1, other arithmetic: 8.91 us -> 0.1 us  [shards(): jnp.concatenate([router_weight.astype(bf16), gains_high.T, gains_low.T, j...]
    reshape x8 -> x1, local copies, waits for them, and re-layouts: 8.31 us -> 0.44 us  [shards(): inproj_grad.reshape(inproj_weight.shape)]
    unnamed x118 -> x83, local copies, waits for them, and re-layouts: 32.7 us -> 33.7 us
  transfers between devices with their start and end apart: 3 -> 3, of which waited for: 0 -> 0; matrix products, arithmetic and copies ran while one was open for 11% -> 7% of each run, Pallas kernels for 25% -> 32%
where the time goes in v5:
time: 717 us; the launch traced here: 712 us
  Pallas kernels  581 us (81%)
  matrix products  42.9 us (6%)
  local copies, waits for them, and re-layouts  38.4 us (5%)
  other arithmetic  32.8 us (5%)
  between operations  16.2 us (2%)
    pallas_call x1, Pallas kernels, last_call(): pl.pallas_call(functools.partial(last_kernel, n, n_dp, len(weights)), out...  166 us
    pallas_call x1, Pallas kernels, expert_grads_call(): pl.pallas_call(functools.partial(expert_grads_kernel, n, shape), grid=(a...  122 us
    pallas_call x1, Pallas kernels, line_gather(): pl.pallas_call(functools.partial(line_gather_kernel, n, n_dp), out_shape=...  112 us
    pallas_call x1, Pallas kernels, attention_back_call(): pl.pallas_call(functools.partial(attention_back_kernel, heads, n), in_spe...  44.7 us
    pallas_call x1, Pallas kernels, expert_call(): pl.pallas_call(functools.partial(expert_kernel, group, steps), grid=(step...  43.1 us
    pallas_call x1, Pallas kernels, attention_call(): pl.pallas_call(functools.partial(attention_kernel, heads, n), in_specs=[w...  34.4 us
    unnamed x83, local copies, waits for them, and re-layouts  33.7 us
    pallas_call x1, Pallas kernels, gather(): pl.pallas_call(functools.partial(gather_kernel, n, group, len(arrays)), o...  26.3 us
  transfers between devices with their start and end apart: 3, of which 0 were waited for; matrix products, arithmetic and copies ran while one was open for 7% of the time, Pallas kernels for 32%

profile of v5, /device:TPU:0, one launch (start us, length us, event | category | flops | bytes accessed | tf_op | source)
XLA Modules:
  0.0 711.9 jit_solution(17986627284281451764)
XLA Ops:
  8.1 1.4 broadcast_multiply_fusion.1
  9.6 0.8 subtract_convert_fusion
  10.7 1.3 convert_element_type.77
  12.2 1.0 convert_element_type.79
  13.6 1.9 copy-done.2
  15.4 26.3 %shard_map.374 = (bf16[8,192,640]{2,1,0:T(8,128)(2,1)S(1)}, bf16[8,192,384]{2,1,0:T(8,128)(2,1)S(1)}, bf16[8,192,128]{2,1,0:T(8,128)(2,1)S(1)}, bf16[192,4096]{1,0:T(8,128)(2,1)S(1)}) custom-call(bf16[192,640]{1,0:T(8,128)(2,1)S(1)} %convert_element_type.78.refs_0_, bf16[192,384]{1,0:T(8,128)(2,1)S(1)} %bitcast.65, ...), custom_call_target="tpu_custom_call" | custom-call | tf_op jit(solution)/shard_map/pallas_call | solution.py:329
  41.7 1.0 copy-done.7
  42.7 1.3 copy-done.15
  44.4 1.5 bitcast_bitcast_fusion
  46.2 1.5 copy-done.16
  47.8 1.1 copy-done.20
  48.9 1.1 copy-done.21
  50.0 7.9 %shard_map.375 = (bf16[1280,1536]{1,0:T(8,128)(2,1)}, bf16[1280,384]{1,0:T(8,128)(2,1)S(1)}, bf16[1280,256]{1,0:T(8,128)(2,1)S(1)}) custom-call(bf16[1280,1536]{1,0:T(8,128)(2,1)} %tokens_ref.1, f32[8,1536]{1,0:T(8,128)S(1)} %convert_bitcast_fusion.2.gain_ref, bf16[1536,640]{1,0:T(8,128)(2,1)S(1)} %bitcast.70, f32[1536,128]{1,0:T(8,128)S(1)} %copy-done.20, ...), custom_call_target="tpu_custom_call" | custom-call | flops 2516582400 | bytes 11796480 | tf_op jit(solution)/shard_map/pallas_call | solution.py:856
  58.0 34.4 %shard_map.376 = (bf16[1280,384]{1,0:T(8,128)(2,1)S(1)}, f32[2,8,640]{2,1,0:T(8,128)S(1)}, bf16[2,1024,256]{2,1,0:T(8,128)(2,1)S(1)}, bf16[8,192,1024]{2,1,0:T(8,128)(2,1)}) custom-call(bf16[1280,384]{1,0:T(8,128)(2,1)S(1)} %get-tuple-element.62.q_ref, bf16[1280,256]{1,0:T(8,128)(2,1)S(1)} %get-tuple-element.63.kv_ref, ...), custom_call_target="tpu_custom_call" | custom-call | flops 12079595520 | bytes 3932160 | tf_op jit(solution)/shard_map/pallas_call | solution.py:1124
  92.4 2.2 convolution_convert_fusion.2.x_ref
  94.7 111.6 %shard_map.377 = (bf16[1280,1536]{1,0:T(8,128)(2,1)S(1)}, bf16[8,192,4096]{2,1,0:T(8,128)(2,1)S(1)}, bf16[8,192,1024]{2,1,0:T(8,128)(2,1)S(1)}) custom-call(bf16[1280,1536]{1,0:T(8,128)(2,1)S(1)} %convolution_convert_fusion.2.x_ref, bf16[192,4096]{1,0:T(8,128)(2,1)S(1)} %get-tuple-element.66.a_ref, bf16[192,1024]{1,0:T(8,128)(2,1)S(1)} %get-tuple-element.177.b_ref), custom_call_target="tpu_custom_call" | custom-call | flops 1966080 | bytes 196608000 | tf_op jit(solution)/shard_map/pallas_call | solution.py:401
  206.3 4.6 copy-done.12
  210.9 4.7 shard_map.378
  215.6 1.8 copy-done.13
  217.5 43.1 %shard_map.379 = (bf16[1280,2048]{1,0:T(8,128)(2,1)}, bf16[1280,4096]{1,0:T(8,128)(2,1)}, f32[1280,128]{1,0:T(8,128)S(1)}) custom-call(bf16[1280,1536]{1,0:T(8,128)(2,1)} %copy-done.13, bf16[1280,1536]{1,0:T(8,128)(2,1)} %outgrad_ref.5, f32[1280,128]{1,0:T(8,128)S(1)} %get-tuple-element.69.gates_ref, bf16[1536,4096]{1,0:T(8,128)(2,1)} %bitcast.66, ...), custom_call_target="tpu_custom_call" | custom-call | flops 24159191040 | bytes 34603008 | tf_op jit(solution)/shard_map/pallas_call | solution.py:781
  260.6 22.2 %convolution_convert_fusion.1 = bf16[1280,1536]{1,0:T(8,128)(2,1)S(1)} fusion(bf16[1280,4096]{1,0:T(8,128)(2,1)} %get-tuple-element.73.hidden_ref, bf16[1536,4096]{1,0:T(8,128)(2,1)} %bitcast.67), kind=kOutput, calls=%fused_computation.2 | convolution fusion | flops 16108093440 | bytes 27000832 | tf_op jit(solution)/shard_map/dot_general | solution.py:1475
  282.8 2.4 pad_maximum_fusion.x_ref
  285.2 121.8 %shard_map.380 = (bf16[1280,1664]{1,0:T(8,128)(2,1)}, bf16[1536,4096]{1,0:T(8,128)(2,1)}, bf16[1536,2048]{1,0:T(8,128)(2,1)}, bf16[1280,1536]{1,0:T(8,128)(2,1)}) custom-call(bf16[1280,1664]{1,0:T(8,128)(2,1)} %pad_maximum_fusion.x_ref, bf16[1280,1536]{1,0:T(8,128)(2,1)} %copy-done.13, bf16[1280,1536]{1,0:T(8,128)(2,1)} %outgrad_ref.5, ...), custom_call_target="tpu_custom_call" | custom-call | flops 32212254720 | bytes 19660800 | tf_op jit(solution)/shard_map/pallas_call | solution.py:689
  407.1 1.2 copy-done.9
  408.3 14.3 %shard_map.381 = (f32[1280,1536]{1,0:T(8,128)}, bf16[1280,1536]{1,0:T(8,128)(2,1)}, bf16[1280,384]{1,0:T(8,128)(2,1)S(1)}, bf16[1280,128]{1,0:T(8,128)(2,1)S(1)}, f32[8,1536]{1,0:T(8,128)S(1)}) custom-call(bf16[1280,1536]{1,0:T(8,128)(2,1)} %tokens_ref.1, bf16[1280,1536]{1,0:T(8,128)(2,1)} %copy-done.1, bf16[1280,1664]{1,0:T(8,128)(2,1)} %get-tuple-element.78.summed_ref, ...), custom_call_target="tpu_custom_call" | custom-call | tf_op jit(solution)/shard_map/pallas_call | solution.py:947
  422.6 0.9 copy-done.18
  424.9 0.7 copy.108
  425.7 4.3 convolution_convert_fusion.5
  429.9 3.3 convolution_convert_fusion.4
  433.2 44.7 %shard_map.382 = bf16[1280,640]{1,0:T(8,128)(2,1)} custom-call(bf16[1280,384]{1,0:T(8,128)(2,1)} %copy-done.22, bf16[1280,256]{1,0:T(8,128)(2,1)} %copy-done.23, bf16[2,1024,256]{2,1,0:T(8,128)(2,1)} %copy-done.26, bf16[1280,384]{1,0:T(8,128)(2,1)} %copy-done.18, bf16[1280,384]{1,0:T(8,128)(2,1)} %copy-done.24, f32[2,8,640]{2,1,0:T(8,128)} %copy-done.27, ...), custom_call_target="tpu_custom_call" | custom-call | flops 30198988800 | bytes 5898240 | tf_op jit(solution)/shard_map/pallas_call | solution.py:1287
  478.0 6.5 convolution_convert_fusion.x_ref
  484.4 4.5 convolution_convert_fusion.3
  488.9 166.4 %shard_map.383 = (f32[1280,1536]{1,0:T(8,128)}, f32[192,1152]{1,0:T(8,128)}, f32[16,256]{1,0:T(8,128)}) custom-call(bf16[1280,1536]{1,0:T(8,128)(2,1)} %convolution_convert_fusion.x_ref, bf16[1280,1536]{1,0:T(8,128)(2,1)} %tokens_ref.1, f32[1280,1536]{1,0:T(8,128)} %get-tuple-element.85.middle_ref, f32[8,1536]{1,0:T(8,128)} %copy-done.10, ...), custom_call_target="tpu_custom_call" | custom-call | flops 1966080 | bytes 1048576 | tf_op jit(solution)/shard_map/pallas_call | solution.py:577
  655.3 1.1 slice.24
  656.9 1.0 slice_bitcast_fusion
  659.8 0.7 copy.106
  660.6 1.7 multiply_subtract_fusion.3
  662.3 1.6 copy.109
  665.9 1.3 multiply_subtract_fusion.4
  667.2 2.3 multiply_subtract_fusion.2
  669.5 3.1 multiply_subtract_fusion.1
  672.7 7.9 %add_convert_fusion = bf16[1280,1536]{1,0:T(8,128)(2,1)} fusion(bf16[1280,1536]{1,0:T(8,128)(2,1)} %all-reduce.2.cloned.1.call-done, bf16[1280,1536]{1,0:T(8,128)(2,1)} %copy-done.1, bf16[1280,1536]{1,0:T(8,128)(2,1)} %tokens_ref.1), kind=kLoop, calls=%fused_computation | loop fusion | flops 11796480 | bytes 15728640 | tf_op jit(solution)/shard_map/convert_element_type | solution.py:1555
  680.6 5.7 multiply_subtract_fusion
  686.3 1.9 copy-done.4
  688.2 1.9 copy-done.5
  690.1 1.4 copy-done.6
  691.5 5.6 shard_map.384
  697.1 7.1 copy.124
  (95 shorter events, 7.5 us)
Async XLA Ops:
  8.0 664.6 %all-reduce.2.cloned.1.call-start = ((), (), s32[]{:S(2)}) async-start(), calls=%async_computation.2 | async-start | bytes 7864320 | tf_op jit(solution)/shard_map/psum | solution.py:1482
  13.5 1.9 copy-start.2
  41.7 1.0 copy-start.7
  42.7 1.3 copy-start.15
  44.0 2.0 copy-start.34
  44.3 362.8 %copy-start.10 = (f32[8,1536]{1,0:T(8,128)}, f32[8,1536]{1,0:T(8,128)S(1)}, u32[]{:S(2)}) copy-start(f32[8,1536]{1,0:T(8,128)S(1)} %convert_bitcast_fusion.2.gain_ref) | copy-start | bytes 147460
  46.2 1.6 copy-start.16
  47.8 1.1 copy-start.20
  48.9 1.1 copy-start.21
  58.0 34.4 %copy-start.22 = (bf16[1280,384]{1,0:T(8,128)(2,1)}, bf16[1280,384]{1,0:T(8,128)(2,1)S(1)}, u32[]{:S(2)}) copy-start(bf16[1280,384]{1,0:T(8,128)(2,1)S(1)} %get-tuple-element.62.q_ref) | copy-start | bytes 2949124
  58.0 34.4 %copy-start.23 = (bf16[1280,256]{1,0:T(8,128)(2,1)}, bf16[1280,256]{1,0:T(8,128)(2,1)S(1)}, u32[]{:S(2)}) copy-start(bf16[1280,256]{1,0:T(8,128)(2,1)S(1)} %get-tuple-element.63.kv_ref) | copy-start | bytes 1966084
  58.0 34.4 %copy-start.8 = (bf16[8,192,384]{2,1,0:T(8,128)(2,1)S(1)}, bf16[8,192,384]{2,1,0:T(8,128)(2,1)}, u32[]{:S(2)}) copy-start(bf16[8,192,384]{2,1,0:T(8,128)(2,1)} %copy-done.7) | copy-start | bytes 3538948
  92.4 2.3 copy-start.24
  92.4 2.3 copy-start.26
  92.4 2.3 copy-start.27
  94.7 116.2 %copy-start = (bf16[1280,1536]{1,0:T(8,128)(2,1)S(1)}, bf16[1280,1536]{1,0:T(8,128)(2,1)}, u32[]{:S(2)}) copy-start(bf16[1280,1536]{1,0:T(8,128)(2,1)} %tokens_ref.1) | copy-start | bytes 11796484
  206.3 4.6 copy-start.12
  210.9 4.7 copy-start.1
  210.9 4.7 copy-start.14
  210.9 6.6 copy-start.19
  215.6 1.8 copy-start.13
  407.0 1.3 copy-start.9
  407.1 273.5 %reduce-scatter.5.cloned.1.call-start = ((), (), s32[]{:S(2)}) async-start(), calls=%async_computation.4 | async-start | bytes 7077888 | tf_op jit(solution)/shard_map/reduce_scatter | solution.py:1490
  422.6 0.9 copy-start.18
  423.6 0.6 copy-start.11
  424.2 0.7 copy-start.32
  424.2 262.1 %reduce-scatter.3.cloned.1.call-start = ((), (), s32[]{:S(2)}) async-start(), calls=%async_computation.3 | async-start | bytes 14155776 | tf_op jit(solution)/shard_map/reduce_scatter | solution.py:1491
  424.9 5.0 copy-start.25
  425.7 4.3 copy-start.35
  433.2 44.7 %copy-start.17 = (bf16[8,192,640]{2,1,0:T(8,128)(2,1)S(1)}, bf16[8,192,640]{2,1,0:T(8,128)(2,1)}, u32[]{:S(2)}) copy-start(bf16[8,192,640]{2,1,0:T(8,128)(2,1)} %copy-done.15) | copy-start | bytes 5898244
  477.9 6.5 copy-start.36
  477.9 6.5 copy-start.37
  655.3 2.8 copy-start.33
  655.3 11.9 %copy-start.29 = (f32[2,192,192]{2,1,0:T(8,128)S(1)}, f32[2,192,192]{2,1,0:T(8,128)}, u32[]{:S(2)}) copy-start(f32[2,192,192]{2,1,0:T(8,128)} %param.29) | copy-start | bytes 884740
  656.5 13.1 %copy-start.28 = (f32[192,2,320]{2,1,0:T(2,128)S(1)}, f32[192,2,320]{2,1,0:T(2,128)}, u32[]{:S(2)}) copy-start(f32[192,2,320]{2,1,0:T(2,128)} %param.26) | copy-start | bytes 1474564
  656.5 13.1 %copy-start.30 = (f32[192,2,320]{2,1,0:T(2,128)S(1)}, f32[192,2,320]{2,1,0:T(2,128)}, u32[]{:S(2)}) copy-start(f32[192,2,320]{2,1,0:T(2,128)} %param.27) | copy-start | bytes 1474564
  656.5 13.1 %copy-start.31 = (f32[192,2,320]{2,1,0:T(2,128)S(1)}, f32[192,2,320]{2,1,0:T(2,128)}, u32[]{:S(2)}) copy-start(f32[192,2,320]{2,1,0:T(2,128)} %param.28) | copy-start | bytes 1474564
  680.6 5.7 copy-start.3
  686.3 1.9 copy-start.4
  688.2 1.9 copy-start.5
  690.1 1.4 copy-start.6
Sparse Core Ops, SparseCore 0:
  407.2 193.7 all-reduce.1
Sparse Core Ops, SparseCore 1:
  423.7 71.6 reduce-scatter.4
  499.1 97.2 reduce-scatter.2

commit v6 on v5

--- a/solution.py
+++ b/solution.py
@@ -50,15 +50,15 @@
     return (weight - learn_rate * (update + decay_rate * weight), first_next, second_next)
 
 
-def line_steps(n):
-    return line_parts + 2 * (n - 1) * line_lag
+def line_steps(n, parts=line_parts):
+    return parts + 2 * (n - 1) * line_lag
 
 
 def line_engine(
-    n, x_ref, o_ref, held, send_red, recv_red, send_out, recv_out, complete=lambda at: None
+    n, x_ref, o_ref, held, send_red, recv_red, send_out, recv_out,
+    complete=lambda at, half, c: None, parts=line_parts,
 ):
     me = lax.axis_index("tensor")
-    parts = line_parts
     rows = x_ref.shape[0] // (2 * parts)
     low, high = me - 1, me + 1
 
@@ -131,7 +131,7 @@
                     def _():
                         o_ref[part(half, c)] = total.astype(o_ref.dtype)
                         out_copy(half, c).start()
-                        complete(part(half, c))
+                        complete(part(half, c), half, c)
 
         for half in (0, 1):
             at = place(half)
@@ -145,7 +145,7 @@
                 def _():
                     out_copy(half, c).start()
 
-                complete(part(half, c))
+                complete(part(half, c), half, c)
 
     def finish():
         def one(c, carry):
@@ -167,9 +167,9 @@
     return greet, begin, slot, finish
 
 
-def line_scratch(shape, dtype):
+def line_scratch(shape, dtype, parts=line_parts):
     return [pltpu.VMEM(shape, dtype)] + [
-        pltpu.SemaphoreType.DMA((2, line_parts)) for _ in range(4)
+        pltpu.SemaphoreType.DMA((2, parts)) for _ in range(4)
     ]
 
 
@@ -416,38 +416,63 @@
 
 
 def last_kernel(
-    n, n_dp, pieces, x_ref, tokens_ref, middle_ref, gain_ref, gain_second_ref, *refs,
+    n, n_dp, pieces, first_ref, tokens_ref, middle_ref, mixture_ref, gain_ref, gain_second_ref, *refs,
 ):
     weights_refs, refs = refs[:pieces], refs[pieces:]
     last_body(
-        n, n_dp, x_ref, tokens_ref, middle_ref, gain_ref, weights_refs, gain_second_ref, *refs
+        n, n_dp, first_ref, tokens_ref, middle_ref, mixture_ref, gain_ref, weights_refs,
+        gain_second_ref, *refs,
     )
 
 
 def last_body(
-    n, n_dp, x_ref, tokens_ref, middle_ref, gain_ref, weights_refs, gain_second_ref,
-    grad_ref, weights_out, gains_out, o_ref, held, send_red, recv_red, send_out, recv_out,
-    tokens_v, middle_v, grad_v, in_sem, out_sem, got, w_send, w_recv,
+    n, n_dp, first_ref, tokens_ref, middle_ref, mixture_ref, gain_ref, weights_refs,
+    gain_second_ref, grad_ref, weights_out, gains_out, mixture_out,
+    x_ref, o_ref, held, send_red, recv_red, send_out, recv_out,
+    tokens_v, middle_v, grad_v, in_sem, out_sem, x_sem, got, w_send, w_recv,
     g_from, g_got, g_send, g_recv, z_from, z_got, z_send, z_recv, acc,
 ):
     me, line = lax.axis_index("dp"), lax.axis_index("tensor")
     model = x_ref.shape[1]
-    rows = x_ref.shape[0] // (2 * line_parts)
+    rows = tokens_v.shape[0] // (2 * line_parts)
     depth = weights_out.shape[0]
+    half_x, half_m = line_parts * rows, TOK_MB // 2
+    half_all = half_x + half_m
+    parts = half_all // rows
+
+    def own_rows(half, c):
+        return pl.ds(pl.multiple_of((half * line_parts + c) * rows, 16), rows)
+
+    def half_copies(x, m, sem, back):
+        for half in (0, 1):
+            for ref, low, size, at in (
+                (x, half * half_x, half_x, half * half_all),
+                (m[0], m[1] + half * half_m, half_m, half * half_all + half_x),
+            ):
+                if ref is not None:
+                    here = (o_ref if back else x_ref).at[pl.ds(at, size)]
+                    there = ref.at[pl.ds(low, size)]
+                    k = half * 2 + (ref is m[0])
+                    yield pltpu.make_async_copy(
+                        *((here, there) if back else (there, here)), sem.at[k]
+                    )
 
     def norm_of(at):
         x = tokens_v[at].astype(f32)
         inverse = lax.rsqrt(jnp.mean(x * x, axis=-1, keepdims=True) + eps_norm)
         return x * inverse, inverse
 
-    def complete(at):
-        norm, inverse = norm_of(at)
-        grad = o_ref[at].astype(f32) * (gain_ref[0:1] + gain_ref[2:3])
-        mean = jnp.mean(grad * norm, axis=-1, keepdims=True)
-        grad_v[at] = middle_v[at] + inverse * (grad - norm * mean)
+    def complete(at, half, c):
+        @pl.when(c < line_parts)
+        def _():
+            own = own_rows(half, c)
+            norm, inverse = norm_of(own)
+            grad = o_ref[at].astype(f32) * (gain_ref[0:1] + gain_ref[2:3])
+            mean = jnp.mean(grad * norm, axis=-1, keepdims=True)
+            grad_v[own] = middle_v[own] + inverse * (grad - norm * mean)
 
     _, _, slot, finish = line_engine(
-        n, x_ref, o_ref, held, send_red, recv_red, send_out, recv_out, complete
+        n, x_ref, o_ref, held, send_red, recv_red, send_out, recv_out, complete, parts
     )
 
     columns, low = [], 0
@@ -489,8 +514,9 @@
 
     load_tokens = pltpu.make_async_copy(tokens_ref, tokens_v, in_sem.at[0])
     load_middle = pltpu.make_async_copy(middle_ref, middle_v, in_sem.at[1])
-    load_tokens.start()
-    load_middle.start()
+    loads = list(half_copies(first_ref, (mixture_ref, TOK_MB), x_sem, False))
+    for load in loads + [load_tokens, load_middle]:
+        load.start()
     barrier = pltpu.get_barrier_semaphore()
 
     def greet(axis, place, count):
@@ -507,24 +533,30 @@
     for j in pieces:
         loop(n_dp, lambda k: weights_copy(k, j).start())
     acc[...] = jnp.zeros_like(acc)
-    load_tokens.wait()
-    load_middle.wait()
+    for load in loads:
+        load.wait()
 
     def step(t, carry):
         slot(t)
-
-        @pl.when(t < line_parts)
-        def _():
-            for half in (0, 1):
-                at = pl.ds(pl.multiple_of((half * line_parts + t) * rows, 16), rows)
-                norm, _ = norm_of(at)
-                term = x_ref[at].astype(f32) * norm
-                acc[...] += jnp.sum(term.reshape(rows // 8, 8, model), axis=0)
-
         return carry
 
-    total = line_steps(n)
-    lax.fori_loop(0, line_parts, step, 0)
+    def gain_step(t, carry):
+        slot(t)
+        c = t - early
+        for half in (0, 1):
+            at = pl.ds(pl.multiple_of(half * half_all + c * rows, 16), rows)
+            norm, _ = norm_of(own_rows(half, c))
+            term = x_ref[at].astype(f32) * norm
+            acc[...] += jnp.sum(term.reshape(rows // 8, 8, model), axis=0)
+        return carry
+
+    total = line_steps(n, parts)
+    early, size = 4, 32
+    lax.fori_loop(0, early, step, 0)
+    for load in (load_tokens, load_middle):
+        load.wait()
+    low = early + line_parts
+    lax.fori_loop(early, low, gain_step, 0)
     width = g_from.shape[2]
     for p in range(n_dp):
         moved = acc[...] if p == 0 else pltpu.roll(acc[...], model - p * depth, 1)
@@ -534,63 +566,70 @@
         )
         g_from[p, 8:] = jnp.where(line == 0, moved[:, :width], 0.0)
     loop(n_dp, lambda k: gains_copy(k).start())
-    late = min(line_parts + 4, total)
-    lax.fori_loop(line_parts, late, step, 0)
-    loop(n_dp, lambda k: gains_copy(k).wait_recv())
-    z_from[...] = lax.fori_loop(1, n_dp, lambda k, t: t + g_got[k], g_from[me])
-    loop(n, lambda k: line_copy(k).start())
     for j in pieces:
         loop(n_dp, lambda k: weights_copy(k, j).wait_recv())
-    lax.fori_loop(late, total, step, 0)
-    size = 32
-
-    def add(b, carry):
-        at = pl.ds(pl.multiple_of(b * size, 16), size)
+
+    def add_step(t, carry):
+        slot(t)
+        at = pl.ds(pl.multiple_of((t - low) * size, 16), size)
         for j, ref in enumerate(weights_refs):
             weights_out[at, columns[j]] = lax.fori_loop(
                 1,
                 n_dp,
-                lambda k, t: t + got[k, at, columns[j]].astype(f32),
+                lambda k, v: v + got[k, at, columns[j]].astype(f32),
                 ref[me, at].astype(f32),
             )
         return carry
 
+    middle = low + depth // size
+    lax.fori_loop(low, middle, add_step, 0)
+    loop(n_dp, lambda k: gains_copy(k).wait_recv())
+    z_from[...] = lax.fori_loop(1, n_dp, lambda k, v: v + g_got[k], g_from[me])
+    loop(n, lambda k: line_copy(k).start())
+    own_done = max(middle, line_steps(n))
+    lax.fori_loop(middle, own_done, step, 0)
     every = pltpu.make_async_copy(grad_v, grad_ref, out_sem)
     every.start()
-    lax.fori_loop(0, depth // size, add, 0)
+    lax.fori_loop(own_done, total, step, 0)
+    stores = list(half_copies(None, (mixture_out, 0), x_sem, True))
+    for store in stores:
+        store.start()
     loop(n, lambda k: line_copy(k).wait_recv())
-    gains_out[...] = lax.fori_loop(1, n, lambda k, t: t + z_got[k], z_from[...])
+    gains_out[...] = lax.fori_loop(1, n, lambda k, v: v + z_got[k], z_from[...])
     finish()
     for j in pieces:
         loop(n_dp, lambda k: weights_copy(k, j).wait_send())
     loop(n_dp, lambda k: gains_copy(k).wait_send())
     loop(n, lambda k: line_copy(k).wait_send())
-    every.wait()
-
-
-def last_call(x, tokens, middle, gain, weights, gain_second, n, n_dp, barrier_id):
+    for store in stores + [every]:
+        store.wait()
+
+
+def last_call(x, tokens, middle, mixture, gain, weights, gain_second, n, n_dp, barrier_id):
     count, model = x.shape
     depth, width = model // n_dp, sum(w.shape[1] for w in weights)
     lanes = -(-depth // 128) * 128
     whole, anywhere = pl.BlockSpec(memory_space=pltpu.VMEM), pl.BlockSpec(memory_space=pl.ANY)
     dma = pltpu.SemaphoreType.DMA
-    grad, weights, gains = pl.pallas_call(
+    grad, weights, gains, mixture = pl.pallas_call(
         functools.partial(last_kernel, n, n_dp, len(weights)),
         out_shape=[
             jax.ShapeDtypeStruct((count, model), f32),
             jax.ShapeDtypeStruct((depth, width), f32),
             jax.ShapeDtypeStruct((16, lanes), f32),
+            jax.ShapeDtypeStruct((TOK_MB, model), bf16),
         ],
-        in_specs=[whole, anywhere, anywhere, whole, whole] + [whole] * len(weights),
-        out_specs=[anywhere, whole, whole],
-        scratch_shapes=[pltpu.VMEM(x.shape, bf16)]
-        + line_scratch(x.shape, x.dtype)
+        in_specs=[anywhere, anywhere, anywhere, anywhere, whole, whole] + [whole] * len(weights),
+        out_specs=[anywhere, whole, whole, anywhere],
+        scratch_shapes=[pltpu.VMEM((count + TOK_MB, model), bf16)] * 2
+        + line_scratch((count + TOK_MB, model), bf16, line_parts * (count + TOK_MB) // count)
         + [
             pltpu.VMEM((count, model), bf16),
             pltpu.VMEM((count, model), f32),
             pltpu.VMEM((count, model), f32),
             dma((2,)),
             dma,
+            dma((4,)),
             pltpu.VMEM((n_dp, depth, width), bf16),
             dma((len(weights), n_dp)),
             dma((len(weights), n_dp)),
@@ -610,9 +649,9 @@
         cost_estimate=pl.CostEstimate(
             flops=count * model, bytes_accessed=2**20, transcendentals=0
         ),
-    )(x, tokens, middle, gain, gain_second, *(w.reshape(n_dp, depth, -1) for w in weights))
+    )(x, tokens, middle, mixture, gain, gain_second, *(w.reshape(n_dp, depth, -1) for w in weights))
     gains = jnp.sum(gains.reshape(2, 8, lanes), axis=1)[:, :depth]
-    return grad, weights, gains
+    return grad, weights, gains, mixture
 
 
 def expert_grads_kernel(
@@ -975,6 +1014,35 @@
     )(tokens, branch, summed, gates, outgrad, gain, router, outproj)
 
 
+def block_out_kernel(x_ref, b_ref, first_ref, second_ref, o_ref):
+    middle = x_ref[...].astype(f32) + b_ref[...].astype(f32)
+
+    @pl.when(pl.program_id(0) == 0)
+    def _():
+        o_ref[...] = (middle + first_ref[...].astype(f32)).astype(bf16)
+
+    @pl.when(pl.program_id(0) == 1)
+    def _():
+        o_ref[...] = (middle + second_ref[...].astype(f32)).astype(bf16)
+
+
+def block_out_call(tokens, branch, first, second):
+    count, model = tokens.shape
+    columns = model // 3
+    row = pl.BlockSpec((TOK_MB, columns), lambda i, j: (i, j))
+    half = lambda place: pl.BlockSpec(
+        (TOK_MB, columns), lambda i, j: (0, jnp.where(i == place, j, 0 if place else 2))
+    )
+    return pl.pallas_call(
+        block_out_kernel,
+        grid=(MICRO, 3),
+        in_specs=[row, row, half(0), half(1)],
+        out_specs=row,
+        out_shape=jax.ShapeDtypeStruct((count, model), bf16),
+        compiler_params=pltpu.CompilerParams(vmem_limit_bytes=32 * 2**20),
+    )(tokens, branch, first, second)
+
+
 def head_places(heads):
     return [(h // GROUP, h % 2, h // 2) for h in range(heads)]
 
@@ -1000,17 +1068,21 @@
     return tiles
 
 
-def meet(me, n):
+def greet(me, n):
     barrier = pltpu.get_barrier_semaphore()
 
-    def greet(k, carry):
+    def one(k, carry):
         pl.semaphore_signal(
             barrier, inc=1, device_id={"dp": lax.rem(me + k, n)}, device_id_type=MESH
         )
         return carry
 
-    lax.fori_loop(1, n, greet, 0)
-    pl.semaphore_wait(barrier, n - 1)
+    lax.fori_loop(1, n, one, 0)
+    return n - 1
+
+
+def meet(me, n):
+    pl.semaphore_wait(pltpu.get_barrier_semaphore(), greet(me, n))
 
 
 def load_spread(m, all_ref, kv_ref, k_ref, v_ref, kt_ref=None):
@@ -1479,7 +1551,7 @@
         jnp.concatenate([rows_grad, gate_grad.astype(bf16)], axis=1),
         normed_second, cotangent, down_start, down_rest, hidden_grad, active, n_tensor, 2,
     )
-    mixture = lax.psum(mixture, "tensor")
+    first_mixture = lax.psum(mixture[:TOK_MB], "tensor")
     model = tokens.shape[1]
     middle_grad, branch_own, attended_grad, logits_grad, gain_second_grad = middle_back_call(
         tokens, branch, summed, gates_wide, cotangent, gain_rows, small_full, outproj_full
@@ -1546,13 +1618,12 @@
             gateup_weight, gateup_first, gateup_second,
             gateup_back(gateup_grad).astype(f32), weight_decay, 0.05,
         )
-    tokens_grad, attn_grad, gains_grad = last_call(
-        normed_first_grad, tokens, middle_grad, gain_rows,
+    tokens_grad, attn_grad, gains_grad, second_mixture = last_call(
+        normed_first_grad, tokens, middle_grad, mixture, gain_rows,
         attn_grad, gain_second_grad, n_tensor, n_dp, 7,
     )
-    mixture, tokens_grad = lax.optimization_barrier((mixture, tokens_grad))
-    middle = tokens.astype(f32) + branch.astype(f32)
-    block_out = (middle + mixture.astype(f32)).astype(bf16)
+    first_mixture, tokens_grad = lax.optimization_barrier((first_mixture, tokens_grad))
+    block_out = block_out_call(tokens, branch, first_mixture, second_mixture)
     split = (in_width, in_width + out_width, in_width + out_width + EXPERTS)
     inproj_grad, outproj_grad, router_grad = (
         attn_grad[:, : split[0]],

time: 717 us -> 707 us (0.986)
  other arithmetic: 32.8 us -> 22.6 us
    pallas_call x1, Pallas kernels: 166 us -> 154 us  [last_call(): pl.pallas_call(functools.partial(last_kernel, n, n_dp, len(weights)), out...]
    convert_element_type x1 -> x0, other arithmetic: 7.92 us -> none  [shards(): block_out = (middle + mixture.astype(f32)).astype(bf16)]
    unnamed x83 -> x101, local copies, waits for them, and re-layouts: 33.7 us -> 37.9 us
  transfers between devices with their start and end apart: 3 -> 3, of which waited for: 0 -> 0; matrix products, arithmetic and copies ran while one was open for 7% -> 5% of each run, Pallas kernels for 32% -> 31%
where the time goes in v6:
time: 707 us; the launch traced here: 702 us
  Pallas kernels  574 us (81%)
  local copies, waits for them, and re-layouts  44.9 us (6%)
  matrix products  42.9 us (6%)
  other arithmetic  22.6 us (3%)
  between operations  16.3 us (2%)
    pallas_call x1, Pallas kernels, last_call(): pl.pallas_call(functools.partial(last_kernel, n, n_dp, len(weights)), out...  154 us
    pallas_call x1, Pallas kernels, expert_grads_call(): pl.pallas_call(functools.partial(expert_grads_kernel, n, shape), grid=(a...  122 us
    pallas_call x1, Pallas kernels, line_gather(): pl.pallas_call(functools.partial(line_gather_kernel, n, n_dp), out_shape=...  112 us
    pallas_call x1, Pallas kernels, attention_back_call(): pl.pallas_call(functools.partial(attention_back_kernel, heads, n), in_spe...  45.5 us
    pallas_call x1, Pallas kernels, expert_call(): pl.pallas_call(functools.partial(expert_kernel, group, steps), grid=(step...  43.1 us
    unnamed x101, local copies, waits for them, and re-layouts  37.9 us
    pallas_call x1, Pallas kernels, attention_call(): pl.pallas_call(functools.partial(attention_kernel, heads, n), in_specs=[w...  34.4 us
    pallas_call x1, Pallas kernels, gather(): pl.pallas_call(functools.partial(gather_kernel, n, group, len(arrays)), o...  26.3 us
  transfers between devices with their start and end apart: 3, of which 0 were waited for; matrix products, arithmetic and copies ran while one was open for 5% of the time, Pallas kernels for 31%

profile of v6, /device:TPU:0, one launch (start us, length us, event | category | flops | bytes accessed | tf_op | source)
XLA Modules:
  0.0 701.6 jit_solution(8272189842245790336)
XLA Ops:
  8.1 1.4 broadcast_multiply_fusion.1
  9.6 0.8 subtract_convert_fusion
  10.7 1.3 convert_element_type.64
  12.2 1.0 convert_element_type.66
  13.6 1.9 copy-done.4
  15.4 26.3 %shard_map.374 = (bf16[8,192,640]{2,1,0:T(8,128)(2,1)S(1)}, bf16[8,192,384]{2,1,0:T(8,128)(2,1)S(1)}, bf16[8,192,128]{2,1,0:T(8,128)(2,1)S(1)}, bf16[192,4096]{1,0:T(8,128)(2,1)S(1)}) custom-call(bf16[192,640]{1,0:T(8,128)(2,1)S(1)} %convert_element_type.65.refs_0_, bf16[192,384]{1,0:T(8,128)(2,1)S(1)} %bitcast.65, ...), custom_call_target="tpu_custom_call" | custom-call | tf_op jit(solution)/shard_map/pallas_call | solution.py:329
  41.7 1.0 copy-done.11
  42.7 1.3 copy-done.19
  44.4 1.5 bitcast_bitcast_fusion
  46.2 1.5 copy-done.20
  47.8 1.1 copy-done.24
  48.9 1.1 copy-done.25
  50.0 7.9 %shard_map.375 = (bf16[1280,1536]{1,0:T(8,128)(2,1)}, bf16[1280,384]{1,0:T(8,128)(2,1)S(1)}, bf16[1280,256]{1,0:T(8,128)(2,1)S(1)}) custom-call(bf16[1280,1536]{1,0:T(8,128)(2,1)} %x_ref.7, f32[8,1536]{1,0:T(8,128)S(1)} %convert_bitcast_fusion.2.gain_ref, bf16[1536,640]{1,0:T(8,128)(2,1)S(1)} %bitcast.70, f32[1536,128]{1,0:T(8,128)S(1)} %copy-done.24, ...), custom_call_target="tpu_custom_call" | custom-call | flops 2516582400 | bytes 11796480 | tf_op jit(solution)/shard_map/pallas_call | solution.py:895
  58.0 34.4 %shard_map.376 = (bf16[1280,384]{1,0:T(8,128)(2,1)S(1)}, f32[2,8,640]{2,1,0:T(8,128)S(1)}, bf16[2,1024,256]{2,1,0:T(8,128)(2,1)S(1)}, bf16[8,192,1024]{2,1,0:T(8,128)(2,1)}) custom-call(bf16[1280,384]{1,0:T(8,128)(2,1)S(1)} %get-tuple-element.63.q_ref, bf16[1280,256]{1,0:T(8,128)(2,1)S(1)} %get-tuple-element.64.kv_ref, ...), custom_call_target="tpu_custom_call" | custom-call | flops 12079595520 | bytes 3932160 | tf_op jit(solution)/shard_map/pallas_call | solution.py:1196
  92.4 2.2 convolution_convert_fusion.2.x_ref
  94.7 111.6 %shard_map.377 = (bf16[1280,1536]{1,0:T(8,128)(2,1)S(1)}, bf16[8,192,4096]{2,1,0:T(8,128)(2,1)S(1)}, bf16[8,192,1024]{2,1,0:T(8,128)(2,1)S(1)}) custom-call(bf16[1280,1536]{1,0:T(8,128)(2,1)S(1)} %convolution_convert_fusion.2.x_ref, bf16[192,4096]{1,0:T(8,128)(2,1)S(1)} %get-tuple-element.67.a_ref, bf16[192,1024]{1,0:T(8,128)(2,1)S(1)} %get-tuple-element.179.b_ref), custom_call_target="tpu_custom_call" | custom-call | flops 1966080 | bytes 196608000 | tf_op jit(solution)/shard_map/pallas_call | solution.py:401
  206.3 4.6 copy-done.16
  210.9 4.7 shard_map.378
  215.6 1.9 copy-done.17
  217.5 43.1 %shard_map.379 = (bf16[1280,2048]{1,0:T(8,128)(2,1)}, bf16[1280,4096]{1,0:T(8,128)(2,1)}, f32[1280,128]{1,0:T(8,128)S(1)}) custom-call(bf16[1280,1536]{1,0:T(8,128)(2,1)} %copy-done.17, bf16[1280,1536]{1,0:T(8,128)(2,1)} %outgrad_ref.5, f32[1280,128]{1,0:T(8,128)S(1)} %get-tuple-element.70.gates_ref, bf16[1536,4096]{1,0:T(8,128)(2,1)} %bitcast.66, ...), custom_call_target="tpu_custom_call" | custom-call | flops 24159191040 | bytes 34603008 | tf_op jit(solution)/shard_map/pallas_call | solution.py:820
  260.6 22.2 %convolution_convert_fusion.1 = bf16[1280,1536]{1,0:T(8,128)(2,1)S(1)} fusion(bf16[1280,4096]{1,0:T(8,128)(2,1)} %get-tuple-element.74.hidden_ref, bf16[1536,4096]{1,0:T(8,128)(2,1)} %bitcast.67), kind=kOutput, calls=%fused_computation.1 | convolution fusion | flops 16108093440 | bytes 27000832 | tf_op jit(solution)/shard_map/dot_general | solution.py:1547
  282.8 2.4 pad_maximum_fusion.x_ref
  285.2 121.6 %shard_map.380 = (bf16[1280,1664]{1,0:T(8,128)(2,1)}, bf16[1536,4096]{1,0:T(8,128)(2,1)}, bf16[1536,2048]{1,0:T(8,128)(2,1)}, bf16[1280,1536]{1,0:T(8,128)(2,1)}) custom-call(bf16[1280,1664]{1,0:T(8,128)(2,1)} %pad_maximum_fusion.x_ref, bf16[1280,1536]{1,0:T(8,128)(2,1)} %copy-done.17, bf16[1280,1536]{1,0:T(8,128)(2,1)} %outgrad_ref.5, ...), custom_call_target="tpu_custom_call" | custom-call | flops 32212254720 | bytes 19660800 | tf_op jit(solution)/shard_map/pallas_call | solution.py:728
  406.8 2.9 slice.27
  409.9 1.2 copy-done.13
  411.0 14.2 %shard_map.381 = (f32[1280,1536]{1,0:T(8,128)}, bf16[1280,1536]{1,0:T(8,128)(2,1)}, bf16[1280,384]{1,0:T(8,128)(2,1)S(1)}, bf16[1280,128]{1,0:T(8,128)(2,1)S(1)}, f32[8,1536]{1,0:T(8,128)S(1)}) custom-call(bf16[1280,1536]{1,0:T(8,128)(2,1)} %x_ref.7, bf16[1280,1536]{1,0:T(8,128)(2,1)} %copy-done.2, bf16[1280,1664]{1,0:T(8,128)(2,1)} %get-tuple-element.79.summed_ref, ...), custom_call_target="tpu_custom_call" | custom-call | tf_op jit(solution)/shard_map/pallas_call | solution.py:986
  425.2 0.9 copy-done.22
  427.6 4.3 convolution_convert_fusion.5
  431.8 3.3 convolution_convert_fusion.4
  435.1 45.5 %shard_map.382 = bf16[1280,640]{1,0:T(8,128)(2,1)} custom-call(bf16[1280,384]{1,0:T(8,128)(2,1)} %copy-done.26, bf16[1280,256]{1,0:T(8,128)(2,1)} %copy-done.27, bf16[2,1024,256]{2,1,0:T(8,128)(2,1)} %copy-done.30, bf16[1280,384]{1,0:T(8,128)(2,1)} %copy-done.22, bf16[1280,384]{1,0:T(8,128)(2,1)} %copy-done.28, f32[2,8,640]{2,1,0:T(8,128)} %copy-done.31, ...), custom_call_target="tpu_custom_call" | custom-call | flops 30198988800 | bytes 5898240 | tf_op jit(solution)/shard_map/pallas_call | solution.py:1359
  480.7 6.4 convolution_convert_fusion.first_ref
  487.1 4.5 convolution_convert_fusion.3
  491.6 154.4 %shard_map.383 = (f32[1280,1536]{1,0:T(8,128)}, f32[192,1152]{1,0:T(8,128)}, f32[16,256]{1,0:T(8,128)}, bf16[640,1536]{1,0:T(8,128)(2,1)}) custom-call(bf16[1280,1536]{1,0:T(8,128)(2,1)} %convolution_convert_fusion.first_ref, bf16[1280,1536]{1,0:T(8,128)(2,1)} %x_ref.7, f32[1280,1536]{1,0:T(8,128)} %get-tuple-element.86.middle_ref, ...), custom_call_target="tpu_custom_call" | custom-call | flops 1966080 | bytes 1048576 | tf_op jit(solution)/shard_map/pallas_call | solution.py:614
  646.1 1.1 slice.28
  647.7 1.0 slice_bitcast_fusion
  649.2 1.0 multiply_subtract_fusion.3
  652.9 2.2 multiply_subtract_fusion.2
  655.1 4.5 multiply_subtract_fusion.1
  659.6 2.1 copy-done.1
  661.7 2.1 copy-done.3
  663.8 1.5 copy-done.8
  665.4 4.9 shard_map.384
  670.3 5.7 multiply_subtract_fusion
  676.0 1.9 copy-done.6
  677.9 1.9 copy-done.7
  679.8 1.4 copy-done.10
  681.2 5.6 shard_map.385
  686.9 7.1 %copy.124 = f32[1280,1536]{1,0:T(8,128)} copy(f32[1280,1536]{1,0:T(8,128)} %get-tuple-element.204) | data formatting | bytes 15728640
  (114 shorter events, 6.9 us)
Async XLA Ops:
  8.0 651.6 %all-reduce.2.cloned.1.call-start = ((), (), s32[]{:S(2)}) async-start(), calls=%async_computation.2 | async-start | bytes 3932160 | tf_op jit(solution)/shard_map/psum | solution.py:1554
  13.5 1.9 copy-start.4
  41.7 1.0 copy-start.11
  42.7 1.3 copy-start.19
  44.3 365.5 %copy-start.14 = (f32[8,1536]{1,0:T(8,128)}, f32[8,1536]{1,0:T(8,128)S(1)}, u32[]{:S(2)}) copy-start(f32[8,1536]{1,0:T(8,128)S(1)} %convert_bitcast_fusion.2.gain_ref) | copy-start | bytes 147460
  44.3 1.6 copy-start.37
  46.2 1.6 copy-start.20
  47.8 1.1 copy-start.24
  48.9 1.1 copy-start.25
  58.0 34.4 %copy-start.26 = (bf16[1280,384]{1,0:T(8,128)(2,1)}, bf16[1280,384]{1,0:T(8,128)(2,1)S(1)}, u32[]{:S(2)}) copy-start(bf16[1280,384]{1,0:T(8,128)(2,1)S(1)} %get-tuple-element.63.q_ref) | copy-start | bytes 2949124
  58.0 34.4 %copy-start.27 = (bf16[1280,256]{1,0:T(8,128)(2,1)}, bf16[1280,256]{1,0:T(8,128)(2,1)S(1)}, u32[]{:S(2)}) copy-start(bf16[1280,256]{1,0:T(8,128)(2,1)S(1)} %get-tuple-element.64.kv_ref) | copy-start | bytes 1966084
  58.0 34.4 %copy-start.12 = (bf16[8,192,384]{2,1,0:T(8,128)(2,1)S(1)}, bf16[8,192,384]{2,1,0:T(8,128)(2,1)}, u32[]{:S(2)}) copy-start(bf16[8,192,384]{2,1,0:T(8,128)(2,1)} %copy-done.11) | copy-start | bytes 3538948
  92.4 2.3 copy-start.28
  92.4 2.3 copy-start.30
  92.4 2.3 copy-start.31
  94.7 116.2 %copy-start = (bf16[1280,1536]{1,0:T(8,128)(2,1)S(1)}, bf16[1280,1536]{1,0:T(8,128)(2,1)}, u32[]{:S(2)}) copy-start(bf16[1280,1536]{1,0:T(8,128)(2,1)} %x_ref.7) | copy-start | bytes 11796484
  206.3 4.6 copy-start.16
  210.9 4.7 copy-start.2
  210.9 4.7 copy-start.18
  210.9 6.6 copy-start.23
  215.6 1.9 copy-start.17
  409.8 1.3 copy-start.13
  409.8 260.5 %reduce-scatter.5.cloned.1.call-start = ((), (), s32[]{:S(2)}) async-start(), calls=%async_computation.4 | async-start | bytes 7077888 | tf_op jit(solution)/shard_map/reduce_scatter | solution.py:1562
  425.2 0.9 copy-start.22
  426.8 249.3 %reduce-scatter.3.cloned.1.call-start = ((), (), s32[]{:S(2)}) async-start(), calls=%async_computation.3 | async-start | bytes 14155776 | tf_op jit(solution)/shard_map/reduce_scatter | solution.py:1563
  427.6 4.3 copy-start.29
  427.6 4.3 copy-start.44
  435.1 45.5 %copy-start.21 = (bf16[8,192,640]{2,1,0:T(8,128)(2,1)S(1)}, bf16[8,192,640]{2,1,0:T(8,128)(2,1)}, u32[]{:S(2)}) copy-start(bf16[8,192,640]{2,1,0:T(8,128)(2,1)} %copy-done.19) | copy-start | bytes 5898244
  480.6 6.5 copy-start.45
  480.6 6.5 copy-start.46
  646.0 2.8 copy-start.36
  646.0 2.9 copy-start.39
  646.0 3.0 copy-start.40
  647.1 5.1 copy-start.38
  647.1 5.1 copy-start.41
  647.2 5.1 copy-start.42
  647.2 5.1 copy-start.43
  647.2 5.7 copy-start.33
  647.2 5.7 copy-start.34
  649.2 5.9 copy-start.32
  655.1 4.5 copy-start.9
  659.6 2.1 copy-start.1
  661.7 2.1 copy-start.3
  663.8 1.5 copy-start.8
  670.3 5.7 copy-start.5
  676.0 1.9 copy-start.6
  677.9 1.9 copy-start.7
  679.8 1.4 copy-start.10
  (2 other events, 1.3 us)
Sparse Core Ops, SparseCore 0:
  409.9 81.8 all-reduce.1
Sparse Core Ops, SparseCore 1:
  426.2 71.8 reduce-scatter.4
  501.9 96.9 reduce-scatter.2

commit v7 on v6

--- a/solution.py
+++ b/solution.py
@@ -340,7 +340,10 @@
     return [t.reshape(n * depth, -1) for t in out[:count]] + list(out[count:])
 
 
-def gateup_adam_kernel(group, w_ref, m_ref, v_ref, grad_ref, w_out, m_out, v_out, g_ref):
+def expert_adam_kernel(
+    group, w_ref, m_ref, v_ref, grad_ref, dw_ref, dm_ref, dv_ref, down_ref,
+    w_out, m_out, v_out, dw_out, dm_out, dv_out, g_ref,
+):
     depth, hidden = grad_ref.shape[0], w_ref.shape[1]
     for e in range(w_ref.shape[0] // (2 * depth)):
         for part in (0, 1):
@@ -350,24 +353,37 @@
         w_out[rows], m_out[rows], v_out[rows] = adam_update(
             w_ref[rows], m_ref[rows], v_ref[rows], g_ref[...], weight_decay, 0.05
         )
-
-
-def gateup_adam(w, m, v, grad, group):
-    experts, depth, parts, hidden = w.shape
-    flat = lambda t: t.reshape(experts * depth * parts, hidden)
+        rows = slice(e * depth, (e + 1) * depth)
+        dw_out[rows], dm_out[rows], dv_out[rows] = adam_update(
+            dw_ref[rows],
+            dm_ref[rows],
+            dv_ref[rows],
+            down_ref[:, e * hidden : (e + 1) * hidden].astype(f32),
+            weight_decay,
+            0.05,
+        )
+
+
+def expert_adam(gateup, gateup_grad, down, down_grad, group):
+    experts, depth, parts, hidden = gateup[0].shape
+    flat = [t.reshape(-1, hidden) for t in gateup]
+    turned = [t.transpose(0, 2, 1).reshape(-1, hidden) for t in down]
     each = 2 * group
-    block = pl.BlockSpec((each * depth * parts, hidden), lambda e: (e, 0))
+    block = lambda n: pl.BlockSpec((each * depth * n, hidden), lambda e: (e, 0))
+    column = lambda n: pl.BlockSpec((depth, each * n * hidden), lambda e: (0, e))
     out = pl.pallas_call(
-        functools.partial(gateup_adam_kernel, group),
+        functools.partial(expert_adam_kernel, group),
         grid=(experts // each,),
-        in_specs=[block] * 3
-        + [pl.BlockSpec((depth, each * parts * hidden), lambda e: (0, e))],
-        out_specs=[block] * 3,
-        out_shape=[jax.ShapeDtypeStruct((experts * depth * parts, hidden), f32)] * 3,
+        in_specs=[block(2)] * 3 + [column(2)] + [block(1)] * 3 + [column(1)],
+        out_specs=[block(2)] * 3 + [block(1)] * 3,
+        out_shape=[jax.ShapeDtypeStruct(t.shape, f32) for t in flat + turned],
         scratch_shapes=[pltpu.VMEM((depth * parts, hidden), f32)],
-        compiler_params=pltpu.CompilerParams(vmem_limit_bytes=32 * 2**20),
-    )(flat(w), flat(m), flat(v), grad)
-    return tuple(t.reshape(w.shape) for t in out)
+        compiler_params=pltpu.CompilerParams(vmem_limit_bytes=60 * 2**20),
+    )(*flat, gateup_grad, *turned, down_grad)
+    return (
+        tuple(t.reshape(gateup[0].shape) for t in out[:3]),
+        tuple(t.reshape(experts, depth, hidden).transpose(0, 2, 1) for t in out[3:]),
+    )
 
 
 def line_gather_kernel(n, n_dp, x_ref, a_ref, b_ref, o_ref, a_out, b_out, *scratch):
@@ -839,7 +855,7 @@
             jax.ShapeDtypeStruct((tokens, 128), f32),
         ],
         scratch_shapes=[pltpu.VMEM((model, width // 2), bf16)],
-        compiler_params=pltpu.CompilerParams(vmem_limit_bytes=48 * 2**20),
+        compiler_params=pltpu.CompilerParams(vmem_limit_bytes=60 * 2**20),
         cost_estimate=pl.CostEstimate(
             flops=2 * tokens * model * steps * width * 3 // 2,
             bytes_accessed=2 * (model * steps * width * 3 // 2 + tokens * steps * width * 3 // 2),
@@ -1039,7 +1055,7 @@
         in_specs=[row, row, half(0), half(1)],
         out_specs=row,
         out_shape=jax.ShapeDtypeStruct((count, model), bf16),
-        compiler_params=pltpu.CompilerParams(vmem_limit_bytes=32 * 2**20),
+        compiler_params=pltpu.CompilerParams(vmem_limit_bytes=60 * 2**20),
     )(tokens, branch, first, second)
 
 
@@ -1607,16 +1623,18 @@
     attn_grad = [inproj_grad, outproj_grad, router_grad]
     if in_width % 128 or out_width % 128:
         attn_grad = [jnp.concatenate(attn_grad, axis=1)]
-    down_next = adam_update(
-        down_weight, down_first, down_second,
-        down_grad.T.reshape(down_weight.shape).astype(f32), weight_decay, 0.05,
-    )
+    gateup_state = (gateup_weight, gateup_first, gateup_second)
+    down_state = (down_weight, down_first, down_second)
     if hidden == 128:
-        gateup_next = gateup_adam(gateup_weight, gateup_first, gateup_second, gateup_grad, group)
+        gateup_next, down_next = expert_adam(
+            gateup_state, gateup_grad, down_state, down_grad, group
+        )
     else:
+        down_next = adam_update(
+            *down_state, down_grad.T.reshape(down_weight.shape).astype(f32), weight_decay, 0.05
+        )
         gateup_next = adam_update(
-            gateup_weight, gateup_first, gateup_second,
-            gateup_back(gateup_grad).astype(f32), weight_decay, 0.05,
+            *gateup_state, gateup_back(gateup_grad).astype(f32), weight_decay, 0.05
         )
     tokens_grad, attn_grad, gains_grad, second_mixture = last_call(
         normed_first_grad, tokens, middle_grad, mixture, gain_rows,

time: 707 us -> 704 us (level)
  Pallas kernels: 574 us -> 584 us
  local copies, waits for them, and re-layouts: 44.9 us -> 35.4 us
    unnamed x101 -> x79, local copies, waits for them, and re-layouts: 37.9 us -> 27.5 us
  transfers between devices with their start and end apart: 3 -> 3, of which waited for: 0 -> 0; matrix products, arithmetic and copies ran while one was open for 5% -> 5% of each run, Pallas kernels for 31% -> 32%
where the time goes in v7:
time: 704 us; the launch traced here: 699 us
  Pallas kernels  584 us (83%)
  matrix products  43 us (6%)
  local copies, waits for them, and re-layouts  35.4 us (5%)
  other arithmetic  19.2 us (3%)
  between operations  16.3 us (2%)
    pallas_call x1, Pallas kernels, last_call(): pl.pallas_call(functools.partial(last_kernel, n, n_dp, len(weights)), out...  154 us
    pallas_call x1, Pallas kernels, expert_grads_call(): pl.pallas_call(functools.partial(expert_grads_kernel, n, shape), grid=(a...  122 us
    pallas_call x1, Pallas kernels, line_gather(): pl.pallas_call(functools.partial(line_gather_kernel, n, n_dp), out_shape=...  112 us
    pallas_call x1, Pallas kernels, attention_back_call(): pl.pallas_call(functools.partial(attention_back_kernel, heads, n), in_spe...  44.7 us
    pallas_call x1, Pallas kernels, expert_call(): pl.pallas_call(functools.partial(expert_kernel, group, steps), grid=(step...  43.5 us
    pallas_call x1, Pallas kernels, attention_call(): pl.pallas_call(functools.partial(attention_kernel, heads, n), in_specs=[w...  34.4 us
    unnamed x79, local copies, waits for them, and re-layouts  27.5 us
    pallas_call x1, Pallas kernels, gather(): pl.pallas_call(functools.partial(gather_kernel, n, group, len(arrays)), o...  26.3 us
  transfers between devices with their start and end apart: 3, of which 0 were waited for; matrix products, arithmetic and copies ran while one was open for 5% of the time, Pallas kernels for 32%

profile of v7, /device:TPU:0, one launch (start us, length us, event | category | flops | bytes accessed | tf_op | source)
XLA Modules:
  0.0 698.8 jit_solution(3562111993973396038)
XLA Ops:
  8.1 1.4 broadcast_multiply_fusion.1
  9.6 0.8 subtract_convert_fusion
  10.7 1.3 convert_element_type.55
  12.2 1.0 convert_element_type.57
  13.6 1.9 copy-done.2
  15.4 26.3 %shard_map.374 = (bf16[8,192,640]{2,1,0:T(8,128)(2,1)S(1)}, bf16[8,192,384]{2,1,0:T(8,128)(2,1)S(1)}, bf16[8,192,128]{2,1,0:T(8,128)(2,1)S(1)}, bf16[192,4096]{1,0:T(8,128)(2,1)S(1)}) custom-call(bf16[192,640]{1,0:T(8,128)(2,1)S(1)} %convert_element_type.56.refs_0_, bf16[192,384]{1,0:T(8,128)(2,1)S(1)} %bitcast.70, ...), custom_call_target="tpu_custom_call" | custom-call | tf_op jit(solution)/shard_map/pallas_call | solution.py:329
  41.7 1.0 copy-done.3
  42.7 1.3 copy-done.13
  44.4 1.5 bitcast_bitcast_fusion
  46.2 1.5 copy-done.14
  47.8 1.1 copy-done.17
  48.9 1.1 copy-done.18
  50.0 7.9 %shard_map.375 = (bf16[1280,1536]{1,0:T(8,128)(2,1)}, bf16[1280,384]{1,0:T(8,128)(2,1)S(1)}, bf16[1280,256]{1,0:T(8,128)(2,1)S(1)}) custom-call(bf16[1280,1536]{1,0:T(8,128)(2,1)} %x_ref.7, f32[8,1536]{1,0:T(8,128)S(1)} %convert_bitcast_fusion.1.gain_ref, bf16[1536,640]{1,0:T(8,128)(2,1)S(1)} %bitcast.75, f32[1536,128]{1,0:T(8,128)S(1)} %copy-done.17, ...), custom_call_target="tpu_custom_call" | custom-call | flops 2516582400 | bytes 11796480 | tf_op jit(solution)/shard_map/pallas_call | solution.py:911
  58.0 34.4 %shard_map.376 = (bf16[1280,384]{1,0:T(8,128)(2,1)S(1)}, f32[2,8,640]{2,1,0:T(8,128)S(1)}, bf16[2,1024,256]{2,1,0:T(8,128)(2,1)S(1)}, bf16[8,192,1024]{2,1,0:T(8,128)(2,1)}) custom-call(bf16[1280,384]{1,0:T(8,128)(2,1)S(1)} %get-tuple-element.66.q_ref, bf16[1280,256]{1,0:T(8,128)(2,1)S(1)} %get-tuple-element.67.kv_ref, ...), custom_call_target="tpu_custom_call" | custom-call | flops 12079595520 | bytes 3932160 | tf_op jit(solution)/shard_map/pallas_call | solution.py:1212
  92.4 2.2 convolution_convert_fusion.2.x_ref
  94.7 111.6 %shard_map.377 = (bf16[1280,1536]{1,0:T(8,128)(2,1)S(1)}, bf16[8,192,4096]{2,1,0:T(8,128)(2,1)S(1)}, bf16[8,192,1024]{2,1,0:T(8,128)(2,1)S(1)}) custom-call(bf16[1280,1536]{1,0:T(8,128)(2,1)S(1)} %convolution_convert_fusion.2.x_ref, bf16[192,4096]{1,0:T(8,128)(2,1)S(1)} %get-tuple-element.70.a_ref, bf16[192,1024]{1,0:T(8,128)(2,1)S(1)} %get-tuple-element.182.b_ref), custom_call_target="tpu_custom_call" | custom-call | flops 1966080 | bytes 196608000 | tf_op jit(solution)/shard_map/pallas_call | solution.py:417
  206.3 4.6 copy-done.10
  210.9 4.7 shard_map.378
  215.6 0.8 copy-done.7
  216.4 1.8 copy-done.11
  218.3 43.5 %shard_map.379 = (bf16[1280,2048]{1,0:T(8,128)(2,1)}, bf16[1280,4096]{1,0:T(8,128)(2,1)}, f32[1280,128]{1,0:T(8,128)}) custom-call(bf16[1280,1536]{1,0:T(8,128)(2,1)} %copy-done.11, bf16[1280,1536]{1,0:T(8,128)(2,1)} %outgrad_ref.5, f32[1280,128]{1,0:T(8,128)} %copy-done.7, bf16[1536,4096]{1,0:T(8,128)(2,1)} %bitcast.71, bf16[1536,1024]{1,0:T(8,128)(2,1)} %bitcast.95, ...), custom_call_target="tpu_custom_call" | custom-call | flops 24159191040 | bytes 34603008 | tf_op jit(solution)/shard_map/pallas_call | solution.py:836
  261.8 22.3 %convolution_convert_fusion.1 = bf16[1280,1536]{1,0:T(8,128)(2,1)S(1)} fusion(bf16[1280,4096]{1,0:T(8,128)(2,1)} %get-tuple-element.77.hidden_ref, bf16[1536,4096]{1,0:T(8,128)(2,1)} %bitcast.72), kind=kOutput, calls=%fused_computation.1 | convolution fusion | flops 16108093440 | bytes 27000832 | tf_op jit(solution)/shard_map/dot_general | solution.py:1563
  284.1 2.4 pad_maximum_fusion.x_ref
  286.5 121.8 %shard_map.380 = (bf16[1280,1664]{1,0:T(8,128)(2,1)}, bf16[1536,4096]{1,0:T(8,128)(2,1)}, bf16[1536,2048]{1,0:T(8,128)(2,1)}, bf16[1280,1536]{1,0:T(8,128)(2,1)}) custom-call(bf16[1280,1664]{1,0:T(8,128)(2,1)} %pad_maximum_fusion.x_ref, bf16[1280,1536]{1,0:T(8,128)(2,1)} %copy-done.11, bf16[1280,1536]{1,0:T(8,128)(2,1)} %outgrad_ref.5, ...), custom_call_target="tpu_custom_call" | custom-call | flops 32212254720 | bytes 19660800 | tf_op jit(solution)/shard_map/pallas_call | solution.py:744
  408.3 3.1 slice.27
  411.5 14.3 %shard_map.381 = (f32[1280,1536]{1,0:T(8,128)}, bf16[1280,1536]{1,0:T(8,128)(2,1)}, bf16[1280,384]{1,0:T(8,128)(2,1)S(1)}, bf16[1280,128]{1,0:T(8,128)(2,1)S(1)}, f32[8,1536]{1,0:T(8,128)S(1)}) custom-call(bf16[1280,1536]{1,0:T(8,128)(2,1)} %x_ref.7, bf16[1280,1536]{1,0:T(8,128)(2,1)} %copy-done.1, bf16[1280,1664]{1,0:T(8,128)(2,1)} %get-tuple-element.82.summed_ref, ...), custom_call_target="tpu_custom_call" | custom-call | tf_op jit(solution)/shard_map/pallas_call | solution.py:1002
  425.8 0.9 copy-done.16
  427.5 0.7 copy.99
  428.3 4.3 convolution_convert_fusion.5
  432.6 3.3 convolution_convert_fusion.4
  435.8 44.7 %shard_map.382 = bf16[1280,640]{1,0:T(8,128)(2,1)} custom-call(bf16[1280,384]{1,0:T(8,128)(2,1)} %copy-done.19, bf16[1280,256]{1,0:T(8,128)(2,1)} %copy-done.20, bf16[2,1024,256]{2,1,0:T(8,128)(2,1)} %copy-done.23, bf16[1280,384]{1,0:T(8,128)(2,1)} %copy-done.16, bf16[1280,384]{1,0:T(8,128)(2,1)} %copy-done.21, f32[2,8,640]{2,1,0:T(8,128)} %copy-done.24, ...), custom_call_target="tpu_custom_call" | custom-call | flops 30198988800 | bytes 5898240 | tf_op jit(solution)/shard_map/pallas_call | solution.py:1375
  480.6 6.5 convolution_convert_fusion.first_ref
  487.1 4.5 convolution_convert_fusion.3
  491.6 154.4 %shard_map.383 = (f32[1280,1536]{1,0:T(8,128)}, f32[192,1152]{1,0:T(8,128)}, f32[16,256]{1,0:T(8,128)}, bf16[640,1536]{1,0:T(8,128)(2,1)}) custom-call(bf16[1280,1536]{1,0:T(8,128)(2,1)} %convolution_convert_fusion.first_ref, bf16[1280,1536]{1,0:T(8,128)(2,1)} %x_ref.7, f32[1280,1536]{1,0:T(8,128)} %get-tuple-element.89.middle_ref, ...), custom_call_target="tpu_custom_call" | custom-call | flops 1966080 | bytes 1048576 | tf_op jit(solution)/shard_map/pallas_call | solution.py:630
  646.1 1.2 slice.28
  647.7 1.0 slice_bitcast_fusion
  649.0 0.7 broadcast_multiply_fusion.2
  649.8 0.7 broadcast_multiply_fusion
  650.6 0.7 copy.97
  651.3 1.7 multiply_subtract_fusion.2
  653.0 1.6 copy.100
  655.9 0.7 bitcast_reduce_fusion
  656.7 1.3 multiply_subtract_fusion.3
  658.0 2.3 multiply_subtract_fusion.1
  660.3 3.1 multiply_subtract_fusion
  663.4 8.4 %shard_map.384 = bf16[1280,1536]{1,0:T(8,128)(2,1)} custom-call(bf16[1280,1536]{1,0:T(8,128)(2,1)} %x_ref.7, bf16[1280,1536]{1,0:T(8,128)(2,1)} %copy-done.1, bf16[640,1536]{1,0:T(8,128)(2,1)} %all-reduce.2.cloned.1.call-done.first_ref, bf16[640,1536]{1,0:T(8,128)(2,1)} %get-tuple-element.96.second_ref), custom_call_target="tpu_custom_call" | custom-call | tf_op jit(solution)/shard_map/pallas_call | solution.py:1052
  671.8 12.1 %shard_map.385 = (f32[6144,128]{1,0:T(8,128)}, f32[6144,128]{1,0:T(8,128)}, f32[6144,128]{1,0:T(8,128)}, f32[3072,128]{1,0:T(8,128)}, f32[3072,128]{1,0:T(8,128)}, /*index=5*/f32[3072,128]{1,0:T(8,128)}) custom-call(f32[6144,128]{1,0:T(8,128)} %bitcast.63, f32[6144,128]{1,0:T(8,128)} %bitcast.78, f32[6144,128]{1,0:T(8,128)} %bitcast.79, ...), custom_call_target="tpu_custom_call" | custom-call | tf_op jit(solution)/shard_map/pallas_call | solution.py:374
  684.0 7.1 %copy.110 = f32[1280,1536]{1,0:T(8,128)} copy(f32[1280,1536]{1,0:T(8,128)} %get-tuple-element.207) | data formatting | bytes 15728640
  (91 shorter events, 4.7 us)
Async XLA Ops:
  8.0 655.4 %all-reduce.2.cloned.1.call-start = ((), (), s32[]{:S(2)}) async-start(), calls=%async_computation.2 | async-start | bytes 3932160 | tf_op jit(solution)/shard_map/psum | solution.py:1570
  13.5 1.9 copy-start.2
  15.4 30.5 %copy-start.32 = (s32[1280,8]{0,1:T(8,128)S(1)}, s32[1280,8]{0,1:T(8,128)}, u32[]{:S(2)}) copy-start(s32[1280,8]{0,1:T(8,128)} %param.25) | copy-start | bytes 122884
  41.7 1.0 copy-start.3
  42.7 1.3 copy-start.13
  44.3 367.2 %copy-start.6 = (f32[8,1536]{1,0:T(8,128)}, f32[8,1536]{1,0:T(8,128)S(1)}, u32[]{:S(2)}) copy-start(f32[8,1536]{1,0:T(8,128)S(1)} %convert_bitcast_fusion.1.gain_ref) | copy-start | bytes 147460
  46.2 1.6 copy-start.14
  47.8 1.1 copy-start.17
  48.9 1.1 copy-start.18
  58.0 34.4 %copy-start.19 = (bf16[1280,384]{1,0:T(8,128)(2,1)}, bf16[1280,384]{1,0:T(8,128)(2,1)S(1)}, u32[]{:S(2)}) copy-start(bf16[1280,384]{1,0:T(8,128)(2,1)S(1)} %get-tuple-element.66.q_ref) | copy-start | bytes 2949124
  58.0 34.4 %copy-start.20 = (bf16[1280,256]{1,0:T(8,128)(2,1)}, bf16[1280,256]{1,0:T(8,128)(2,1)S(1)}, u32[]{:S(2)}) copy-start(bf16[1280,256]{1,0:T(8,128)(2,1)S(1)} %get-tuple-element.67.kv_ref) | copy-start | bytes 1966084
  58.0 34.4 %copy-start.4 = (bf16[8,192,384]{2,1,0:T(8,128)(2,1)S(1)}, bf16[8,192,384]{2,1,0:T(8,128)(2,1)}, u32[]{:S(2)}) copy-start(bf16[8,192,384]{2,1,0:T(8,128)(2,1)} %copy-done.3) | copy-start | bytes 3538948
  92.4 2.3 copy-start.21
  92.4 2.3 copy-start.23
  92.4 2.3 copy-start.24
  94.7 116.2 %copy-start = (bf16[1280,1536]{1,0:T(8,128)(2,1)S(1)}, bf16[1280,1536]{1,0:T(8,128)(2,1)}, u32[]{:S(2)}) copy-start(bf16[1280,1536]{1,0:T(8,128)(2,1)} %x_ref.7) | copy-start | bytes 11796484
  206.3 4.6 copy-start.10
  210.9 4.7 copy-start.1
  210.9 4.7 copy-start.12
  215.6 0.8 copy-start.7
  216.4 1.8 copy-start.11
  261.8 22.3 %copy-start.27 = (f32[1280,128]{1,0:T(8,128)S(1)}, f32[1280,128]{1,0:T(8,128)}, u32[]{:S(2)}) copy-start(f32[1280,128]{1,0:T(8,128)} %get-tuple-element.78) | copy-start | bytes 1966084
  408.3 3.2 copy-start.5
  408.3 3.2 copy-start.8
  411.4 260.4 %reduce-scatter.5.cloned.1.call-start = ((), (), s32[]{:S(2)}) async-start(), calls=%async_computation.4 | async-start | bytes 7077888 | tf_op jit(solution)/shard_map/reduce_scatter | solution.py:1578
  425.8 0.9 copy-start.16
  426.8 0.6 copy-start.9
  426.8 0.7 copy-start.30
  426.8 245.0 %reduce-scatter.3.cloned.1.call-start = ((), (), s32[]{:S(2)}) async-start(), calls=%async_computation.3 | async-start | bytes 14155776 | tf_op jit(solution)/shard_map/reduce_scatter | solution.py:1579
  427.5 5.0 copy-start.22
  428.3 4.3 copy-start.33
  435.8 44.8 %copy-start.15 = (bf16[8,192,640]{2,1,0:T(8,128)(2,1)S(1)}, bf16[8,192,640]{2,1,0:T(8,128)(2,1)}, u32[]{:S(2)}) copy-start(bf16[8,192,640]{2,1,0:T(8,128)(2,1)} %copy-done.13) | copy-start | bytes 5898244
  480.6 6.5 copy-start.34
  480.6 6.5 copy-start.35
  491.6 157.3 %copy-start.31 = (f32[192,16]{0,1:T(8,128)S(1)}, f32[192,16]{0,1:T(8,128)}, u32[]{:S(2)}) copy-start(f32[192,16]{0,1:T(8,128)} %get-tuple-element.184) | copy-start | bytes 36868
  646.0 11.9 %copy-start.26 = (f32[2,192,192]{2,1,0:T(8,128)S(1)}, f32[2,192,192]{2,1,0:T(8,128)}, u32[]{:S(2)}) copy-start(f32[2,192,192]{2,1,0:T(8,128)} %param.29) | copy-start | bytes 884740
  646.1 14.2 %copy-start.25 = (f32[192,2,320]{2,1,0:T(2,128)S(1)}, f32[192,2,320]{2,1,0:T(2,128)}, u32[]{:S(2)}) copy-start(f32[192,2,320]{2,1,0:T(2,128)} %param.26) | copy-start | bytes 1474564
  646.1 14.2 %copy-start.28 = (f32[192,2,320]{2,1,0:T(2,128)S(1)}, f32[192,2,320]{2,1,0:T(2,128)}, u32[]{:S(2)}) copy-start(f32[192,2,320]{2,1,0:T(2,128)} %param.27) | copy-start | bytes 1474564
  646.1 14.2 %copy-start.29 = (f32[192,2,320]{2,1,0:T(2,128)S(1)}, f32[192,2,320]{2,1,0:T(2,128)}, u32[]{:S(2)}) copy-start(f32[192,2,320]{2,1,0:T(2,128)} %param.28) | copy-start | bytes 1474564
Sparse Core Ops, SparseCore 0:
  411.6 81.8 all-reduce.1
Sparse Core Ops, SparseCore 1:
  426.9 71.1 reduce-scatter.4
  501.8 96.9 reduce-scatter.2

commit v8 on v7

--- a/solution.py
+++ b/solution.py
@@ -960,7 +960,7 @@
             jax.ShapeDtypeStruct((count, model), bf16),
             jax.ShapeDtypeStruct((count, 128), f32),
         ],
-        compiler_params=pltpu.CompilerParams(vmem_limit_bytes=32 * 2**20),
+        compiler_params=pltpu.CompilerParams(vmem_limit_bytes=60 * 2**20),
     )(tokens, branch, gain, router, routes)
 
 
@@ -1026,7 +1026,7 @@
             jax.ShapeDtypeStruct((count, 128), bf16),
             jax.ShapeDtypeStruct((8, model), f32),
         ],
-        compiler_params=pltpu.CompilerParams(vmem_limit_bytes=48 * 2**20),
+        compiler_params=pltpu.CompilerParams(vmem_limit_bytes=60 * 2**20),
     )(tokens, branch, summed, gates, outgrad, gain, router, outproj)
 
 

time: 704 us -> 715 us (1.016)
    unnamed x79 -> x67, local copies, waits for them, and re-layouts: 27.5 us -> 30 us
where the time goes in v8:
time: 715 us; the launch traced here: 709 us
  Pallas kernels  590 us (83%)
  matrix products  43.1 us (6%)
  local copies, waits for them, and re-layouts  38.6 us (5%)
  other arithmetic  20.5 us (3%)
  between operations  16.2 us (2%)
    pallas_call x1, Pallas kernels, last_call(): pl.pallas_call(functools.partial(last_kernel, n, n_dp, len(weights)), out...  154 us
    pallas_call x1, Pallas kernels, expert_grads_call(): pl.pallas_call(functools.partial(expert_grads_kernel, n, shape), grid=(a...  122 us
    pallas_call x1, Pallas kernels, line_gather(): pl.pallas_call(functools.partial(line_gather_kernel, n, n_dp), out_shape=...  112 us
    pallas_call x1, Pallas kernels, attention_back_call(): pl.pallas_call(functools.partial(attention_back_kernel, heads, n), in_spe...  45.9 us
    pallas_call x1, Pallas kernels, expert_call(): pl.pallas_call(functools.partial(expert_kernel, group, steps), grid=(step...  43.6 us
    pallas_call x1, Pallas kernels, attention_call(): pl.pallas_call(functools.partial(attention_kernel, heads, n), in_specs=[w...  34.4 us
    unnamed x67, local copies, waits for them, and re-layouts  30 us
    pallas_call x1, Pallas kernels, gather(): pl.pallas_call(functools.partial(gather_kernel, n, group, len(arrays)), o...  26.3 us
  transfers between devices with their start and end apart: 3, of which 0 were waited for; matrix products, arithmetic and copies ran while one was open for 5% of the time, Pallas kernels for 32%

profile of v8, /device:TPU:0, one launch (start us, length us, event | category | flops | bytes accessed | tf_op | source)
XLA Modules:
  0.0 709.3 jit_solution(1741871815055117056)
XLA Ops:
  8.1 1.4 broadcast_multiply_fusion.1
  9.6 0.8 subtract_convert_fusion
  10.7 1.3 convert_element_type.55
  12.2 1.0 convert_element_type.57
  13.6 1.9 copy-done.1
  15.4 26.3 %shard_map.374 = (bf16[8,192,640]{2,1,0:T(8,128)(2,1)S(1)}, bf16[8,192,384]{2,1,0:T(8,128)(2,1)S(1)}, bf16[8,192,128]{2,1,0:T(8,128)(2,1)S(1)}, bf16[192,4096]{1,0:T(8,128)(2,1)S(1)}) custom-call(bf16[192,640]{1,0:T(8,128)(2,1)S(1)} %convert_element_type.56.refs_0_, bf16[192,384]{1,0:T(8,128)(2,1)S(1)} %bitcast.70, ...), custom_call_target="tpu_custom_call" | custom-call | tf_op jit(solution)/shard_map/pallas_call | solution.py:329
  41.7 1.3 copy-done.8
  43.2 0.9 copy.105
  44.1 1.4 convert_bitcast_fusion.1.gain_ref
  45.5 1.5 bitcast_bitcast_fusion
  47.0 0.8 fusion.8
  47.8 1.9 copy.91.routes_ref
  49.7 0.8 copy-done.4
  50.5 1.5 copy-done.9
  52.0 1.1 copy-done.11
  53.1 1.1 copy-done.12
  54.3 8.0 %shard_map.375 = (bf16[1280,1536]{1,0:T(8,128)(2,1)}, bf16[1280,384]{1,0:T(8,128)(2,1)S(1)}, bf16[1280,256]{1,0:T(8,128)(2,1)S(1)}) custom-call(bf16[1280,1536]{1,0:T(8,128)(2,1)} %x_ref.7, f32[8,1536]{1,0:T(8,128)S(1)} %copy-done.4, bf16[1536,640]{1,0:T(8,128)(2,1)S(1)} %bitcast.75, f32[1536,128]{1,0:T(8,128)S(1)} %copy-done.11, f32[1536,128]{1,0:T(8,128)S(1)} %copy-done.12), custom_call_target="tpu_custom_call" | custom-call | flops 2516582400 | bytes 11796480 | tf_op jit(solution)/shard_map/pallas_call | solution.py:911
  62.3 34.4 %shard_map.376 = (bf16[1280,384]{1,0:T(8,128)(2,1)S(1)}, f32[2,8,640]{2,1,0:T(8,128)S(1)}, bf16[2,1024,256]{2,1,0:T(8,128)(2,1)S(1)}, bf16[8,192,1024]{2,1,0:T(8,128)(2,1)}) custom-call(bf16[1280,384]{1,0:T(8,128)(2,1)S(1)} %get-tuple-element.66.q_ref, bf16[1280,256]{1,0:T(8,128)(2,1)S(1)} %get-tuple-element.67.kv_ref, bf16[192,1024]{1,0:T(8,128)(2,1)S(1)} %copy-done.5), custom_call_target="tpu_custom_call" | custom-call | flops 12079595520 | bytes 3932160 | tf_op jit(solution)/shard_map/pallas_call | solution.py:1212
  96.8 2.2 convolution_convert_fusion.2.x_ref
  99.0 111.6 %shard_map.377 = (bf16[1280,1536]{1,0:T(8,128)(2,1)S(1)}, bf16[8,192,4096]{2,1,0:T(8,128)(2,1)S(1)}, bf16[8,192,1024]{2,1,0:T(8,128)(2,1)S(1)}) custom-call(bf16[1280,1536]{1,0:T(8,128)(2,1)S(1)} %convolution_convert_fusion.2.x_ref, bf16[192,4096]{1,0:T(8,128)(2,1)S(1)} %get-tuple-element.70.a_ref, bf16[192,1024]{1,0:T(8,128)(2,1)S(1)} %get-tuple-element.182.b_ref), custom_call_target="tpu_custom_call" | custom-call | flops 1966080 | bytes 196608000 | tf_op jit(solution)/shard_map/pallas_call | solution.py:417
  210.7 1.9 copy-done
  212.6 4.5 copy-done.6
  217.1 1.7 copy-done.7
  218.8 8.1 %shard_map.378 = (bf16[1280,1536]{1,0:T(8,128)(2,1)}, f32[1280,128]{1,0:T(8,128)}) custom-call(bf16[1280,1536]{1,0:T(8,128)(2,1)} %x_ref.7, bf16[1280,1536]{1,0:T(8,128)(2,1)} %copy-done, f32[8,1536]{1,0:T(8,128)} %convert_bitcast_fusion.1.gain_ref, bf16[1536,128]{1,0:T(8,128)(2,1)} %bitcast.66, s32[1280,8]{1,0:T(8,128)} %copy.91.routes_ref), custom_call_target="tpu_custom_call" | custom-call | tf_op jit(solution)/shard_map/pallas_call | solution.py:954
  226.9 43.6 %shard_map.379 = (bf16[1280,2048]{1,0:T(8,128)(2,1)}, bf16[1280,4096]{1,0:T(8,128)(2,1)}, f32[1280,128]{1,0:T(8,128)}) custom-call(bf16[1280,1536]{1,0:T(8,128)(2,1)} %get-tuple-element.72.rows_ref, bf16[1280,1536]{1,0:T(8,128)(2,1)} %outgrad_ref.5, f32[1280,128]{1,0:T(8,128)} %get-tuple-element.73.gates_ref, bf16[1536,4096]{1,0:T(8,128)(2,1)} %bitcast.71, ...), custom_call_target="tpu_custom_call" | custom-call | flops 24159191040 | bytes 34603008 | tf_op jit(solution)/shard_map/pallas_call | solution.py:836
  270.5 22.3 %convolution_convert_fusion.1 = bf16[1280,1536]{1,0:T(8,128)(2,1)S(1)} fusion(bf16[1280,4096]{1,0:T(8,128)(2,1)} %get-tuple-element.77.hidden_ref, bf16[1536,4096]{1,0:T(8,128)(2,1)} %bitcast.72), kind=kOutput, calls=%fused_computation.1 | convolution fusion | flops 16108093440 | bytes 27000832 | tf_op jit(solution)/shard_map/dot_general | solution.py:1563
  292.8 2.4 pad_maximum_fusion.x_ref
  295.2 121.9 %shard_map.380 = (bf16[1280,1664]{1,0:T(8,128)(2,1)}, bf16[1536,4096]{1,0:T(8,128)(2,1)}, bf16[1536,2048]{1,0:T(8,128)(2,1)}, bf16[1280,1536]{1,0:T(8,128)(2,1)}) custom-call(bf16[1280,1664]{1,0:T(8,128)(2,1)} %pad_maximum_fusion.x_ref, bf16[1280,1536]{1,0:T(8,128)(2,1)} %get-tuple-element.72.rows_ref, bf16[1280,1536]{1,0:T(8,128)(2,1)} %outgrad_ref.5, ...), custom_call_target="tpu_custom_call" | custom-call | flops 32212254720 | bytes 19660800 | tf_op jit(solution)/shard_map/pallas_call | solution.py:744
  417.1 2.9 slice.27
  420.1 15.8 %shard_map.381 = (f32[1280,1536]{1,0:T(8,128)}, bf16[1280,1536]{1,0:T(8,128)(2,1)}, bf16[1280,384]{1,0:T(8,128)(2,1)}, bf16[1280,128]{1,0:T(8,128)(2,1)}, f32[8,1536]{1,0:T(8,128)}) custom-call(bf16[1280,1536]{1,0:T(8,128)(2,1)} %x_ref.7, bf16[1280,1536]{1,0:T(8,128)(2,1)} %copy-done, bf16[1280,1664]{1,0:T(8,128)(2,1)} %get-tuple-element.82.summed_ref, ...), custom_call_target="tpu_custom_call" | custom-call | tf_op jit(solution)/shard_map/pallas_call | solution.py:1002
  436.9 4.3 convolution_convert_fusion.5
  441.2 3.3 convolution_convert_fusion.4
  444.5 45.9 %shard_map.382 = bf16[1280,640]{1,0:T(8,128)(2,1)} custom-call(bf16[1280,384]{1,0:T(8,128)(2,1)} %copy-done.13, bf16[1280,256]{1,0:T(8,128)(2,1)} %copy-done.14, bf16[2,1024,256]{2,1,0:T(8,128)(2,1)} %copy-done.17, bf16[1280,384]{1,0:T(8,128)(2,1)} %get-tuple-element.87.do_ref, bf16[1280,384]{1,0:T(8,128)(2,1)} %copy-done.15, f32[2,8,640]{2,1,0:T(8,128)} %copy-done.18, ...), custom_call_target="tpu_custom_call" | custom-call | flops 30198988800 | bytes 5898240 | tf_op jit(solution)/shard_map/pallas_call | solution.py:1375
  490.4 6.5 convolution_convert_fusion.first_ref
  496.9 4.5 convolution_convert_fusion.3
  501.4 154.4 %shard_map.383 = (f32[1280,1536]{1,0:T(8,128)}, f32[192,1152]{1,0:T(8,128)}, f32[16,256]{1,0:T(8,128)}, bf16[640,1536]{1,0:T(8,128)(2,1)}) custom-call(bf16[1280,1536]{1,0:T(8,128)(2,1)} %convolution_convert_fusion.first_ref, bf16[1280,1536]{1,0:T(8,128)(2,1)} %x_ref.7, f32[1280,1536]{1,0:T(8,128)} %get-tuple-element.89.middle_ref, ...), custom_call_target="tpu_custom_call" | custom-call | flops 1966080 | bytes 1048576 | tf_op jit(solution)/shard_map/pallas_call | solution.py:630
  655.8 1.2 slice.28
  657.5 1.0 slice_bitcast_fusion
  660.3 0.7 copy.97
  661.0 1.7 multiply_subtract_fusion.2
  662.7 1.6 copy.100
  664.3 1.6 copy.101
  667.2 1.3 multiply_subtract_fusion.3
  668.6 2.3 multiply_subtract_fusion.1
  670.9 3.1 multiply_subtract_fusion
  674.0 8.4 %shard_map.384 = bf16[1280,1536]{1,0:T(8,128)(2,1)} custom-call(bf16[1280,1536]{1,0:T(8,128)(2,1)} %x_ref.7, bf16[1280,1536]{1,0:T(8,128)(2,1)} %copy-done, bf16[640,1536]{1,0:T(8,128)(2,1)} %all-reduce.2.cloned.1.call-done.first_ref, bf16[640,1536]{1,0:T(8,128)(2,1)} %get-tuple-element.96.second_ref), custom_call_target="tpu_custom_call" | custom-call | tf_op jit(solution)/shard_map/pallas_call | solution.py:1052
  682.4 12.1 %shard_map.385 = (f32[6144,128]{1,0:T(8,128)}, f32[6144,128]{1,0:T(8,128)}, f32[6144,128]{1,0:T(8,128)}, f32[3072,128]{1,0:T(8,128)}, f32[3072,128]{1,0:T(8,128)}, /*index=5*/f32[3072,128]{1,0:T(8,128)}) custom-call(f32[6144,128]{1,0:T(8,128)} %bitcast.63, f32[6144,128]{1,0:T(8,128)} %bitcast.78, f32[6144,128]{1,0:T(8,128)} %bitcast.79, ...), custom_call_target="tpu_custom_call" | custom-call | tf_op jit(solution)/shard_map/pallas_call | solution.py:374
  694.5 7.1 %copy.110 = f32[1280,1536]{1,0:T(8,128)} copy(f32[1280,1536]{1,0:T(8,128)} %get-tuple-element.207) | data formatting | bytes 15728640
  (79 shorter events, 6.0 us)
Async XLA Ops:
  8.0 666.0 %all-reduce.2.cloned.1.call-start = ((), (), s32[]{:S(2)}) async-start(), calls=%async_computation.2 | async-start | bytes 3932160 | tf_op jit(solution)/shard_map/psum | solution.py:1570
  13.5 1.9 copy-start.1
  41.7 1.3 copy-start.8
  43.0 19.3 %copy-start.2 = (bf16[8,192,128]{2,1,0:T(8,128)(2,1)}, bf16[8,192,128]{2,1,0:T(8,128)(2,1)S(1)}, u32[]{:S(2)}) copy-start(bf16[8,192,128]{2,1,0:T(8,128)(2,1)S(1)} %get-tuple-element.64) | copy-start | bytes 1179652
  43.0 53.8 %copy-start.3 = (bf16[8,192,384]{2,1,0:T(8,128)(2,1)}, bf16[8,192,384]{2,1,0:T(8,128)(2,1)S(1)}, u32[]{:S(2)}) copy-start(bf16[8,192,384]{2,1,0:T(8,128)(2,1)S(1)} %get-tuple-element.69) | copy-start | bytes 3538948
  49.7 0.8 copy-start.4
  50.5 1.5 copy-start.9
  52.0 1.1 copy-start.11
  53.1 1.1 copy-start.12
  54.3 8.0 %copy-start.5 = (bf16[192,1024]{1,0:T(8,128)(2,1)S(1)}, bf16[192,1024]{1,0:T(8,128)(2,1)}, u32[]{:S(2)}) copy-start(bf16[192,1024]{1,0:T(8,128)(2,1)} %get-tuple-element.183.w_ref) | copy-start | bytes 1179652
  62.3 34.4 %copy-start.13 = (bf16[1280,384]{1,0:T(8,128)(2,1)}, bf16[1280,384]{1,0:T(8,128)(2,1)S(1)}, u32[]{:S(2)}) copy-start(bf16[1280,384]{1,0:T(8,128)(2,1)S(1)} %get-tuple-element.66.q_ref) | copy-start | bytes 2949124
  62.3 34.4 %copy-start.14 = (bf16[1280,256]{1,0:T(8,128)(2,1)}, bf16[1280,256]{1,0:T(8,128)(2,1)S(1)}, u32[]{:S(2)}) copy-start(bf16[1280,256]{1,0:T(8,128)(2,1)S(1)} %get-tuple-element.67.kv_ref) | copy-start | bytes 1966084
  96.7 2.3 copy-start.15
  96.7 2.3 copy-start.17
  96.7 2.3 copy-start.18
  210.7 1.9 copy-start
  212.6 4.5 copy-start.6
  217.1 1.7 copy-start.7
  270.5 22.3 %copy-start.21 = (f32[1280,128]{1,0:T(8,128)S(1)}, f32[1280,128]{1,0:T(8,128)}, u32[]{:S(2)}) copy-start(f32[1280,128]{1,0:T(8,128)} %get-tuple-element.78) | copy-start | bytes 1966084
  420.1 262.3 %reduce-scatter.5.cloned.1.call-start = ((), (), s32[]{:S(2)}) async-start(), calls=%async_computation.4 | async-start | bytes 7077888 | tf_op jit(solution)/shard_map/reduce_scatter | solution.py:1578
  435.9 0.7 copy-start.24
  435.9 1.0 copy-start.27
  435.9 246.5 %reduce-scatter.3.cloned.1.call-start = ((), (), s32[]{:S(2)}) async-start(), calls=%async_computation.3 | async-start | bytes 14155776 | tf_op jit(solution)/shard_map/reduce_scatter | solution.py:1579
  436.6 4.6 copy-start.16
  436.7 4.5 copy-start.26
  444.5 45.9 %copy-start.10 = (bf16[8,192,640]{2,1,0:T(8,128)(2,1)S(1)}, bf16[8,192,640]{2,1,0:T(8,128)(2,1)}, u32[]{:S(2)}) copy-start(bf16[8,192,640]{2,1,0:T(8,128)(2,1)} %copy-done.8) | copy-start | bytes 5898244
  490.3 6.6 copy-start.28
  490.3 6.6 copy-start.29
  501.4 157.2 %copy-start.25 = (f32[192,16]{0,1:T(8,128)S(1)}, f32[192,16]{0,1:T(8,128)}, u32[]{:S(2)}) copy-start(f32[192,16]{0,1:T(8,128)} %get-tuple-element.184) | copy-start | bytes 36868
  655.8 12.8 %copy-start.20 = (f32[2,192,192]{2,1,0:T(8,128)S(1)}, f32[2,192,192]{2,1,0:T(8,128)}, u32[]{:S(2)}) copy-start(f32[2,192,192]{2,1,0:T(8,128)} %param.29) | copy-start | bytes 884740
  655.8 15.1 %copy-start.19 = (f32[192,2,320]{2,1,0:T(2,128)S(1)}, f32[192,2,320]{2,1,0:T(2,128)}, u32[]{:S(2)}) copy-start(f32[192,2,320]{2,1,0:T(2,128)} %param.26) | copy-start | bytes 1474564
  655.8 15.1 %copy-start.22 = (f32[192,2,320]{2,1,0:T(2,128)S(1)}, f32[192,2,320]{2,1,0:T(2,128)}, u32[]{:S(2)}) copy-start(f32[192,2,320]{2,1,0:T(2,128)} %param.27) | copy-start | bytes 1474564
  655.8 15.1 %copy-start.23 = (f32[192,2,320]{2,1,0:T(2,128)S(1)}, f32[192,2,320]{2,1,0:T(2,128)}, u32[]{:S(2)}) copy-start(f32[192,2,320]{2,1,0:T(2,128)} %param.28) | copy-start | bytes 1474564
Sparse Core Ops, SparseCore 0:
  420.2 81.8 all-reduce.1
Sparse Core Ops, SparseCore 1:
  436.0 71.6 reduce-scatter.4
  511.4 97.0 reduce-scatter.2
